TPU v7x, 32 devices: a whole 2x2x4 slice. The times are simulated.
32 devices in a mesh: groups: 2 (over x), rows: 16 (over z, y, core).
Axes of the slice: x: 2, y: 2, z: 4, core: 2. Of those that a mesh axis runs over, the one named last changes fastest.
Arguments:
- ensemble: float32 [131072, 256], P(('groups', 'rows')), parts along dimension 0, may hold values from -60 to 60
- mean_state: float32 [131072], P(('groups', 'rows')), parts along dimension 0, may hold values from -6 to 6
- observed: float32 [4, 128], P('groups'), parts along dimension 0, may hold values from -8 to 8
- error_var: float32 [4, 128], P('groups'), parts along dimension 0, may hold values from 0.5 to 4
- owner: int32 [4], P('groups'), parts along dimension 0, may hold values from 0 to 15
- obs_rows: int32 [4, 128], P('groups'), parts along dimension 0, may hold values from 0 to 4095
Outputs:
- analysis_ensemble: float32 [131072, 256], P(('groups', 'rows')), parts along dimension 0
- analysis_mean: float32 [131072], P(('groups', 'rows')), parts along dimension 0
There are 2 independent parts, one for each index of `groups`. A program takes and returns all parts, laid end to end along the dimension named above; each array names one. Nothing has to cross between parts.
Inputs may be any that keep to these rules, and one draw needn't show every extreme that they name: `obs_rows`: rows may repeat.
All inputs are finite; a program needn't handle non-finite values.
Results may differ from a plain program's by a relative error of at most 0.0003.
Values sent between devices are 32-bit elements; how exact they have to be, the bound alone decides.
No kernel may reach another device: no remote copies, remote signals or barrier semaphores. Data moves between devices by JAX's collectives and lax.ppermute only.
A program may use at most 64 MiB of HBM per device.

v0:
```python
import functools

import jax
import jax.numpy as jnp
from jax import lax
from jax.experimental import pallas as pl
from jax.experimental.pallas import tpu as pltpu
from jax.sharding import PartitionSpec as P

RELAX = 0.6
HI = lax.Precision.HIGHEST
AXIS = "rows"
F32 = jnp.float32
BF16 = jnp.bfloat16
LANES = 128
SUB = 8
OBS = 128
VMEM_LIMIT = 40 * 1024 * 1024

S1, S2, G0, G1, INNOV, PACKED = 0, 128, 256, 384, 448, 480


def dot(a, b, dims=((1,), (0,)), precision=HI):
    return lax.dot_general(a, b, (dims, ((), ())), precision=precision, preferred_element_type=F32)


def column(row):
    return jnp.broadcast_to(row, (LANES, LANES)).T


def split(x):
    high = x.astype(BF16)
    return high, (x - high.astype(F32)).astype(BF16)


def gather_kernel(
    chunks, owner_s, rows_s, rows_v, observed, error_var, mean_v, x_hbm, packed, x_buf, picked, sem
):
    me = lax.axis_index(AXIS)
    members = x_buf.shape[1]
    size = x_buf.shape[0] // chunks

    def copy(i):
        part = pl.ds(i * size, size)
        return pltpu.make_async_copy(x_hbm.at[part], x_buf.at[part], sem.at[i])

    for i in range(chunks):
        copy(i).start()

    innovations = []
    scales = []
    lane = lax.broadcasted_iota(jnp.int32, (OBS, LANES), 1)
    for k in range(2):
        index = column(rows_v[k : k + 1, :].astype(F32)).astype(jnp.int32)
        prior = jnp.zeros((OBS, LANES), F32)
        for r in range(mean_v.shape[0]):
            prior = prior + jnp.where(index == lane + r * LANES, mean_v[r : r + 1, :], 0.0)
        prior = jnp.sum(prior.T, axis=0, keepdims=True)
        scale = lax.rsqrt(error_var[k : k + 1, :] * (members - 1.0))
        scale = jnp.where(owner_s[k] == me, scale, 0.0)
        innovations.append(scale * (observed[k : k + 1, :] - prior))
        scales.append(column(scale))

    def gram(i, carry):
        copy(i).wait()
        x = x_buf[pl.ds(pl.multiple_of(i * size, size), size), :]
        high = x.astype(BF16)
        rest = x - high.astype(F32)
        mid = rest.astype(BF16)
        low = (rest - mid.astype(F32)).astype(BF16)
        both = dot(high, high, ((0,), (0,)), None) + dot(mid, mid, ((0,), (0,)), None)
        cross = dot(high, mid, ((0,), (0,)), None) + dot(high, low, ((0,), (0,)), None)
        return carry[0] + both, carry[1] + cross

    zero = jnp.zeros((members, members), F32)
    both, cross = lax.fori_loop(0, chunks, gram, (zero, zero))
    total = both + cross + cross.T
    half = members // 2
    packed[G0 : G0 + half, :] = total[:half, :]
    packed[G1 : G1 + half // 2, :half] = total[half : half + half // 2, half:]
    packed[G1 : G1 + half // 2, half:] = total[half + half // 2 :, half:]

    for k, at in ((0, S1), (1, S2)):

        def take(o, _, k=k):
            picked[pl.ds(o, 1), :] = x_buf[pl.ds(rows_s[k, o], 1), :]
            return 0

        lax.fori_loop(0, OBS, take, 0, unroll=8)
        packed[at : at + OBS, :half] = picked[:, :half] * scales[k]
        packed[at : at + OBS, half:] = picked[:, half:] * scales[k]

    packed[INNOV:PACKED, :] = jnp.zeros((PACKED - INNOV, members), F32)
    packed[INNOV : INNOV + 1, :half] = innovations[0]
    packed[INNOV : INNOV + 1, half:] = innovations[1]


def factor(a):
    count = LANES // SUB
    lane = lax.broadcasted_iota(jnp.int32, (SUB, LANES), 1)
    sub = lax.broadcasted_iota(jnp.int32, (SUB, LANES), 0)
    rows = [a[SUB * i : SUB * (i + 1), :] for i in range(count)]
    out = []

    def spread(x, c):
        return jnp.broadcast_to(x[:, c : c + 1], (SUB, LANES))

    def row(x, j):
        return jnp.broadcast_to(x[j : j + 1, :], (SUB, LANES))

    for s in range(count):
        base = SUB * s
        here = (lane >= base) & (lane < base + SUB)
        cols = [spread(rows[s], base + j) for j in range(SUB)]
        work = jnp.where(here, (lane - base == sub).astype(F32), rows[s])
        done = jnp.zeros((SUB, LANES), F32)
        for j in range(0, SUB, 2):
            left, right = cols[j], cols[j + 1]
            pa, pb, pc = row(left, j), row(right, j), row(right, j + 1)
            det = pa * pc - pb * pb
            inv_det = pl.reciprocal(det, approx=True)
            top, low = row(work, j), row(work, j + 1)
            num0 = pc * top - pb * low
            num1 = pa * low - pb * top
            done = jnp.where(sub == j, top * lax.rsqrt(pa), done)
            done = jnp.where(sub == j + 1, num1 * lax.rsqrt(pa * det), done)
            pair = (sub == j) | (sub == j + 1)
            base_of = lambda v: jnp.where(pair, 0.0, v)
            mult0 = jnp.where(sub == j, -1.0, jnp.where(sub == j + 1, 0.0, left))
            mult1 = jnp.where(sub == j + 1, -1.0, jnp.where(sub == j, 0.0, right))
            work = base_of(work) - (mult0 * num0 + mult1 * num1) * inv_det
            for q in range(j + 2, SUB):
                t, l = row(cols[q], j), row(cols[q], j + 1)
                step = mult0 * (pc * t - pb * l) + mult1 * (pa * l - pb * t)
                cols[q] = base_of(cols[q]) - step * inv_det
        out.append(jnp.where(lane <= base + sub, done, 0.0))
        for i in range(s + 1, count):
            total = None
            for j in range(SUB):
                term = spread(rows[i], base + j) * row(work, j)
                total = term if total is None else total + term
            rows[i] = jnp.where(here, 0.0, rows[i]) - total
    return jnp.concatenate(out, axis=0)


def blend(before, after):
    return 1.0 + RELAX * (jnp.sqrt(before / after) - 1.0)


def update_kernel(chunks, half_v, other_v, mean_v, x_hbm, out_hbm, mean_out, full, x_buf, o_buf, in_sem, out_sem):
    members = x_buf.shape[1]
    size = x_buf.shape[0] // chunks

    def load(i):
        part = pl.ds(i * size, size)
        return pltpu.make_async_copy(x_hbm.at[part], x_buf.at[part], in_sem.at[i])

    def store(i):
        part = pl.ds(i * size, size)
        return pltpu.make_async_copy(o_buf.at[part], out_hbm.at[part], out_sem.at[i])

    for i in range(chunks):
        load(i).start()

    mine = lax.axis_index(AXIS) & 1
    span = half_v.shape[0]
    full[pl.ds(pl.multiple_of(mine * span, SUB), span), :] = half_v[...]
    full[pl.ds(pl.multiple_of((1 - mine) * span, SUB), span), :] = other_v[...]

    half = members // 2
    quarter = half // 2
    first = full[S1 : S1 + OBS, :]
    second = full[S2 : S2 + OBS, :]
    g01 = full[G0 : G0 + half, half:]
    g11 = jnp.concatenate([full[G1 : G1 + quarter, :half], full[G1 : G1 + quarter, half:]], axis=0)
    gram = jnp.concatenate(
        [full[G0 : G0 + half, :], jnp.concatenate([g01.T, g11], axis=1)], axis=0
    )
    innov1 = column(full[INNOV : INNOV + 1, :half])
    innov2 = column(full[INNOV : INNOV + 1, half:])
    eye = (
        lax.broadcasted_iota(jnp.int32, (half, half), 0) == lax.broadcasted_iota(jnp.int32, (half, half), 1)
    ).astype(F32)

    inv_m = factor(eye + dot(first, first, ((1,), (1,))))
    v_and_f = dot(inv_m, jnp.concatenate([first, innov1], axis=1))
    v, f = v_and_f[:, :members], v_and_f[:, members:]
    before = jnp.sum(eye * full[G0 : G0 + half, :half]) + jnp.sum(eye * g11)
    after1 = before - jnp.sum(dot(v, gram) * v)
    factor1 = blend(before, after1)
    v_scaled = v * jnp.concatenate([f, f], axis=1)
    increment = jnp.sum(v_scaled, axis=0, keepdims=True)
    innov2 = innov2 - jnp.sum(second * increment, axis=1, keepdims=True)

    a1 = dot(first, first, ((0,), (0,)))
    a2 = dot(second, jnp.concatenate([second, innov2], axis=1), ((0,), (0,))) * (factor1 * factor1)
    k00 = eye + a1[:half, :half] + a2[:half, :half]
    k01 = a1[:half, half:] + a2[:half, half:members]
    k11 = eye + a1[half:, half:] + a2[half:, half:members]
    inv00 = factor(k00)
    u = dot(inv00, k01)
    inv11 = factor(k11 - dot(u, u, ((0,), (0,))))
    inv10 = -dot(inv11, dot(u, inv00, ((0,), (0,))))
    y0 = dot(inv00, a2[:half, members:])
    y1 = dot(inv11, a2[half:, members:] - dot(u, y0, ((0,), (0,))))
    increment0 = jnp.sum(y0 * inv00 + y1 * inv10, axis=0, keepdims=True)
    increment1 = jnp.sum(y1 * inv11, axis=0, keepdims=True)
    increment = increment + jnp.concatenate([increment0, increment1], axis=1)
    inverse = jnp.concatenate(
        [jnp.concatenate([inv00, jnp.zeros_like(inv00)], axis=1), jnp.concatenate([inv10, inv11], axis=1)], axis=0
    )
    after2 = jnp.sum(dot(inverse, gram) * inverse)
    transform = inverse * (factor1 * blend(after1, after2))

    t_high, t_low = split(transform)
    t_all = jnp.concatenate([t_high, t_high, t_low], axis=1)
    w_high, w_low = split(increment)
    row16 = lax.broadcasted_iota(jnp.int32, (16, members), 0)
    w = jnp.where(row16 == 0, w_high.astype(F32), jnp.where(row16 == 1, w_low.astype(F32), 0.0)).astype(BF16)

    def apply(i, _):
        load(i).wait()
        part = pl.ds(pl.multiple_of(i * size, size), size)
        high, low = split(x_buf[part, :])
        o_buf[part, :] = dot(jnp.concatenate([high, low, high], axis=1), t_all, ((1,), (1,)), None)
        store(i).start()
        step = dot(w, high, ((1,), (1,)), None) + dot(w, low, ((1,), (1,)), None)
        where = pl.ds(pl.multiple_of(i * size, size), size)
        mean_out[:, where] = mean_v[:, where] + step[0:1, :] + step[1:2, :]
        return 0

    lax.fori_loop(0, chunks, apply, 0)
    for i in range(chunks):
        store(i).wait()


def spec(space):
    return pl.BlockSpec(memory_space=space)


def gather(ensemble, mean_state, observed, error_var, owner, obs_rows):
    rows, members = ensemble.shape
    chunks = 8
    return pl.pallas_call(
        functools.partial(gather_kernel, chunks),
        out_shape=jax.ShapeDtypeStruct((PACKED, members), F32),
        in_specs=[spec(pltpu.SMEM), spec(pltpu.SMEM)] + [spec(pltpu.VMEM)] * 4 + [spec(pl.ANY)],
        out_specs=spec(pltpu.VMEM),
        scratch_shapes=[
            pltpu.VMEM((rows, members), F32),
            pltpu.VMEM((OBS, members), F32),
            pltpu.SemaphoreType.DMA((chunks,)),
        ],
        compiler_params=pltpu.CompilerParams(vmem_limit_bytes=VMEM_LIMIT),
    )(owner, obs_rows, obs_rows, observed, error_var, mean_state.reshape(-1, LANES), ensemble)


def update(half, other, ensemble, mean_state):
    rows, members = ensemble.shape
    chunks = 8
    out, mean = pl.pallas_call(
        functools.partial(update_kernel, chunks),
        out_shape=(jax.ShapeDtypeStruct((rows, members), F32), jax.ShapeDtypeStruct((1, rows), F32)),
        in_specs=[spec(pltpu.VMEM)] * 3 + [spec(pl.ANY)],
        out_specs=(spec(pl.ANY), spec(pltpu.VMEM)),
        scratch_shapes=[
            pltpu.VMEM((PACKED, members), F32),
            pltpu.VMEM((rows, members), F32),
            pltpu.VMEM((rows, members), F32),
            pltpu.SemaphoreType.DMA((chunks,)),
            pltpu.SemaphoreType.DMA((chunks,)),
        ],
        compiler_params=pltpu.CompilerParams(vmem_limit_bytes=VMEM_LIMIT),
    )(half, other, mean_state.reshape(1, rows), ensemble)
    return out, mean.reshape(rows)


def swap(value, count, mask):
    return lax.ppermute(value, AXIS, [(i, i ^ mask) for i in range(count)])


def total(value, count):
    me = lax.axis_index(AXIS)
    for bit in (0, 1):
        odd = ((me >> bit) & 1) == 1
        low, high = jnp.split(value, 2, axis=0)
        value = jnp.where(odd, high, low) + swap(jnp.where(odd, low, high), count, 1 << bit)
    mask = 4
    while mask < count:
        value = value + swap(value, count, mask)
        mask *= 2
    got = swap(value, count, 2)
    odd = ((me >> 1) & 1) == 1
    value = jnp.concatenate([jnp.where(odd, got, value), jnp.where(odd, value, got)], axis=0)
    return value, swap(value, count, 1)


def on_device(count, ensemble, mean_state, observed, error_var, owner, obs_rows):
    packed = gather(ensemble, mean_state, observed, error_var, owner, obs_rows)
    half, other = total(packed, count)
    return update(half, other, ensemble, mean_state)


def solution(mesh):
    count = mesh.shape[AXIS]
    in_specs = (
        P(("groups", "rows"), None),
        P(("groups", "rows")),
        P("groups", None),
        P("groups", None),
        P("groups"),
        P("groups", None),
    )
    out_specs = (P(("groups", "rows"), None), P(("groups", "rows")))

    def body(*args):
        return on_device(count, *args)

    return jax.shard_map(body, mesh=mesh, in_specs=in_specs, out_specs=out_specs, check_vma=False)
```

profile of v0, /device:TPU:0, one launch (start us, length us, event | category | flops | bytes accessed | tf_op | source)
XLA Modules:
  0.0 63.0 jit_solution(5239057821958007185)
XLA Ops:
  0.6 0.0 copy-start
  0.6 2.2 %copy-done = f32[4096,256]{1,0:T(8,128)S(1)} copy-done((f32[4096,256]{1,0:T(8,128)S(1)}, f32[4096,256]{1,0:T(8,128)}, u32[]{:S(2)}) %copy-start) | copy-done | bytes 4194328
  2.8 0.0 copy-start.2
  2.8 0.7 %copy-done.2 = f32[4096]{0:T(1024)S(1)} copy-done((f32[4096]{0:T(1024)S(1)}, f32[4096]{0:T(1024)}, u32[]{:S(2)}) %copy-start.2) | copy-done | bytes 16408
  3.5 0.0 copy-start.4
  3.5 0.7 %copy-done.4 = s32[2,128]{1,0:T(2,128)S(1)} copy-done((s32[2,128]{1,0:T(2,128)S(1)}, s32[2,128]{1,0:T(2,128)}, u32[]{:S(2)}) %copy-start.4) | copy-done | bytes 1048
  4.2 0.0 copy-start.5
  4.2 0.7 %copy-done.5 = f32[2,128]{1,0:T(2,128)S(1)} copy-done((f32[2,128]{1,0:T(2,128)S(1)}, f32[2,128]{1,0:T(2,128)}, u32[]{:S(2)}) %copy-start.5) | copy-done | bytes 1048
  4.9 0.0 copy-start.6
  4.9 0.7 %copy-done.6 = f32[2,128]{1,0:T(2,128)S(1)} copy-done((f32[2,128]{1,0:T(2,128)S(1)}, f32[2,128]{1,0:T(2,128)}, u32[]{:S(2)}) %copy-start.6) | copy-done | bytes 1048
  5.6 0.0 copy-start.7
  5.6 0.7 %copy-done.7 = s32[2]{0:T(128)S(1)} copy-done((s32[2]{0:T(128)S(1)}, s32[2]{0:T(128)}, u32[]{:S(2)}) %copy-start.7) | copy-done | bytes 32
  6.2 0.0 copy-start.3
  6.2 7.1 %shard_map.77 = f32[480,256]{1,0:T(8,128)S(1)} custom-call(s32[2]{0:T(128)S(1)} %copy-done.7, s32[2,128]{1,0:T(2,128)S(1)} %copy-done.4, s32[2,128]{1,0:T(2,128)S(1)} %copy-done.4, f32[2,128]{1,0:T(2,128)S(1)} %copy-done.5, f32[2,128]{1,0:T(2,128)S(1)} %copy-done.6, f32[32,128]{1,0:T(8,128)S(1)} %bitcast.3, f32[4096,256]{1,0:T(8,128)S(1)} %copy-done), custom_call_target="tpu_custom_call" | custom-call | tf_op jit(solution)/shard_map/pallas_call | solution.py:244
  13.4 0.5 collective-permute-start
  13.9 1.1 %collective-permute-done = f32[240,256]{1,0:T(8,128)S(1)} collective-permute-done((f32[240,256]{1,0:T(8,128)S(1)}, f32[240,256]{1,0:T(8,128)S(1)}, u32[]{:S(2)}, u32[]{:S(2)}) %collective-permute-start) | collective-permute-done | bytes 245792 | tf_op jit(solution)/shard_map/ppermute | solution.py:279
  15.2 2.9 %collective-permute-start.1 = (f32[120,256]{1,0:T(8,128)S(1)}, f32[120,256]{1,0:T(8,128)S(1)}, u32[]{:S(2)}, u32[]{:S(2)}) collective-permute-start(f32[120,256]{1,0:T(8,128)S(1)} %slice_select_fusion.1), channel_id=1, source_target_pairs={{0,2},{1,3},{2,0},{3,1},{4,6},{5,7},{6,4},{7,5},{8,10},{9,11},{10,... | collective-permute-start | bytes 368648 | tf_op jit(solution)/shard_map/ppermute | solution.py:279
  18.1 3.6 %collective-permute-done.1 = f32[120,256]{1,0:T(8,128)S(1)} collective-permute-done((f32[120,256]{1,0:T(8,128)S(1)}, f32[120,256]{1,0:T(8,128)S(1)}, u32[]{:S(2)}, u32[]{:S(2)}) %collective-permute-start.1) | collective-permute-done | bytes 122912 | tf_op jit(solution)/shard_map/ppermute | solution.py:279
  21.8 1.9 %collective-permute-start.2 = (f32[120,256]{1,0:T(8,128)S(1)}, f32[120,256]{1,0:T(8,128)S(1)}, u32[]{:S(2)}, u32[]{:S(2)}) collective-permute-start(f32[120,256]{1,0:T(8,128)S(1)} %select_add_fusion.1), channel_id=1, source_target_pairs={{0,4},{1,5},{2,6},{3,7},{4,0},{5,1},{6,2},{7,3},{8,12},{9,13},{10,... | collective-permute-start | bytes 368648 | tf_op jit(solution)/shard_map/ppermute | solution.py:279
  23.6 3.1 %collective-permute-done.2 = f32[120,256]{1,0:T(8,128)S(1)} collective-permute-done((f32[120,256]{1,0:T(8,128)S(1)}, f32[120,256]{1,0:T(8,128)S(1)}, u32[]{:S(2)}, u32[]{:S(2)}) %collective-permute-start.2) | collective-permute-done | bytes 122912 | tf_op jit(solution)/shard_map/ppermute | solution.py:279
  26.7 2.9 %collective-permute-start.3 = (f32[120,256]{1,0:T(8,128)S(1)}, f32[120,256]{1,0:T(8,128)S(1)}, u32[]{:S(2)}, u32[]{:S(2)}) collective-permute-start(f32[120,256]{1,0:T(8,128)S(1)} %add.14), channel_id=1, source_target_pairs={{0,8},{1,9},{2,10},{3,11},{4,12},{5,13},{6,14},{7,15},{8,0},{9,1},... | collective-permute-start | bytes 368648 | tf_op jit(solution)/shard_map/ppermute | solution.py:279
  29.6 4.4 %collective-permute-done.3 = f32[120,256]{1,0:T(8,128)S(1)} collective-permute-done((f32[120,256]{1,0:T(8,128)S(1)}, f32[120,256]{1,0:T(8,128)S(1)}, u32[]{:S(2)}, u32[]{:S(2)}) %collective-permute-start.3) | collective-permute-done | bytes 122912 | tf_op jit(solution)/shard_map/ppermute | solution.py:279
  34.0 1.7 %collective-permute-start.4 = (f32[120,256]{1,0:T(8,128)S(1)}, f32[120,256]{1,0:T(8,128)S(1)}, u32[]{:S(2)}, u32[]{:S(2)}) collective-permute-start(f32[120,256]{1,0:T(8,128)S(1)} %add.15), channel_id=1, source_target_pairs={{0,2},{1,3},{2,0},{3,1},{4,6},{5,7},{6,4},{7,5},{8,10},{9,11},{10,... | collective-permute-start | bytes 368648 | tf_op jit(solution)/shard_map/ppermute | solution.py:279
  35.7 3.3 %collective-permute-done.4 = f32[120,256]{1,0:T(8,128)S(1)} collective-permute-done((f32[120,256]{1,0:T(8,128)S(1)}, f32[120,256]{1,0:T(8,128)S(1)}, u32[]{:S(2)}, u32[]{:S(2)}) %collective-permute-start.4) | collective-permute-done | bytes 122912 | tf_op jit(solution)/shard_map/ppermute | solution.py:279
  39.0 0.1 collective-permute-start.5
  39.1 1.5 %collective-permute-done.5.other_v = f32[240,256]{1,0:T(8,128)S(1)} collective-permute-done((f32[240,256]{1,0:T(8,128)S(1)}, f32[240,256]{1,0:T(8,128)S(1)}, u32[]{:S(2)}, u32[]{:S(2)}) %collective-permute-start.5) | collective-permute-done | bytes 245792 | tf_op jit(solution)/shard_map/ppermute | solution.py:279
  40.6 0.0 copy-done.3
  40.6 0.0 copy-start.1
  40.6 2.2 %copy-done.1 = f32[4096,256]{1,0:T(8,128)S(1)} copy-done((f32[4096,256]{1,0:T(8,128)S(1)}, f32[4096,256]{1,0:T(8,128)}, u32[]{:S(2)}) %copy-start.1) | copy-done | bytes 4194328
  42.8 20.1 %shard_map.78 = (f32[4096,256]{1,0:T(8,128)}, f32[1,4096]{1,0:T(1,128)}) custom-call(f32[240,256]{1,0:T(8,128)S(1)} %pad_maximum_fusion.half_v, f32[240,256]{1,0:T(8,128)S(1)} %collective-permute-done.5.other_v, f32[1,4096]{1,0:T(1,128)S(1)} %bitcast.4, f32[4096,256]{1,0:T(8,128)S(1)} %copy-done.1), custom_call_target="tpu_custom_call" | custom-call | tf_op jit(solution)/shard_map/pallas_call | solution.py:261
  (8 shorter events, 0.2 us)
Async XLA Ops:
  0.6 2.2 %copy-start = (f32[4096,256]{1,0:T(8,128)S(1)}, f32[4096,256]{1,0:T(8,128)}, u32[]{:S(2)}) copy-start(f32[4096,256]{1,0:T(8,128)} %x_hbm.3) | copy-start | bytes 12582916
  2.8 0.7 %copy-start.2 = (f32[4096]{0:T(1024)S(1)}, f32[4096]{0:T(1024)}, u32[]{:S(2)}) copy-start(f32[4096]{0:T(1024)} %param.7) | copy-start | bytes 49156
  3.5 0.7 %copy-start.4 = (s32[2,128]{1,0:T(2,128)S(1)}, s32[2,128]{1,0:T(2,128)}, u32[]{:S(2)}) copy-start(s32[2,128]{1,0:T(2,128)} %rows_v.1) | copy-start | bytes 3076
  4.2 0.7 %copy-start.5 = (f32[2,128]{1,0:T(2,128)S(1)}, f32[2,128]{1,0:T(2,128)}, u32[]{:S(2)}) copy-start(f32[2,128]{1,0:T(2,128)} %observed.1) | copy-start | bytes 3076
  4.9 0.7 %copy-start.6 = (f32[2,128]{1,0:T(2,128)S(1)}, f32[2,128]{1,0:T(2,128)}, u32[]{:S(2)}) copy-start(f32[2,128]{1,0:T(2,128)} %error_var.1) | copy-start | bytes 3076
  5.6 0.7 %copy-start.7 = (s32[2]{0:T(128)S(1)}, s32[2]{0:T(128)}, u32[]{:S(2)}) copy-start(s32[2]{0:T(128)} %owner_s.1) | copy-start | bytes 28
  6.2 34.4 %copy-start.3 = (f32[4096]{0:T(1024)S(1)}, f32[4096]{0:T(1024)}, u32[]{:S(2)}) copy-start(f32[4096]{0:T(1024)} %param.7) | copy-start | bytes 49156
  13.4 1.7 %collective-permute-start = (f32[240,256]{1,0:T(8,128)S(1)}, f32[240,256]{1,0:T(8,128)S(1)}, u32[]{:S(2)}, u32[]{:S(2)}) collective-permute-start(f32[240,256]{1,0:T(8,128)S(1)} %slice_select_fusion), channel_id=1, source_target_pairs={{0,1},{1,0},{2,3},{3,2},{4,5},{5,4},{6,7},{7,6},{8,9},{9,8},{10,11... | collective-permute-start | bytes 737288 | tf_op jit(solution)/shard_map/ppermute | solution.py:279
  15.2 6.6 %collective-permute-start.1 = (f32[120,256]{1,0:T(8,128)S(1)}, f32[120,256]{1,0:T(8,128)S(1)}, u32[]{:S(2)}, u32[]{:S(2)}) collective-permute-start(f32[120,256]{1,0:T(8,128)S(1)} %slice_select_fusion.1), channel_id=1, source_target_pairs={{0,2},{1,3},{2,0},{3,1},{4,6},{5,7},{6,4},{7,5},{8,10},{9,11},{10,... | collective-permute-start | bytes 368648 | tf_op jit(solution)/shard_map/ppermute | solution.py:279
  21.8 4.9 %collective-permute-start.2 = (f32[120,256]{1,0:T(8,128)S(1)}, f32[120,256]{1,0:T(8,128)S(1)}, u32[]{:S(2)}, u32[]{:S(2)}) collective-permute-start(f32[120,256]{1,0:T(8,128)S(1)} %select_add_fusion.1), channel_id=1, source_target_pairs={{0,4},{1,5},{2,6},{3,7},{4,0},{5,1},{6,2},{7,3},{8,12},{9,13},{10,... | collective-permute-start | bytes 368648 | tf_op jit(solution)/shard_map/ppermute | solution.py:279
  26.7 7.3 %collective-permute-start.3 = (f32[120,256]{1,0:T(8,128)S(1)}, f32[120,256]{1,0:T(8,128)S(1)}, u32[]{:S(2)}, u32[]{:S(2)}) collective-permute-start(f32[120,256]{1,0:T(8,128)S(1)} %add.14), channel_id=1, source_target_pairs={{0,8},{1,9},{2,10},{3,11},{4,12},{5,13},{6,14},{7,15},{8,0},{9,1},... | collective-permute-start | bytes 368648 | tf_op jit(solution)/shard_map/ppermute | solution.py:279
  34.0 4.9 %collective-permute-start.4 = (f32[120,256]{1,0:T(8,128)S(1)}, f32[120,256]{1,0:T(8,128)S(1)}, u32[]{:S(2)}, u32[]{:S(2)}) collective-permute-start(f32[120,256]{1,0:T(8,128)S(1)} %add.15), channel_id=1, source_target_pairs={{0,2},{1,3},{2,0},{3,1},{4,6},{5,7},{6,4},{7,5},{8,10},{9,11},{10,... | collective-permute-start | bytes 368648 | tf_op jit(solution)/shard_map/ppermute | solution.py:279
  39.0 1.6 %collective-permute-start.5 = (f32[240,256]{1,0:T(8,128)S(1)}, f32[240,256]{1,0:T(8,128)S(1)}, u32[]{:S(2)}, u32[]{:S(2)}) collective-permute-start(f32[240,256]{1,0:T(8,128)S(1)} %pad_maximum_fusion.half_v), channel_id=1, source_target_pairs={{0,1},{1,0},{2,3},{3,2},{4,5},{5,4},{6,7},{7,6},{8,9},{9,8},{10,11... | collective-permute-start | bytes 737288 | tf_op jit(solution)/shard_map/ppermute | solution.py:279
  40.6 2.2 %copy-start.1 = (f32[4096,256]{1,0:T(8,128)S(1)}, f32[4096,256]{1,0:T(8,128)}, u32[]{:S(2)}) copy-start(f32[4096,256]{1,0:T(8,128)} %x_hbm.3) | copy-start | bytes 12582916
where the time goes:
time: 63.3 us; the launch traced here: 63 us
  Pallas kernels  27.2 us (43%)
  waiting for transfers between devices  17.1 us (27%)
  starting transfers between devices  9.94 us (16%)
  local copies, waits for them, and re-layouts  7.78 us (12%)
  between operations  0.87 us (1%)
    pallas_call x1, Pallas kernels, update(): pl.pallas_call(functools.partial(update_kernel, chunks), out_shape=(jax.S...  20.1 us
    ppermute x6, waiting for transfers between devices, swap(): return lax.ppermute(value, AXIS, [(i, i ^ mask) for i in range(count)])  17.1 us
    ppermute x6, starting transfers between devices, swap(): return lax.ppermute(value, AXIS, [(i, i ^ mask) for i in range(count)])  9.94 us
    unnamed x16, local copies, waits for them, and re-layouts  7.78 us
    pallas_call x1, Pallas kernels, gather(): pl.pallas_call(functools.partial(gather_kernel, chunks), out_shape=jax.Sh...  7.13 us
  transfers between devices with their start and end apart: 6, of which 6 were waited for; matrix products, arithmetic and copies ran while one was open for 0% of the time, Pallas kernels for 0%

commit v1 on v0

--- a/solution.py
+++ b/solution.py
@@ -15,7 +15,8 @@
 LANES = 128
 SUB = 8
 OBS = 128
-VMEM_LIMIT = 40 * 1024 * 1024
+VMEM_LIMIT = 64 * 1024 * 1024
+UPDATE_LIMIT = 51 * 1024 * 1024
 
 S1, S2, G0, G1, INNOV, PACKED = 0, 128, 256, 384, 448, 480
 
@@ -34,11 +35,18 @@
 
 
 def gather_kernel(
-    chunks, owner_s, rows_s, rows_v, observed, error_var, mean_v, x_hbm, packed, x_buf, picked, sem
+    chunks, owner_h, rows_h, observed_h, error_h, mean_h, x_hbm, packed,
+    owner_s, rows_s, rows_v, observed, error_var, mean_v, x_buf, picked, sem, small_sem,
 ):
     me = lax.axis_index(AXIS)
     members = x_buf.shape[1]
     size = x_buf.shape[0] // chunks
+    pairs = (
+        (rows_h, rows_v), (observed_h, observed), (error_h, error_var), (mean_h, mean_v), (owner_h, owner_s), (rows_h, rows_s)
+    )
+    small = [pltpu.make_async_copy(a, b, small_sem.at[i]) for i, (a, b) in enumerate(pairs)]
+    for item in small:
+        item.start()
 
     def copy(i):
         part = pl.ds(i * size, size)
@@ -46,6 +54,9 @@
 
     for i in range(chunks):
         copy(i).start()
+
+    for item in small:
+        item.wait()
 
     innovations = []
     scales = []
@@ -65,12 +76,10 @@
         copy(i).wait()
         x = x_buf[pl.ds(pl.multiple_of(i * size, size), size), :]
         high = x.astype(BF16)
-        rest = x - high.astype(F32)
-        mid = rest.astype(BF16)
-        low = (rest - mid.astype(F32)).astype(BF16)
-        both = dot(high, high, ((0,), (0,)), None) + dot(mid, mid, ((0,), (0,)), None)
-        cross = dot(high, mid, ((0,), (0,)), None) + dot(high, low, ((0,), (0,)), None)
-        return carry[0] + both, carry[1] + cross
+        mid = (x - high.astype(F32)).astype(BF16)
+        first = dot(high, jnp.concatenate([high, mid], axis=1), ((0,), (0,)), None)
+        both = first[:, :members] + dot(mid, mid, ((0,), (0,)), None)
+        return carry[0] + both, carry[1] + first[:, members:]
 
     zero = jnp.zeros((members, members), F32)
     both, cross = lax.fori_loop(0, chunks, gram, (zero, zero))
@@ -244,15 +253,22 @@
     return pl.pallas_call(
         functools.partial(gather_kernel, chunks),
         out_shape=jax.ShapeDtypeStruct((PACKED, members), F32),
-        in_specs=[spec(pltpu.SMEM), spec(pltpu.SMEM)] + [spec(pltpu.VMEM)] * 4 + [spec(pl.ANY)],
+        in_specs=[spec(pltpu.HBM)] * 6,
         out_specs=spec(pltpu.VMEM),
         scratch_shapes=[
+            pltpu.SMEM(owner.shape, jnp.int32),
+            pltpu.SMEM(obs_rows.shape, jnp.int32),
+            pltpu.VMEM(obs_rows.shape, jnp.int32),
+            pltpu.VMEM(observed.shape, F32),
+            pltpu.VMEM(error_var.shape, F32),
+            pltpu.VMEM((rows // LANES, LANES), F32),
             pltpu.VMEM((rows, members), F32),
             pltpu.VMEM((OBS, members), F32),
             pltpu.SemaphoreType.DMA((chunks,)),
+            pltpu.SemaphoreType.DMA((6,)),
         ],
         compiler_params=pltpu.CompilerParams(vmem_limit_bytes=VMEM_LIMIT),
-    )(owner, obs_rows, obs_rows, observed, error_var, mean_state.reshape(-1, LANES), ensemble)
+    )(owner, obs_rows, observed, error_var, mean_state.reshape(-1, LANES), ensemble)
 
 
 def update(half, other, ensemble, mean_state):
@@ -261,8 +277,8 @@
     out, mean = pl.pallas_call(
         functools.partial(update_kernel, chunks),
         out_shape=(jax.ShapeDtypeStruct((rows, members), F32), jax.ShapeDtypeStruct((1, rows), F32)),
-        in_specs=[spec(pltpu.VMEM)] * 3 + [spec(pl.ANY)],
-        out_specs=(spec(pl.ANY), spec(pltpu.VMEM)),
+        in_specs=[spec(pltpu.VMEM)] * 3 + [spec(pltpu.HBM)],
+        out_specs=(spec(pltpu.HBM), spec(pltpu.VMEM)),
         scratch_shapes=[
             pltpu.VMEM((PACKED, members), F32),
             pltpu.VMEM((rows, members), F32),
@@ -270,7 +286,7 @@
             pltpu.SemaphoreType.DMA((chunks,)),
             pltpu.SemaphoreType.DMA((chunks,)),
         ],
-        compiler_params=pltpu.CompilerParams(vmem_limit_bytes=VMEM_LIMIT),
+        compiler_params=pltpu.CompilerParams(vmem_limit_bytes=UPDATE_LIMIT),
     )(half, other, mean_state.reshape(1, rows), ensemble)
     return out, mean.reshape(rows)
 

time: 63.3 us -> 57.8 us (0.913)
  local copies, waits for them, and re-layouts: 7.78 us -> 0.01 us
  other arithmetic: 0.2 us -> 2.32 us
    unnamed x16 -> x2, local copies, waits for them, and re-layouts: 7.78 us -> 0.01 us
    select_n x2, other arithmetic: 0.05 us -> 1.12 us  [total(): jnp.where(odd, low, high)]
    add x2, other arithmetic: 0.08 us -> 1.14 us  [total(): jnp.where(odd, high, low) + swap(jnp.where(odd, low, high), count, 1 << bit)]
    pallas_call x1, Pallas kernels: 7.13 us -> 8.03 us  [gather(): pl.pallas_call(functools.partial(gather_kernel, chunks), out_shape=jax.Sh...]
where the time goes in v1:
time: 57.8 us; the launch traced here: 57.6 us
  Pallas kernels  27.6 us (48%)
  waiting for transfers between devices  17 us (29%)
  starting transfers between devices  9.95 us (17%)
  other arithmetic  2.32 us (4%)
  between operations  0.7 us (1%)
    pallas_call x1, Pallas kernels, update(): pl.pallas_call(functools.partial(update_kernel, chunks), out_shape=(jax.S...  19.6 us
    ppermute x6, waiting for transfers between devices, swap(): return lax.ppermute(value, AXIS, [(i, i ^ mask) for i in range(count)])  17 us
    ppermute x6, starting transfers between devices, swap(): return lax.ppermute(value, AXIS, [(i, i ^ mask) for i in range(count)])  9.95 us
    pallas_call x1, Pallas kernels, gather(): pl.pallas_call(functools.partial(gather_kernel, chunks), out_shape=jax.Sh...  8.03 us
  transfers between devices with their start and end apart: 6, of which 6 were waited for; matrix products, arithmetic and copies ran while one was open for 0% of the time, Pallas kernels for 0%

profile of v1, /device:TPU:0, one launch (start us, length us, event | category | flops | bytes accessed | tf_op | source)
XLA Modules:
  0.0 57.6 jit_solution(49935419636791995)
XLA Ops:
  0.6 8.0 %shard_map.77 = f32[480,256]{1,0:T(8,128)} custom-call(s32[2]{0:T(128)} %owner_h.1, s32[2,128]{1,0:T(2,128)} %rows_h.1, f32[2,128]{1,0:T(2,128)} %observed_h.1, f32[2,128]{1,0:T(2,128)} %error_h.1, f32[32,128]{1,0:T(8,128)} %bitcast.3, f32[4096,256]{1,0:T(8,128)} %x_hbm.3), custom_call_target="tpu_custom_call" | custom-call | tf_op jit(solution)/shard_map/pallas_call | solution.py:253
  8.7 0.0 copy-start
  8.7 1.1 %slice_select_fusion = f32[240,256]{1,0:T(8,128)S(1)} fusion(f32[480,256]{1,0:T(8,128)} %shard_map.77, pred[]{:T(512)S(6)} %eq.8), kind=kLoop, calls=%fused_computation.2 | loop fusion | flops 61440 | bytes 737281 | tf_op jit(solution)/shard_map/jit(_where)/select_n | solution.py:303
  9.8 0.5 collective-permute-start
  10.3 1.1 %collective-permute-done = f32[240,256]{1,0:T(8,128)S(1)} collective-permute-done((f32[240,256]{1,0:T(8,128)S(1)}, f32[240,256]{1,0:T(8,128)S(1)}, u32[]{:S(2)}, u32[]{:S(2)}) %collective-permute-start) | collective-permute-done | bytes 245792 | tf_op jit(solution)/shard_map/ppermute | solution.py:295
  11.5 1.1 %select_add_fusion = f32[240,256]{1,0:T(8,128)S(1)} fusion(f32[240,256]{1,0:T(8,128)S(1)} %collective-permute-done, f32[480,256]{1,0:T(8,128)} %shard_map.77, pred[]{:T(512)S(6)} %eq.8), kind=kLoop, calls=%fused_computation.1 | loop fusion | flops 122880 | bytes 983041 | tf_op jit(solution)/shard_map/add | solution.py:303
  12.6 3.0 %collective-permute-start.1 = (f32[120,256]{1,0:T(8,128)S(1)}, f32[120,256]{1,0:T(8,128)S(1)}, u32[]{:S(2)}, u32[]{:S(2)}) collective-permute-start(f32[120,256]{1,0:T(8,128)S(1)} %slice_select_fusion.1), channel_id=1, source_target_pairs={{0,2},{1,3},{2,0},{3,1},{4,6},{5,7},{6,4},{7,5},{8,10},{9,11},{10,... | collective-permute-start | bytes 368648 | tf_op jit(solution)/shard_map/ppermute | solution.py:295
  15.5 3.6 %collective-permute-done.1 = f32[120,256]{1,0:T(8,128)S(1)} collective-permute-done((f32[120,256]{1,0:T(8,128)S(1)}, f32[120,256]{1,0:T(8,128)S(1)}, u32[]{:S(2)}, u32[]{:S(2)}) %collective-permute-start.1) | collective-permute-done | bytes 122912 | tf_op jit(solution)/shard_map/ppermute | solution.py:295
  19.2 1.9 %collective-permute-start.2 = (f32[120,256]{1,0:T(8,128)S(1)}, f32[120,256]{1,0:T(8,128)S(1)}, u32[]{:S(2)}, u32[]{:S(2)}) collective-permute-start(f32[120,256]{1,0:T(8,128)S(1)} %select_add_fusion.1), channel_id=1, source_target_pairs={{0,4},{1,5},{2,6},{3,7},{4,0},{5,1},{6,2},{7,3},{8,12},{9,13},{10,... | collective-permute-start | bytes 368648 | tf_op jit(solution)/shard_map/ppermute | solution.py:295
  21.1 3.1 %collective-permute-done.2 = f32[120,256]{1,0:T(8,128)S(1)} collective-permute-done((f32[120,256]{1,0:T(8,128)S(1)}, f32[120,256]{1,0:T(8,128)S(1)}, u32[]{:S(2)}, u32[]{:S(2)}) %collective-permute-start.2) | collective-permute-done | bytes 122912 | tf_op jit(solution)/shard_map/ppermute | solution.py:295
  24.2 2.9 %collective-permute-start.3 = (f32[120,256]{1,0:T(8,128)S(1)}, f32[120,256]{1,0:T(8,128)S(1)}, u32[]{:S(2)}, u32[]{:S(2)}) collective-permute-start(f32[120,256]{1,0:T(8,128)S(1)} %add.14), channel_id=1, source_target_pairs={{0,8},{1,9},{2,10},{3,11},{4,12},{5,13},{6,14},{7,15},{8,0},{9,1},... | collective-permute-start | bytes 368648 | tf_op jit(solution)/shard_map/ppermute | solution.py:295
  27.0 4.4 %collective-permute-done.3 = f32[120,256]{1,0:T(8,128)S(1)} collective-permute-done((f32[120,256]{1,0:T(8,128)S(1)}, f32[120,256]{1,0:T(8,128)S(1)}, u32[]{:S(2)}, u32[]{:S(2)}) %collective-permute-start.3) | collective-permute-done | bytes 122912 | tf_op jit(solution)/shard_map/ppermute | solution.py:295
  31.5 1.7 %collective-permute-start.4 = (f32[120,256]{1,0:T(8,128)S(1)}, f32[120,256]{1,0:T(8,128)S(1)}, u32[]{:S(2)}, u32[]{:S(2)}) collective-permute-start(f32[120,256]{1,0:T(8,128)S(1)} %add.15), channel_id=1, source_target_pairs={{0,2},{1,3},{2,0},{3,1},{4,6},{5,7},{6,4},{7,5},{8,10},{9,11},{10,... | collective-permute-start | bytes 368648 | tf_op jit(solution)/shard_map/ppermute | solution.py:295
  33.1 3.3 %collective-permute-done.4 = f32[120,256]{1,0:T(8,128)S(1)} collective-permute-done((f32[120,256]{1,0:T(8,128)S(1)}, f32[120,256]{1,0:T(8,128)S(1)}, u32[]{:S(2)}, u32[]{:S(2)}) %collective-permute-start.4) | collective-permute-done | bytes 122912 | tf_op jit(solution)/shard_map/ppermute | solution.py:295
  36.5 0.1 collective-permute-start.5
  36.6 1.5 %collective-permute-done.5.other_v = f32[240,256]{1,0:T(8,128)S(1)} collective-permute-done((f32[240,256]{1,0:T(8,128)S(1)}, f32[240,256]{1,0:T(8,128)S(1)}, u32[]{:S(2)}, u32[]{:S(2)}) %collective-permute-start.5) | collective-permute-done | bytes 245792 | tf_op jit(solution)/shard_map/ppermute | solution.py:295
  38.1 0.0 copy-done
  38.1 19.6 %shard_map.78 = (f32[4096,256]{1,0:T(8,128)}, f32[1,4096]{1,0:T(1,128)}) custom-call(f32[240,256]{1,0:T(8,128)S(1)} %pad_maximum_fusion.half_v, f32[240,256]{1,0:T(8,128)S(1)} %collective-permute-done.5.other_v, f32[1,4096]{1,0:T(1,128)S(1)} %bitcast.4, f32[4096,256]{1,0:T(8,128)} %x_hbm.3), custom_call_target="tpu_custom_call" | custom-call | tf_op jit(solution)/shard_map/pallas_call | solution.py:277
  (6 shorter events, 0.1 us)
Async XLA Ops:
  8.7 29.4 %copy-start = (f32[4096]{0:T(1024)S(1)}, f32[4096]{0:T(1024)}, u32[]{:S(2)}) copy-start(f32[4096]{0:T(1024)} %param.7) | copy-start | bytes 49156
  9.8 1.7 %collective-permute-start = (f32[240,256]{1,0:T(8,128)S(1)}, f32[240,256]{1,0:T(8,128)S(1)}, u32[]{:S(2)}, u32[]{:S(2)}) collective-permute-start(f32[240,256]{1,0:T(8,128)S(1)} %slice_select_fusion), channel_id=1, source_target_pairs={{0,1},{1,0},{2,3},{3,2},{4,5},{5,4},{6,7},{7,6},{8,9},{9,8},{10,11... | collective-permute-start | bytes 737288 | tf_op jit(solution)/shard_map/ppermute | solution.py:295
  12.6 6.6 %collective-permute-start.1 = (f32[120,256]{1,0:T(8,128)S(1)}, f32[120,256]{1,0:T(8,128)S(1)}, u32[]{:S(2)}, u32[]{:S(2)}) collective-permute-start(f32[120,256]{1,0:T(8,128)S(1)} %slice_select_fusion.1), channel_id=1, source_target_pairs={{0,2},{1,3},{2,0},{3,1},{4,6},{5,7},{6,4},{7,5},{8,10},{9,11},{10,... | collective-permute-start | bytes 368648 | tf_op jit(solution)/shard_map/ppermute | solution.py:295
  19.2 4.9 %collective-permute-start.2 = (f32[120,256]{1,0:T(8,128)S(1)}, f32[120,256]{1,0:T(8,128)S(1)}, u32[]{:S(2)}, u32[]{:S(2)}) collective-permute-start(f32[120,256]{1,0:T(8,128)S(1)} %select_add_fusion.1), channel_id=1, source_target_pairs={{0,4},{1,5},{2,6},{3,7},{4,0},{5,1},{6,2},{7,3},{8,12},{9,13},{10,... | collective-permute-start | bytes 368648 | tf_op jit(solution)/shard_map/ppermute | solution.py:295
  24.2 7.3 %collective-permute-start.3 = (f32[120,256]{1,0:T(8,128)S(1)}, f32[120,256]{1,0:T(8,128)S(1)}, u32[]{:S(2)}, u32[]{:S(2)}) collective-permute-start(f32[120,256]{1,0:T(8,128)S(1)} %add.14), channel_id=1, source_target_pairs={{0,8},{1,9},{2,10},{3,11},{4,12},{5,13},{6,14},{7,15},{8,0},{9,1},... | collective-permute-start | bytes 368648 | tf_op jit(solution)/shard_map/ppermute | solution.py:295
  31.5 4.9 %collective-permute-start.4 = (f32[120,256]{1,0:T(8,128)S(1)}, f32[120,256]{1,0:T(8,128)S(1)}, u32[]{:S(2)}, u32[]{:S(2)}) collective-permute-start(f32[120,256]{1,0:T(8,128)S(1)} %add.15), channel_id=1, source_target_pairs={{0,2},{1,3},{2,0},{3,1},{4,6},{5,7},{6,4},{7,5},{8,10},{9,11},{10,... | collective-permute-start | bytes 368648 | tf_op jit(solution)/shard_map/ppermute | solution.py:295
  36.5 1.6 %collective-permute-start.5 = (f32[240,256]{1,0:T(8,128)S(1)}, f32[240,256]{1,0:T(8,128)S(1)}, u32[]{:S(2)}, u32[]{:S(2)}) collective-permute-start(f32[240,256]{1,0:T(8,128)S(1)} %pad_maximum_fusion.half_v), channel_id=1, source_target_pairs={{0,1},{1,0},{2,3},{3,2},{4,5},{5,4},{6,7},{7,6},{8,9},{9,8},{10,11... | collective-permute-start | bytes 737288 | tf_op jit(solution)/shard_map/ppermute | solution.py:295

commit v2 on v0

v2 whole, which is shorter than its diff:
```python
import functools

import jax
import jax.numpy as jnp
from jax import lax
from jax.experimental import pallas as pl
from jax.experimental.pallas import tpu as pltpu
from jax.sharding import PartitionSpec as P

RELAX = 0.6
HI = lax.Precision.HIGHEST
AXIS = "rows"
F32 = jnp.float32
BF16 = jnp.bfloat16
LANES = 128
SUB = 8
OBS = 128
VMEM_LIMIT = 51 * 1024 * 1024
STEP = 16

G0, G1, GRAM_ROWS = 0, 128, 192
S1, S2, INNOV, OBS_ROWS = 0, 128, 256, 288


def dot(a, b, dims=((1,), (0,)), precision=HI):
    return lax.dot_general(a, b, (dims, ((), ())), precision=precision, preferred_element_type=F32)


def column(row):
    return jnp.broadcast_to(row, (LANES, LANES)).T


def split(x):
    high = x.astype(BF16)
    return high, (x - high.astype(F32)).astype(BF16)


def deal(full, keep, send):
    mine = lax.axis_index(AXIS) & 1
    span = keep.shape[0]
    keep[...] = full[pl.ds(pl.multiple_of(mine * span, SUB), span), :]
    send[...] = full[pl.ds(pl.multiple_of((1 - mine) * span, SUB), span), :]


def chunk_copy(source, target, sem, chunks):
    size = source.shape[0] // chunks

    def copy(i):
        part = pl.ds(i * size, size)
        return pltpu.make_async_copy(source.at[part], target.at[part], sem.at[i])

    return copy


def gram_kernel(chunks, x_hbm, keep, send, full, x_buf, sem):
    members = x_buf.shape[1]
    size = x_buf.shape[0] // chunks
    half = members // 2
    copy = chunk_copy(x_hbm, x_buf, sem, chunks)
    for i in range(chunks):
        copy(i).start()
    total = None
    for i in range(chunks):
        copy(i).wait()
        high, low = split(x_buf[i * size : (i + 1) * size, :])
        part = dot(high, jnp.concatenate([high, low], axis=1), ((0,), (0,)), None)
        total = part if total is None else total + part
    cross = total[:, members:]
    total = total[:, :members] + cross + cross.T
    full[G0 : G0 + half, :] = total[:half, :]
    full[G1 : G1 + half // 2, :half] = total[half : half + half // 2, half:]
    full[G1 : G1 + half // 2, half:] = total[half + half // 2 :, half:]
    deal(full, keep, send)


def gather_kernel(
    chunks, owner_s, rows_s, rows_v, observed, error_var, mean_v, x_hbm, keep, send, full, x_buf, picked, sem
):
    me = lax.axis_index(AXIS)
    members = x_buf.shape[1]
    half = members // 2
    copy = chunk_copy(x_hbm, x_buf, sem, chunks)
    for i in range(chunks):
        copy(i).start()

    full[INNOV:OBS_ROWS, :] = jnp.zeros((OBS_ROWS - INNOV, members), F32)
    scales = []
    lane = lax.broadcasted_iota(jnp.int32, (OBS, LANES), 1)
    for k in range(2):
        index = column(rows_v[k : k + 1, :].astype(F32)).astype(jnp.int32)
        prior = jnp.zeros((OBS, LANES), F32)
        for r in range(mean_v.shape[0]):
            prior = prior + jnp.where(index == lane + r * LANES, mean_v[r : r + 1, :], 0.0)
        prior = jnp.sum(prior.T, axis=0, keepdims=True)
        scale = lax.rsqrt(error_var[k : k + 1, :] * (members - 1.0))
        scale = jnp.where(owner_s[k] == me, scale, 0.0)
        full[INNOV : INNOV + 1, k * half : (k + 1) * half] = scale * (observed[k : k + 1, :] - prior)
        scales.append(column(scale))

    for i in range(chunks):
        copy(i).wait()
    for k, at in ((0, S1), (1, S2)):

        def take(o, _, k=k):
            picked[pl.ds(o, 1), :] = x_buf[pl.ds(rows_s[k, o], 1), :]
            return 0

        lax.fori_loop(0, OBS, take, 0, unroll=8)
        full[at : at + OBS, :half] = picked[:, :half] * scales[k]
        full[at : at + OBS, half:] = picked[:, half:] * scales[k]
    deal(full, keep, send)


def tree(terms):
    while len(terms) > 1:
        terms = [terms[i] + terms[i + 1] if i + 1 < len(terms) else terms[i] for i in range(0, len(terms), 2)]
    return terms[0]


def factor(a):
    count = LANES // SUB
    lane = lax.broadcasted_iota(jnp.int32, (SUB, LANES), 1)
    sub = lax.broadcasted_iota(jnp.int32, (SUB, LANES), 0)
    rows = [a[SUB * i : SUB * (i + 1), :] for i in range(count)]
    out = []

    def spread(x, c):
        return jnp.broadcast_to(x[:, c : c + 1], (SUB, LANES))

    def row(x, j):
        return jnp.broadcast_to(x[j : j + 1, :], (SUB, LANES))

    groups = STEP // SUB
    for s in range(0, count, groups):
        base = SUB * s
        here = (lane >= base) & (lane < base + STEP)
        cols = [[spread(rows[s + g], base + q) for g in range(groups)] for q in range(STEP)]
        work = [
            jnp.where(here, (lane - base == sub + SUB * g).astype(F32), rows[s + g]) for g in range(groups)
        ]
        done = [jnp.zeros((SUB, LANES), F32) for _ in range(groups)]
        for p in range(0, STEP, 2):
            at, j = divmod(p, SUB)
            first, second = sub == j, sub == j + 1
            pair = first | second
            pa, pb, pc = row(cols[p][at], j), row(cols[p][at], j + 1), row(cols[p + 1][at], j + 1)
            det = pa * pc - pb * pb
            inv = pl.reciprocal(det, approx=True)
            top, low = row(work[at], j), row(work[at], j + 1)
            done[at] = jnp.where(first, top * lax.rsqrt(pa), done[at])
            done[at] = jnp.where(second, (pa * low - pb * top) * lax.rsqrt(pa * det), done[at])
            raw, scaled = [], []
            for g in range(groups):
                m0, m1 = cols[p][g], cols[p + 1][g]
                if g == at:
                    m0 = jnp.where(first, -1.0, jnp.where(second, 0.0, m0))
                    m1 = jnp.where(second, -1.0, jnp.where(first, 0.0, m1))
                u0, u1 = m0 * pc - m1 * pb, m1 * pa - m0 * pb
                raw.append((u0, u1))
                scaled.append((u0 * inv, u1 * inv))
            for q in range(p + 2, STEP + 1):
                kept = cols[q] if q < STEP else work
                t, l = row(kept[at], j), row(kept[at], j + 1)
                moved = []
                for g in range(groups):
                    old = jnp.where(pair, 0.0, kept[g]) if g == at else kept[g]
                    if q < p + 4:
                        moved.append(old - (raw[g][0] * t + raw[g][1] * l) * inv)
                    else:
                        moved.append(old - (scaled[g][0] * t + scaled[g][1] * l))
                if q < STEP:
                    cols[q] = moved
                else:
                    work = moved
        for g in range(groups):
            out.append(jnp.where(lane <= base + SUB * g + sub, done[g], 0.0))
        lines = [row(work[p // SUB], p % SUB) for p in range(STEP)]
        for i in range(s + groups, count):
            change = tree([spread(rows[i], base + p) * lines[p] for p in range(STEP)])
            rows[i] = jnp.where(here, 0.0, rows[i]) - change
    return jnp.concatenate(out, axis=0)


def blend(before, after):
    return 1.0 + RELAX * (jnp.sqrt(before / after) - 1.0)


def join(mine, other, full):
    bit = lax.axis_index(AXIS) & 1
    span = mine.shape[0]
    full[pl.ds(pl.multiple_of(bit * span, SUB), span), :] = mine[...]
    full[pl.ds(pl.multiple_of((1 - bit) * span, SUB), span), :] = other[...]


def update_kernel(
    chunks, gram_mine, gram_other, obs_mine, obs_other, mean_v, x_hbm, out_hbm, mean_out,
    gram_full, full, x_buf, o_buf, in_sem, out_sem,
):
    members = x_buf.shape[1]
    size = x_buf.shape[0] // chunks
    load = chunk_copy(x_hbm, x_buf, in_sem, chunks)
    store = chunk_copy(o_buf, out_hbm, out_sem, chunks)
    for i in range(chunks):
        load(i).start()

    join(gram_mine, gram_other, gram_full)
    join(obs_mine, obs_other, full)

    half = members // 2
    quarter = half // 2
    first = full[S1 : S1 + OBS, :]
    second = full[S2 : S2 + OBS, :]
    g00 = gram_full[G0 : G0 + half, :half]
    g01 = gram_full[G0 : G0 + half, half:]
    g11 = jnp.concatenate([gram_full[G1 : G1 + quarter, :half], gram_full[G1 : G1 + quarter, half:]], axis=0)
    gram = jnp.concatenate(
        [jnp.concatenate([g00, g01], axis=1), jnp.concatenate([g01.T, g11], axis=1)], axis=0
    )
    innov1 = column(full[INNOV : INNOV + 1, :half])
    innov2 = column(full[INNOV : INNOV + 1, half:])
    eye = (
        lax.broadcasted_iota(jnp.int32, (half, half), 0) == lax.broadcasted_iota(jnp.int32, (half, half), 1)
    ).astype(F32)

    inv_m = factor(eye + dot(first, first, ((1,), (1,))))
    v_and_f = dot(inv_m, jnp.concatenate([first, innov1], axis=1))
    v, f = v_and_f[:, :members], v_and_f[:, members:]
    before = jnp.sum(eye * (g00 + g11))
    after1 = before - jnp.sum(dot(v, gram) * v)
    factor1 = blend(before, after1)
    v_scaled = v * jnp.concatenate([f, f], axis=1)
    increment = jnp.sum(v_scaled, axis=0, keepdims=True)
    innov2 = innov2 - jnp.sum(second * increment, axis=1, keepdims=True)

    a1 = dot(first, first, ((0,), (0,)))
    a2 = dot(second, jnp.concatenate([second, innov2], axis=1), ((0,), (0,))) * (factor1 * factor1)
    k00 = eye + a1[:half, :half] + a2[:half, :half]
    k01 = a1[:half, half:] + a2[:half, half:members]
    k11 = eye + a1[half:, half:] + a2[half:, half:members]
    inv00 = factor(k00)
    u = dot(inv00, k01)
    inv11 = factor(k11 - dot(u, u, ((0,), (0,))))
    inv10 = -dot(inv11, dot(u, inv00, ((0,), (0,))))
    y0 = dot(inv00, a2[:half, members:])
    y1 = dot(inv11, a2[half:, members:] - dot(u, y0, ((0,), (0,))))
    increment0 = jnp.sum(y0 * inv00 + y1 * inv10, axis=0, keepdims=True)
    increment1 = jnp.sum(y1 * inv11, axis=0, keepdims=True)
    increment = increment + jnp.concatenate([increment0, increment1], axis=1)
    inverse = jnp.concatenate(
        [jnp.concatenate([inv00, jnp.zeros_like(inv00)], axis=1), jnp.concatenate([inv10, inv11], axis=1)], axis=0
    )
    after2 = jnp.sum(dot(inverse, gram) * inverse)
    transform = inverse * (factor1 * blend(after1, after2))

    t_high, t_low = split(transform)
    t_all = jnp.concatenate([t_high, t_high, t_low], axis=1)
    w_high, w_low = split(increment)
    row16 = lax.broadcasted_iota(jnp.int32, (16, members), 0)
    w = jnp.where(row16 == 0, w_high.astype(F32), jnp.where(row16 == 1, w_low.astype(F32), 0.0)).astype(BF16)

    def apply(i, _):
        load(i).wait()
        part = pl.ds(pl.multiple_of(i * size, size), size)
        high, low = split(x_buf[part, :])
        o_buf[part, :] = dot(jnp.concatenate([high, low, high], axis=1), t_all, ((1,), (1,)), None)
        store(i).start()
        step = dot(w, high, ((1,), (1,)), None) + dot(w, low, ((1,), (1,)), None)
        where = pl.ds(pl.multiple_of(i * size, size), size)
        mean_out[:, where] = mean_v[:, where] + step[0:1, :] + step[1:2, :]
        return 0

    lax.fori_loop(0, chunks, apply, 0)
    for i in range(chunks):
        store(i).wait()


def spec(space):
    return pl.BlockSpec(memory_space=space)


def params():
    return pltpu.CompilerParams(vmem_limit_bytes=VMEM_LIMIT)


def gram_halves(ensemble):
    rows, members = ensemble.shape
    chunks = 4
    half = jax.ShapeDtypeStruct((GRAM_ROWS // 2, members), F32)
    return pl.pallas_call(
        functools.partial(gram_kernel, chunks),
        out_shape=(half, half),
        in_specs=[spec(pltpu.HBM)],
        out_specs=(spec(pltpu.VMEM), spec(pltpu.VMEM)),
        scratch_shapes=[
            pltpu.VMEM((GRAM_ROWS, members), F32),
            pltpu.VMEM((rows, members), F32),
            pltpu.SemaphoreType.DMA((chunks,)),
        ],
        cost_estimate=pl.CostEstimate(
            flops=4 * rows * members * members, bytes_accessed=4 * rows * members, transcendentals=0
        ),
        compiler_params=params(),
    )(ensemble)


def gather(ensemble, mean_state, observed, error_var, owner, obs_rows):
    rows, members = ensemble.shape
    chunks = 4
    half = jax.ShapeDtypeStruct((OBS_ROWS // 2, members), F32)
    return pl.pallas_call(
        functools.partial(gather_kernel, chunks),
        out_shape=(half, half),
        in_specs=[spec(pltpu.SMEM), spec(pltpu.SMEM)] + [spec(pltpu.VMEM)] * 4 + [spec(pltpu.HBM)],
        out_specs=(spec(pltpu.VMEM), spec(pltpu.VMEM)),
        scratch_shapes=[
            pltpu.VMEM((OBS_ROWS, members), F32),
            pltpu.VMEM((rows, members), F32),
            pltpu.VMEM((OBS, members), F32),
            pltpu.SemaphoreType.DMA((chunks,)),
        ],
        cost_estimate=pl.CostEstimate(
            flops=2 * rows * members * members, bytes_accessed=4 * rows * members, transcendentals=0
        ),
        compiler_params=params(),
    )(owner, obs_rows, obs_rows, observed, error_var, mean_state.reshape(-1, LANES), ensemble)


def update(gram, obs, ensemble, mean_state):
    rows, members = ensemble.shape
    chunks = 8
    out, mean = pl.pallas_call(
        functools.partial(update_kernel, chunks),
        out_shape=(jax.ShapeDtypeStruct((rows, members), F32), jax.ShapeDtypeStruct((1, rows), F32)),
        in_specs=[spec(pltpu.VMEM)] * 5 + [spec(pltpu.HBM)],
        out_specs=(spec(pltpu.HBM), spec(pltpu.VMEM)),
        scratch_shapes=[
            pltpu.VMEM((GRAM_ROWS, members), F32),
            pltpu.VMEM((OBS_ROWS, members), F32),
            pltpu.VMEM((rows, members), F32),
            pltpu.VMEM((rows, members), F32),
            pltpu.SemaphoreType.DMA((chunks,)),
            pltpu.SemaphoreType.DMA((chunks,)),
        ],
        compiler_params=params(),
    )(*gram, *obs, mean_state.reshape(1, rows), ensemble)
    return out, mean.reshape(rows)


def swap(value, count, mask):
    return lax.ppermute(value, AXIS, [(i, i ^ mask) for i in range(count)])


def total(halves, count):
    me = lax.axis_index(AXIS)
    keep, send = halves
    value = keep + swap(send, count, 1)
    odd = ((me >> 1) & 1) == 1
    low, high = jnp.split(value, 2, axis=0)
    value = jnp.where(odd, high, low) + swap(jnp.where(odd, low, high), count, 2)
    mask = 4
    while mask < count:
        value = value + swap(value, count, mask)
        mask *= 2
    got = swap(value, count, 2)
    value = jnp.concatenate([jnp.where(odd, got, value), jnp.where(odd, value, got)], axis=0)
    return value, swap(value, count, 1)


def on_device(count, ensemble, mean_state, observed, error_var, owner, obs_rows):
    gram = total(gram_halves(ensemble), count)
    obs = total(gather(ensemble, mean_state, observed, error_var, owner, obs_rows), count)
    return update(gram, obs, ensemble, mean_state)


def solution(mesh):
    count = mesh.shape[AXIS]
    in_specs = (
        P(("groups", "rows"), None),
        P(("groups", "rows")),
        P("groups", None),
        P("groups", None),
        P("groups"),
        P("groups", None),
    )
    out_specs = (P(("groups", "rows"), None), P(("groups", "rows")))

    def body(*args):
        return on_device(count, *args)

    return jax.shard_map(body, mesh=mesh, in_specs=in_specs, out_specs=out_specs, check_vma=False)
```

time: 63.3 us -> 57.1 us (0.902)
  local copies, waits for them, and re-layouts: 7.78 us -> 0.02 us
  starting transfers between devices: 9.94 us -> 13.6 us
  waiting for transfers between devices: 17.1 us -> 15.2 us
    unnamed x16 -> x10, local copies, waits for them, and re-layouts: 7.78 us -> 0.02 us
    ppermute x6 -> x12, starting transfers between devices: 9.94 us -> 13.6 us  [swap(): return lax.ppermute(value, AXIS, [(i, i ^ mask) for i in range(count)])]
    ppermute x6 -> x12, waiting for transfers between devices: 17.1 us -> 15.2 us  [swap(): return lax.ppermute(value, AXIS, [(i, i ^ mask) for i in range(count)])]
    pallas_call x1 -> x2, Pallas kernels: 7.13 us -> 7.54 us  [the longest x1 4.12 us: gather(): pl.pallas_call(functools.partial(gather_kernel, chunks), out_shape=(half,...]
  transfers between devices with their start and end apart: 6 -> 12, of which waited for: 6 -> 8; matrix products, arithmetic and copies ran while one was open for 0% -> 0% of each run, Pallas kernels for 0% -> 7%
where the time goes in v2:
time: 57.1 us; the launch traced here: 57 us
  Pallas kernels  27.1 us (47%)
  waiting for transfers between devices  15.2 us (27%)
  starting transfers between devices  13.6 us (24%)
  between operations  0.94 us (2%)
    pallas_call x1, Pallas kernels, update(): pl.pallas_call(functools.partial(update_kernel, chunks), out_shape=(jax.S...  19.5 us
    ppermute x12, waiting for transfers between devices, swap(): return lax.ppermute(value, AXIS, [(i, i ^ mask) for i in range(count)])  15.2 us
    ppermute x12, starting transfers between devices, swap(): return lax.ppermute(value, AXIS, [(i, i ^ mask) for i in range(count)])  13.6 us
    pallas_call x1, Pallas kernels, gather(): pl.pallas_call(functools.partial(gather_kernel, chunks), out_shape=(half,...  4.12 us
    pallas_call x1, Pallas kernels, gram_halves(): pl.pallas_call(functools.partial(gram_kernel, chunks), out_shape=(half, h...  3.42 us
  transfers between devices with their start and end apart: 12, of which 8 were waited for; matrix products, arithmetic and copies ran while one was open for 0% of the time, Pallas kernels for 7%

profile of v2, /device:TPU:0, one launch (start us, length us, event | category | flops | bytes accessed | tf_op | source)
XLA Modules:
  0.0 57.0 jit_solution(4365306479647823011)
XLA Ops:
  0.6 0.0 copy-start
  0.6 0.0 copy-start.1
  0.7 0.0 copy-start.4
  0.7 0.0 copy-start.3
  0.7 0.0 copy-start.2
  0.7 3.4 %shard_map.77 = (f32[96,256]{1,0:T(8,128)S(1)}, f32[96,256]{1,0:T(8,128)S(1)}) custom-call(f32[4096,256]{1,0:T(8,128)} %x_hbm.5), custom_call_target="tpu_custom_call" | custom-call | flops 1073741824 | bytes 4194304 | tf_op jit(solution)/shard_map/pallas_call | solution.py:289
  4.1 0.5 collective-permute-start
  4.6 0.0 copy-done
  4.6 0.0 copy-done.1
  4.6 0.0 copy-done.4
  4.6 0.0 copy-done.3
  4.6 0.0 copy-done.2
  4.6 4.1 %shard_map.78 = (f32[144,256]{1,0:T(8,128)S(1)}, f32[144,256]{1,0:T(8,128)S(1)}) custom-call(s32[2]{0:T(128)S(1)} %copy-done.4, s32[2,128]{1,0:T(2,128)S(1)} %copy-done.1, s32[2,128]{1,0:T(2,128)S(1)} %copy-done.1, f32[2,128]{1,0:T(2,128)S(1)} %copy-done.2, f32[2,128]{1,0:T(2,128)S(1)} %copy-done.3, f32[32,128]{1,0:T(8,128)S(1)} %bitcast.3, f32[4096,256]{1,0:T(8,128)} %x_hbm.5), custom_call_target="tpu_custom_call" | custom-call | flops 536870912 | bytes 4194304 | tf_op jit(solution)/shard_map/pallas_call | solution.py:310
  8.8 0.1 collective-permute-start.6
  8.9 0.0 collective-permute-done
  8.9 3.0 %collective-permute-start.1 = (f32[48,256]{1,0:T(8,128)S(1)}, f32[48,256]{1,0:T(8,128)S(1)}, u32[]{:S(2)}, u32[]{:S(2)}) collective-permute-start(f32[48,256]{1,0:T(8,128)S(1)} %slice_select_fusion.1), channel_id=1, source_target_pairs={{0,2},{1,3},{2,0},{3,1},{4,6},{5,7},{6,4},{7,5},{8,10},{9,11},{10,... | collective-permute-start | bytes 147464 | tf_op jit(solution)/shard_map/ppermute | solution.py:350
  12.0 0.0 collective-permute-done.6
  12.0 1.0 %collective-permute-start.7 = (f32[72,256]{1,0:T(8,128)S(1)}, f32[72,256]{1,0:T(8,128)S(1)}, u32[]{:S(2)}, u32[]{:S(2)}) collective-permute-start(f32[72,256]{1,0:T(8,128)S(1)} %slice_select_fusion), channel_id=1, source_target_pairs={{0,2},{1,3},{2,0},{3,1},{4,6},{5,7},{6,4},{7,5},{8,10},{9,11},{10,... | collective-permute-start | bytes 221192 | tf_op jit(solution)/shard_map/ppermute | solution.py:350
  13.0 1.0 %collective-permute-done.1 = f32[48,256]{1,0:T(8,128)S(1)} collective-permute-done((f32[48,256]{1,0:T(8,128)S(1)}, f32[48,256]{1,0:T(8,128)S(1)}, u32[]{:S(2)}, u32[]{:S(2)}) %collective-permute-start.1) | collective-permute-done | bytes 49184 | tf_op jit(solution)/shard_map/ppermute | solution.py:350
  14.1 2.4 %collective-permute-done.7 = f32[72,256]{1,0:T(8,128)S(1)} collective-permute-done((f32[72,256]{1,0:T(8,128)S(1)}, f32[72,256]{1,0:T(8,128)S(1)}, u32[]{:S(2)}, u32[]{:S(2)}) %collective-permute-start.7) | collective-permute-done | bytes 73760 | tf_op jit(solution)/shard_map/ppermute | solution.py:350
  16.5 1.6 %collective-permute-start.8 = (f32[72,256]{1,0:T(8,128)S(1)}, f32[72,256]{1,0:T(8,128)S(1)}, u32[]{:S(2)}, u32[]{:S(2)}) collective-permute-start(f32[72,256]{1,0:T(8,128)S(1)} %select_add_fusion), channel_id=1, source_target_pairs={{0,4},{1,5},{2,6},{3,7},{4,0},{5,1},{6,2},{7,3},{8,12},{9,13},{10,... | collective-permute-start | bytes 221192 | tf_op jit(solution)/shard_map/ppermute | solution.py:350
  18.1 0.4 collective-permute-start.2
  18.5 3.6 %collective-permute-done.2 = f32[48,256]{1,0:T(8,128)S(1)} collective-permute-done((f32[48,256]{1,0:T(8,128)S(1)}, f32[48,256]{1,0:T(8,128)S(1)}, u32[]{:S(2)}, u32[]{:S(2)}) %collective-permute-start.2) | collective-permute-done | bytes 49184 | tf_op jit(solution)/shard_map/ppermute | solution.py:350
  22.2 3.0 %collective-permute-start.3 = (f32[48,256]{1,0:T(8,128)S(1)}, f32[48,256]{1,0:T(8,128)S(1)}, u32[]{:S(2)}, u32[]{:S(2)}) collective-permute-start(f32[48,256]{1,0:T(8,128)S(1)} %add.26), channel_id=1, source_target_pairs={{0,8},{1,9},{2,10},{3,11},{4,12},{5,13},{6,14},{7,15},{8,0},{9,1},... | collective-permute-start | bytes 147464 | tf_op jit(solution)/shard_map/ppermute | solution.py:350
  25.2 0.0 collective-permute-done.8
  25.3 0.1 collective-permute-start.9
  25.3 2.7 %collective-permute-done.3 = f32[48,256]{1,0:T(8,128)S(1)} collective-permute-done((f32[48,256]{1,0:T(8,128)S(1)}, f32[48,256]{1,0:T(8,128)S(1)}, u32[]{:S(2)}, u32[]{:S(2)}) %collective-permute-start.3) | collective-permute-done | bytes 49184 | tf_op jit(solution)/shard_map/ppermute | solution.py:350
  28.1 2.0 %collective-permute-start.4 = (f32[48,256]{1,0:T(8,128)S(1)}, f32[48,256]{1,0:T(8,128)S(1)}, u32[]{:S(2)}, u32[]{:S(2)}) collective-permute-start(f32[48,256]{1,0:T(8,128)S(1)} %add.27), channel_id=1, source_target_pairs={{0,2},{1,3},{2,0},{3,1},{4,6},{5,7},{6,4},{7,5},{8,10},{9,11},{10,... | collective-permute-start | bytes 147464 | tf_op jit(solution)/shard_map/ppermute | solution.py:350
  30.1 1.1 %collective-permute-done.9 = f32[72,256]{1,0:T(8,128)S(1)} collective-permute-done((f32[72,256]{1,0:T(8,128)S(1)}, f32[72,256]{1,0:T(8,128)S(1)}, u32[]{:S(2)}, u32[]{:S(2)}) %collective-permute-start.9) | collective-permute-done | bytes 73760 | tf_op jit(solution)/shard_map/ppermute | solution.py:350
  31.2 1.0 %collective-permute-start.10 = (f32[72,256]{1,0:T(8,128)S(1)}, f32[72,256]{1,0:T(8,128)S(1)}, u32[]{:S(2)}, u32[]{:S(2)}) collective-permute-start(f32[72,256]{1,0:T(8,128)S(1)} %add.31), channel_id=1, source_target_pairs={{0,2},{1,3},{2,0},{3,1},{4,6},{5,7},{6,4},{7,5},{8,10},{9,11},{10,... | collective-permute-start | bytes 221192 | tf_op jit(solution)/shard_map/ppermute | solution.py:350
  32.3 0.4 collective-permute-done.4
  32.7 3.0 %collective-permute-done.10 = f32[72,256]{1,0:T(8,128)S(1)} collective-permute-done((f32[72,256]{1,0:T(8,128)S(1)}, f32[72,256]{1,0:T(8,128)S(1)}, u32[]{:S(2)}, u32[]{:S(2)}) %collective-permute-start.10) | collective-permute-done | bytes 73760 | tf_op jit(solution)/shard_map/ppermute | solution.py:350
  35.7 0.1 collective-permute-start.11
  35.8 0.5 collective-permute-start.5
  36.3 0.9 %collective-permute-done.5.gram_other = f32[96,256]{1,0:T(8,128)S(1)} collective-permute-done((f32[96,256]{1,0:T(8,128)S(1)}, f32[96,256]{1,0:T(8,128)S(1)}, u32[]{:S(2)}, u32[]{:S(2)}) %collective-permute-start.5) | collective-permute-done | bytes 98336 | tf_op jit(solution)/shard_map/ppermute | solution.py:350
  37.3 0.0 collective-permute-done.11.obs_other
  37.3 19.5 %shard_map.79 = (f32[4096,256]{1,0:T(8,128)}, f32[1,4096]{1,0:T(1,128)}) custom-call(f32[96,256]{1,0:T(8,128)S(1)} %pad_maximum_fusion.1.gram_mine, f32[96,256]{1,0:T(8,128)S(1)} %collective-permute-done.5.gram_other, f32[144,256]{1,0:T(8,128)S(1)} %pad_maximum_fusion.obs_mine, f32[144,256]{1,0:T(8,128)S(1)} %collective-permute-done.11.obs_other, ...), custom_call_target="tpu_custom_call" | custom-call | tf_op jit(solution)/shard_map/pallas_call | solution.py:331
  (14 shorter events, 0.2 us)
Async XLA Ops:
  0.6 4.0 %copy-start = (f32[4096]{0:T(1024)S(1)}, f32[4096]{0:T(1024)}, u32[]{:S(2)}) copy-start(f32[4096]{0:T(1024)} %param.7) | copy-start | bytes 49156
  0.6 4.0 %copy-start.1 = (s32[2,128]{1,0:T(2,128)S(1)}, s32[2,128]{1,0:T(2,128)}, u32[]{:S(2)}) copy-start(s32[2,128]{1,0:T(2,128)} %rows_v.1) | copy-start | bytes 3076
  0.7 4.0 %copy-start.4 = (s32[2]{0:T(128)S(1)}, s32[2]{0:T(128)}, u32[]{:S(2)}) copy-start(s32[2]{0:T(128)} %owner_s.1) | copy-start | bytes 28
  0.7 4.0 %copy-start.3 = (f32[2,128]{1,0:T(2,128)S(1)}, f32[2,128]{1,0:T(2,128)}, u32[]{:S(2)}) copy-start(f32[2,128]{1,0:T(2,128)} %error_var.1) | copy-start | bytes 3076
  0.7 4.0 %copy-start.2 = (f32[2,128]{1,0:T(2,128)S(1)}, f32[2,128]{1,0:T(2,128)}, u32[]{:S(2)}) copy-start(f32[2,128]{1,0:T(2,128)} %observed.1) | copy-start | bytes 3076
  4.1 4.8 %collective-permute-start = (f32[96,256]{1,0:T(8,128)S(1)}, f32[96,256]{1,0:T(8,128)S(1)}, u32[]{:S(2)}, u32[]{:S(2)}) collective-permute-start(f32[96,256]{1,0:T(8,128)S(1)} %get-tuple-element.9), channel_id=1, source_target_pairs={{0,1},{1,0},{2,3},{3,2},{4,5},{5,4},{6,7},{7,6},{8,9},{9,8},{10,11... | collective-permute-start | bytes 294920 | tf_op jit(solution)/shard_map/ppermute | solution.py:350
  8.8 3.2 %collective-permute-start.6 = (f32[144,256]{1,0:T(8,128)S(1)}, f32[144,256]{1,0:T(8,128)S(1)}, u32[]{:S(2)}, u32[]{:S(2)}) collective-permute-start(f32[144,256]{1,0:T(8,128)S(1)} %get-tuple-element.11), channel_id=1, source_target_pairs={{0,1},{1,0},{2,3},{3,2},{4,5},{5,4},{6,7},{7,6},{8,9},{9,8},{10,11... | collective-permute-start | bytes 442376 | tf_op jit(solution)/shard_map/ppermute | solution.py:350
  8.9 5.1 %collective-permute-start.1 = (f32[48,256]{1,0:T(8,128)S(1)}, f32[48,256]{1,0:T(8,128)S(1)}, u32[]{:S(2)}, u32[]{:S(2)}) collective-permute-start(f32[48,256]{1,0:T(8,128)S(1)} %slice_select_fusion.1), channel_id=1, source_target_pairs={{0,2},{1,3},{2,0},{3,1},{4,6},{5,7},{6,4},{7,5},{8,10},{9,11},{10,... | collective-permute-start | bytes 147464 | tf_op jit(solution)/shard_map/ppermute | solution.py:350
  12.0 4.4 %collective-permute-start.7 = (f32[72,256]{1,0:T(8,128)S(1)}, f32[72,256]{1,0:T(8,128)S(1)}, u32[]{:S(2)}, u32[]{:S(2)}) collective-permute-start(f32[72,256]{1,0:T(8,128)S(1)} %slice_select_fusion), channel_id=1, source_target_pairs={{0,2},{1,3},{2,0},{3,1},{4,6},{5,7},{6,4},{7,5},{8,10},{9,11},{10,... | collective-permute-start | bytes 221192 | tf_op jit(solution)/shard_map/ppermute | solution.py:350
  16.5 8.8 %collective-permute-start.8 = (f32[72,256]{1,0:T(8,128)S(1)}, f32[72,256]{1,0:T(8,128)S(1)}, u32[]{:S(2)}, u32[]{:S(2)}) collective-permute-start(f32[72,256]{1,0:T(8,128)S(1)} %select_add_fusion), channel_id=1, source_target_pairs={{0,4},{1,5},{2,6},{3,7},{4,0},{5,1},{6,2},{7,3},{8,12},{9,13},{10,... | collective-permute-start | bytes 221192 | tf_op jit(solution)/shard_map/ppermute | solution.py:350
  18.1 4.1 %collective-permute-start.2 = (f32[48,256]{1,0:T(8,128)S(1)}, f32[48,256]{1,0:T(8,128)S(1)}, u32[]{:S(2)}, u32[]{:S(2)}) collective-permute-start(f32[48,256]{1,0:T(8,128)S(1)} %select_add_fusion.1), channel_id=1, source_target_pairs={{0,4},{1,5},{2,6},{3,7},{4,0},{5,1},{6,2},{7,3},{8,12},{9,13},{10,... | collective-permute-start | bytes 147464 | tf_op jit(solution)/shard_map/ppermute | solution.py:350
  22.2 5.9 %collective-permute-start.3 = (f32[48,256]{1,0:T(8,128)S(1)}, f32[48,256]{1,0:T(8,128)S(1)}, u32[]{:S(2)}, u32[]{:S(2)}) collective-permute-start(f32[48,256]{1,0:T(8,128)S(1)} %add.26), channel_id=1, source_target_pairs={{0,8},{1,9},{2,10},{3,11},{4,12},{5,13},{6,14},{7,15},{8,0},{9,1},... | collective-permute-start | bytes 147464 | tf_op jit(solution)/shard_map/ppermute | solution.py:350
  25.3 5.9 %collective-permute-start.9 = (f32[72,256]{1,0:T(8,128)S(1)}, f32[72,256]{1,0:T(8,128)S(1)}, u32[]{:S(2)}, u32[]{:S(2)}) collective-permute-start(f32[72,256]{1,0:T(8,128)S(1)} %add.30), channel_id=1, source_target_pairs={{0,8},{1,9},{2,10},{3,11},{4,12},{5,13},{6,14},{7,15},{8,0},{9,1},... | collective-permute-start | bytes 221192 | tf_op jit(solution)/shard_map/ppermute | solution.py:350
  28.1 4.6 %collective-permute-start.4 = (f32[48,256]{1,0:T(8,128)S(1)}, f32[48,256]{1,0:T(8,128)S(1)}, u32[]{:S(2)}, u32[]{:S(2)}) collective-permute-start(f32[48,256]{1,0:T(8,128)S(1)} %add.27), channel_id=1, source_target_pairs={{0,2},{1,3},{2,0},{3,1},{4,6},{5,7},{6,4},{7,5},{8,10},{9,11},{10,... | collective-permute-start | bytes 147464 | tf_op jit(solution)/shard_map/ppermute | solution.py:350
  31.2 4.4 %collective-permute-start.10 = (f32[72,256]{1,0:T(8,128)S(1)}, f32[72,256]{1,0:T(8,128)S(1)}, u32[]{:S(2)}, u32[]{:S(2)}) collective-permute-start(f32[72,256]{1,0:T(8,128)S(1)} %add.31), channel_id=1, source_target_pairs={{0,2},{1,3},{2,0},{3,1},{4,6},{5,7},{6,4},{7,5},{8,10},{9,11},{10,... | collective-permute-start | bytes 221192 | tf_op jit(solution)/shard_map/ppermute | solution.py:350
  35.7 1.6 %collective-permute-start.11 = (f32[144,256]{1,0:T(8,128)S(1)}, f32[144,256]{1,0:T(8,128)S(1)}, u32[]{:S(2)}, u32[]{:S(2)}) collective-permute-start(f32[144,256]{1,0:T(8,128)S(1)} %pad_maximum_fusion.obs_mine), channel_id=1, source_target_pairs={{0,1},{1,0},{2,3},{3,2},{4,5},{5,4},{6,7},{7,6},{8,9},{9,8},{10,11... | collective-permute-start | bytes 442376 | tf_op jit(solution)/shard_map/ppermute | solution.py:350
  35.8 1.5 %collective-permute-start.5 = (f32[96,256]{1,0:T(8,128)S(1)}, f32[96,256]{1,0:T(8,128)S(1)}, u32[]{:S(2)}, u32[]{:S(2)}) collective-permute-start(f32[96,256]{1,0:T(8,128)S(1)} %pad_maximum_fusion.1.gram_mine), channel_id=1, source_target_pairs={{0,1},{1,0},{2,3},{3,2},{4,5},{5,4},{6,7},{7,6},{8,9},{9,8},{10,11... | collective-permute-start | bytes 294920 | tf_op jit(solution)/shard_map/ppermute | solution.py:350

commit v3 on v2

--- a/solution.py
+++ b/solution.py
@@ -18,8 +18,8 @@
 VMEM_LIMIT = 51 * 1024 * 1024
 STEP = 16
 
-G0, G1, GRAM_ROWS = 0, 128, 192
-S1, S2, INNOV, OBS_ROWS = 0, 128, 256, 288
+FIRST_ROWS, FIRST_HALF = 64, 80
+GRAM_ROWS, SECOND_ROWS, SECOND_HALF = 96, 64, 160
 
 
 def dot(a, b, dims=((1,), (0,)), precision=HI):
@@ -35,11 +35,9 @@
     return high, (x - high.astype(F32)).astype(BF16)
 
 
-def deal(full, keep, send):
+def halves(full, span):
     mine = lax.axis_index(AXIS) & 1
-    span = keep.shape[0]
-    keep[...] = full[pl.ds(pl.multiple_of(mine * span, SUB), span), :]
-    send[...] = full[pl.ds(pl.multiple_of((1 - mine) * span, SUB), span), :]
+    return [full[pl.ds(pl.multiple_of(bit * span, SUB), span), :] for bit in (mine, 1 - mine)]
 
 
 def chunk_copy(source, target, sem, chunks):
@@ -67,14 +65,15 @@
         total = part if total is None else total + part
     cross = total[:, members:]
     total = total[:, :members] + cross + cross.T
-    full[G0 : G0 + half, :] = total[:half, :]
-    full[G1 : G1 + half // 2, :half] = total[half : half + half // 2, half:]
-    full[G1 : G1 + half // 2, half:] = total[half + half // 2 :, half:]
-    deal(full, keep, send)
+    full[:half, :] = total[:half, :]
+    full[half:, :half] = total[half : half + half // 2, half:]
+    full[half:, half:] = total[half + half // 2 :, half:]
+    keep[...], send[...] = halves(full, GRAM_ROWS)
 
 
 def gather_kernel(
-    chunks, owner_s, rows_s, rows_v, observed, error_var, mean_v, x_hbm, keep, send, full, x_buf, picked, sem
+    chunks, owner_s, rows_s, rows_v, observed, error_var, mean_v, gram_keep, gram_send, x_hbm,
+    first_keep, first_send, second_keep, second_send, picked, x_buf, sem,
 ):
     me = lax.axis_index(AXIS)
     members = x_buf.shape[1]
@@ -83,7 +82,9 @@
     for i in range(chunks):
         copy(i).start()
 
-    full[INNOV:OBS_ROWS, :] = jnp.zeros((OBS_ROWS - INNOV, members), F32)
+    second_keep[:GRAM_ROWS, :] = gram_keep[...]
+    second_send[:GRAM_ROWS, :] = gram_send[...]
+    innovations = []
     scales = []
     lane = lax.broadcasted_iota(jnp.int32, (OBS, LANES), 1)
     for k in range(2):
@@ -94,21 +95,25 @@
         prior = jnp.sum(prior.T, axis=0, keepdims=True)
         scale = lax.rsqrt(error_var[k : k + 1, :] * (members - 1.0))
         scale = jnp.where(owner_s[k] == me, scale, 0.0)
-        full[INNOV : INNOV + 1, k * half : (k + 1) * half] = scale * (observed[k : k + 1, :] - prior)
+        innovations.append(scale * (observed[k : k + 1, :] - prior))
         scales.append(column(scale))
+    line = lax.broadcasted_iota(jnp.int32, (FIRST_HALF - FIRST_ROWS, members), 0)
+    tail = jnp.where(line == 0, jnp.concatenate(innovations, axis=1), 0.0)
+    first_keep[FIRST_ROWS:, :] = tail
+    first_send[FIRST_ROWS:, :] = tail
 
     for i in range(chunks):
         copy(i).wait()
-    for k, at in ((0, S1), (1, S2)):
+    for k, keep, send, at in ((0, first_keep, first_send, 0), (1, second_keep, second_send, GRAM_ROWS)):
 
         def take(o, _, k=k):
             picked[pl.ds(o, 1), :] = x_buf[pl.ds(rows_s[k, o], 1), :]
             return 0
 
-        lax.fori_loop(0, OBS, take, 0, unroll=8)
-        full[at : at + OBS, :half] = picked[:, :half] * scales[k]
-        full[at : at + OBS, half:] = picked[:, half:] * scales[k]
-    deal(full, keep, send)
+        lax.fori_loop(0, OBS, take, 0, unroll=16)
+        picked[:, :half] = picked[:, :half] * scales[k]
+        picked[:, half:] = picked[:, half:] * scales[k]
+        keep[at : at + OBS // 2, :], send[at : at + OBS // 2, :] = halves(picked, OBS // 2)
 
 
 def tree(terms):
@@ -185,16 +190,37 @@
     return 1.0 + RELAX * (jnp.sqrt(before / after) - 1.0)
 
 
-def join(mine, other, full):
+def join(mine, other, full, at, span):
     bit = lax.axis_index(AXIS) & 1
-    span = mine.shape[0]
-    full[pl.ds(pl.multiple_of(bit * span, SUB), span), :] = mine[...]
-    full[pl.ds(pl.multiple_of((1 - bit) * span, SUB), span), :] = other[...]
+    full[pl.ds(pl.multiple_of(bit * span, SUB), span), :] = mine[at : at + span, :]
+    full[pl.ds(pl.multiple_of((1 - bit) * span, SUB), span), :] = other[at : at + span, :]
+
+
+def identity(size):
+    return (
+        lax.broadcasted_iota(jnp.int32, (size, size), 0) == lax.broadcasted_iota(jnp.int32, (size, size), 1)
+    ).astype(F32)
+
+
+def first_kernel(mine, other, v_out, system_out, extra_out, full):
+    join(mine, other, full, 0, FIRST_ROWS)
+    rows = full[...]
+    members = rows.shape[1]
+    half = members // 2
+    innovations = mine[FIRST_ROWS : FIRST_ROWS + 1, :]
+    inv_m = factor(identity(OBS) + dot(rows, rows, ((1,), (1,))))
+    v_and_f = dot(inv_m, jnp.concatenate([rows, column(innovations[:, :half])], axis=1))
+    v, f = v_and_f[:, :members], v_and_f[:, members:]
+    v_out[...] = v
+    system_out[...] = identity(members) + dot(rows, rows, ((0,), (0,)))
+    increment = jnp.sum(v * jnp.concatenate([f, f], axis=1), axis=0, keepdims=True)
+    line = lax.broadcasted_iota(jnp.int32, (SUB, members), 0)
+    extra_out[...] = jnp.where(line == 0, increment, jnp.where(line == 1, innovations, 0.0))
 
 
 def update_kernel(
-    chunks, gram_mine, gram_other, obs_mine, obs_other, mean_v, x_hbm, out_hbm, mean_out,
-    gram_full, full, x_buf, o_buf, in_sem, out_sem,
+    chunks, mine, other, v_in, system, extra, mean_v, x_hbm, out_hbm, mean_out,
+    gram_full, obs_full, x_buf, o_buf, in_sem, out_sem,
 ):
     members = x_buf.shape[1]
     size = x_buf.shape[0] // chunks
@@ -203,40 +229,28 @@
     for i in range(chunks):
         load(i).start()
 
-    join(gram_mine, gram_other, gram_full)
-    join(obs_mine, obs_other, full)
-
+    join(mine, other, gram_full, 0, GRAM_ROWS)
+    join(mine, other, obs_full, GRAM_ROWS, SECOND_ROWS)
     half = members // 2
     quarter = half // 2
-    first = full[S1 : S1 + OBS, :]
-    second = full[S2 : S2 + OBS, :]
-    g00 = gram_full[G0 : G0 + half, :half]
-    g01 = gram_full[G0 : G0 + half, half:]
-    g11 = jnp.concatenate([gram_full[G1 : G1 + quarter, :half], gram_full[G1 : G1 + quarter, half:]], axis=0)
+    second = obs_full[...]
+    g00 = gram_full[:half, :half]
+    g01 = gram_full[:half, half:]
+    g11 = jnp.concatenate([gram_full[half:, :half], gram_full[half:, half:]], axis=0)
     gram = jnp.concatenate(
         [jnp.concatenate([g00, g01], axis=1), jnp.concatenate([g01.T, g11], axis=1)], axis=0
     )
-    innov1 = column(full[INNOV : INNOV + 1, :half])
-    innov2 = column(full[INNOV : INNOV + 1, half:])
-    eye = (
-        lax.broadcasted_iota(jnp.int32, (half, half), 0) == lax.broadcasted_iota(jnp.int32, (half, half), 1)
-    ).astype(F32)
-
-    inv_m = factor(eye + dot(first, first, ((1,), (1,))))
-    v_and_f = dot(inv_m, jnp.concatenate([first, innov1], axis=1))
-    v, f = v_and_f[:, :members], v_and_f[:, members:]
-    before = jnp.sum(eye * (g00 + g11))
+    v = v_in[...]
+    increment = extra[0:1, :]
+    innov2 = column(extra[1:2, half:]) - jnp.sum(second * increment, axis=1, keepdims=True)
+    before = jnp.sum(identity(half) * (g00 + g11))
     after1 = before - jnp.sum(dot(v, gram) * v)
     factor1 = blend(before, after1)
-    v_scaled = v * jnp.concatenate([f, f], axis=1)
-    increment = jnp.sum(v_scaled, axis=0, keepdims=True)
-    innov2 = innov2 - jnp.sum(second * increment, axis=1, keepdims=True)
-
-    a1 = dot(first, first, ((0,), (0,)))
+
     a2 = dot(second, jnp.concatenate([second, innov2], axis=1), ((0,), (0,))) * (factor1 * factor1)
-    k00 = eye + a1[:half, :half] + a2[:half, :half]
-    k01 = a1[:half, half:] + a2[:half, half:members]
-    k11 = eye + a1[half:, half:] + a2[half:, half:members]
+    k00 = system[:half, :half] + a2[:half, :half]
+    k01 = system[:half, half:] + a2[:half, half:members]
+    k11 = system[half:, half:] + a2[half:, half:members]
     inv00 = factor(k00)
     u = dot(inv00, k01)
     inv11 = factor(k11 - dot(u, u, ((0,), (0,))))
@@ -282,67 +296,85 @@
     return pltpu.CompilerParams(vmem_limit_bytes=VMEM_LIMIT)
 
 
+def cost(flops, bytes_accessed):
+    return pl.CostEstimate(flops=flops, bytes_accessed=bytes_accessed, transcendentals=0)
+
+
 def gram_halves(ensemble):
     rows, members = ensemble.shape
     chunks = 4
-    half = jax.ShapeDtypeStruct((GRAM_ROWS // 2, members), F32)
+    half = jax.ShapeDtypeStruct((GRAM_ROWS, members), F32)
     return pl.pallas_call(
         functools.partial(gram_kernel, chunks),
         out_shape=(half, half),
         in_specs=[spec(pltpu.HBM)],
         out_specs=(spec(pltpu.VMEM), spec(pltpu.VMEM)),
         scratch_shapes=[
-            pltpu.VMEM((GRAM_ROWS, members), F32),
+            pltpu.VMEM((2 * GRAM_ROWS, members), F32),
             pltpu.VMEM((rows, members), F32),
             pltpu.SemaphoreType.DMA((chunks,)),
         ],
-        cost_estimate=pl.CostEstimate(
-            flops=4 * rows * members * members, bytes_accessed=4 * rows * members, transcendentals=0
-        ),
+        cost_estimate=cost(4 * rows * members * members, 4 * rows * members),
         compiler_params=params(),
     )(ensemble)
 
 
-def gather(ensemble, mean_state, observed, error_var, owner, obs_rows):
+def gather(ensemble, mean_state, observed, error_var, owner, obs_rows, gram):
     rows, members = ensemble.shape
     chunks = 4
-    half = jax.ShapeDtypeStruct((OBS_ROWS // 2, members), F32)
-    return pl.pallas_call(
+    first = jax.ShapeDtypeStruct((FIRST_HALF, members), F32)
+    second = jax.ShapeDtypeStruct((SECOND_HALF, members), F32)
+    out = pl.pallas_call(
         functools.partial(gather_kernel, chunks),
-        out_shape=(half, half),
-        in_specs=[spec(pltpu.SMEM), spec(pltpu.SMEM)] + [spec(pltpu.VMEM)] * 4 + [spec(pltpu.HBM)],
-        out_specs=(spec(pltpu.VMEM), spec(pltpu.VMEM)),
+        out_shape=(first, first, second, second),
+        in_specs=[spec(pltpu.SMEM), spec(pltpu.SMEM)] + [spec(pltpu.VMEM)] * 6 + [spec(pltpu.HBM)],
+        out_specs=[spec(pltpu.VMEM)] * 4,
         scratch_shapes=[
-            pltpu.VMEM((OBS_ROWS, members), F32),
+            pltpu.VMEM((OBS, members), F32),
             pltpu.VMEM((rows, members), F32),
-            pltpu.VMEM((OBS, members), F32),
             pltpu.SemaphoreType.DMA((chunks,)),
         ],
-        cost_estimate=pl.CostEstimate(
-            flops=2 * rows * members * members, bytes_accessed=4 * rows * members, transcendentals=0
+        cost_estimate=cost(2 * rows * members * members, 4 * rows * members),
+        compiler_params=params(),
+    )(owner, obs_rows, obs_rows, observed, error_var, mean_state.reshape(-1, LANES), *gram, ensemble)
+    return out[:2], out[2:]
+
+
+def first_batch(first):
+    members = first[0].shape[1]
+    return pl.pallas_call(
+        first_kernel,
+        out_shape=(
+            jax.ShapeDtypeStruct((OBS, members), F32),
+            jax.ShapeDtypeStruct((members, members), F32),
+            jax.ShapeDtypeStruct((SUB, members), F32),
         ),
+        in_specs=[spec(pltpu.VMEM)] * 2,
+        out_specs=[spec(pltpu.VMEM)] * 3,
+        scratch_shapes=[pltpu.VMEM((OBS, members), F32)],
+        cost_estimate=cost(5 * 10**9, 2 * OBS * members * 4),
         compiler_params=params(),
-    )(owner, obs_rows, obs_rows, observed, error_var, mean_state.reshape(-1, LANES), ensemble)
-
-
-def update(gram, obs, ensemble, mean_state):
+    )(*first)
+
+
+def update(second, batch, ensemble, mean_state):
     rows, members = ensemble.shape
     chunks = 8
     out, mean = pl.pallas_call(
         functools.partial(update_kernel, chunks),
         out_shape=(jax.ShapeDtypeStruct((rows, members), F32), jax.ShapeDtypeStruct((1, rows), F32)),
-        in_specs=[spec(pltpu.VMEM)] * 5 + [spec(pltpu.HBM)],
+        in_specs=[spec(pltpu.VMEM)] * 6 + [spec(pltpu.HBM)],
         out_specs=(spec(pltpu.HBM), spec(pltpu.VMEM)),
         scratch_shapes=[
-            pltpu.VMEM((GRAM_ROWS, members), F32),
-            pltpu.VMEM((OBS_ROWS, members), F32),
+            pltpu.VMEM((2 * GRAM_ROWS, members), F32),
+            pltpu.VMEM((OBS, members), F32),
             pltpu.VMEM((rows, members), F32),
             pltpu.VMEM((rows, members), F32),
             pltpu.SemaphoreType.DMA((chunks,)),
             pltpu.SemaphoreType.DMA((chunks,)),
         ],
         compiler_params=params(),
-    )(*gram, *obs, mean_state.reshape(1, rows), ensemble)
+    )(*second, *batch, mean_state.reshape(1, rows), ensemble)
     return out, mean.reshape(rows)
 
 
@@ -350,7 +382,7 @@
     return lax.ppermute(value, AXIS, [(i, i ^ mask) for i in range(count)])
 
 
-def total(halves, count):
+def total(halves, count, beside=None):
     me = lax.axis_index(AXIS)
     keep, send = halves
     value = keep + swap(send, count, 1)
@@ -362,14 +394,18 @@
         value = value + swap(value, count, mask)
         mask *= 2
     got = swap(value, count, 2)
+    if beside is not None:
+        got, beside = lax.optimization_barrier((got, beside))
     value = jnp.concatenate([jnp.where(odd, got, value), jnp.where(odd, value, got)], axis=0)
-    return value, swap(value, count, 1)
+    return (value, swap(value, count, 1)), beside
 
 
 def on_device(count, ensemble, mean_state, observed, error_var, owner, obs_rows):
-    gram = total(gram_halves(ensemble), count)
-    obs = total(gather(ensemble, mean_state, observed, error_var, owner, obs_rows), count)
-    return update(gram, obs, ensemble, mean_state)
+    gram = gram_halves(ensemble)
+    first, second = gather(ensemble, mean_state, observed, error_var, owner, obs_rows, gram)
+    batch = first_batch(total(first, count)[0])
+    second, batch = total(second, count, batch)
+    return update(second, batch, ensemble, mean_state)
 
 
 def solution(mesh):

time: 57.1 us -> 57.6 us (level)
  starting transfers between devices: 13.6 us -> 16.6 us
  waiting for transfers between devices: 15.2 us -> 13.2 us
    pallas_call x1, Pallas kernels: 19.5 us -> 14.9 us  [update(): pl.pallas_call(functools.partial(update_kernel, chunks), out_shape=(jax.S...]
    pallas_call x1 -> x2, Pallas kernels: 4.12 us -> 8.27 us  [the longest x1 4.18 us: gather(): pl.pallas_call(functools.partial(gather_kernel, chunks), out_shape=(first...]
    ppermute x12, starting transfers between devices: 13.6 us -> 16.6 us  [swap(): return lax.ppermute(value, AXIS, [(i, i ^ mask) for i in range(count)])]
    ppermute x12, waiting for transfers between devices: 15.2 us -> 13.2 us  [swap(): return lax.ppermute(value, AXIS, [(i, i ^ mask) for i in range(count)])]
where the time goes in v3:
time: 57.6 us; the launch traced here: 57.5 us
  Pallas kernels  26.6 us (46%)
  starting transfers between devices  16.6 us (29%)
  waiting for transfers between devices  13.2 us (23%)
  between operations  0.97 us (2%)
    ppermute x12, starting transfers between devices, swap(): return lax.ppermute(value, AXIS, [(i, i ^ mask) for i in range(count)])  16.6 us
    pallas_call x1, Pallas kernels, update(): pl.pallas_call(functools.partial(update_kernel, chunks), out_shape=(jax.S...  14.9 us
    ppermute x12, waiting for transfers between devices, swap(): return lax.ppermute(value, AXIS, [(i, i ^ mask) for i in range(count)])  13.2 us
    pallas_call x1, Pallas kernels, gather(): pl.pallas_call(functools.partial(gather_kernel, chunks), out_shape=(first...  4.18 us
    pallas_call x1, Pallas kernels, first_batch(): pl.pallas_call(first_kernel, out_shape=(jax.ShapeDtypeStruct((OBS, member...  4.09 us
    pallas_call x1, Pallas kernels, gram_halves(): pl.pallas_call(functools.partial(gram_kernel, chunks), out_shape=(half, h...  3.42 us
  transfers between devices with their start and end apart: 12, of which 8 were waited for; matrix products, arithmetic and copies ran while one was open for 0% of the time, Pallas kernels for 7%

profile of v3, /device:TPU:0, one launch (start us, length us, event | category | flops | bytes accessed | tf_op | source)
XLA Modules:
  0.0 57.5 jit_solution(1717132394824921644)
XLA Ops:
  0.6 0.0 copy-start
  0.6 0.0 copy-start.1
  0.7 0.0 copy-start.4
  0.7 0.0 copy-start.3
  0.7 0.0 copy-start.2
  0.7 3.4 %shard_map.77 = (f32[96,256]{1,0:T(8,128)S(1)}, f32[96,256]{1,0:T(8,128)S(1)}) custom-call(f32[4096,256]{1,0:T(8,128)} %x_hbm.5), custom_call_target="tpu_custom_call" | custom-call | flops 1073741824 | bytes 4194304 | tf_op jit(solution)/shard_map/pallas_call | solution.py:307
  4.1 0.0 copy-done
  4.1 0.0 copy-done.1
  4.1 0.0 copy-done.4
  4.1 0.0 copy-done.3
  4.2 0.0 copy-done.2
  4.2 4.2 %shard_map.78 = (f32[80,256]{1,0:T(8,128)S(1)}, f32[80,256]{1,0:T(8,128)S(1)}, f32[160,256]{1,0:T(8,128)S(1)}, f32[160,256]{1,0:T(8,128)S(1)}) custom-call(s32[2]{0:T(128)S(1)} %copy-done.4, s32[2,128]{1,0:T(2,128)S(1)} %copy-done.1, s32[2,128]{1,0:T(2,128)S(1)} %copy-done.1, f32[2,128]{1,0:T(2,128)S(1)} %copy-done.2, f32[2,128]{1,0:T(2,128)S(1)} %copy-done.3, ...), custom_call_target="tpu_custom_call" | custom-call | flops 536870912 | bytes 4194304 | tf_op jit(solution)/shard_map/pallas_call | solution.py:327
  8.3 0.5 collective-permute-start.5
  8.9 0.9 %collective-permute-done.5 = f32[80,256]{1,0:T(8,128)S(1)} collective-permute-done((f32[80,256]{1,0:T(8,128)S(1)}, f32[80,256]{1,0:T(8,128)S(1)}, u32[]{:S(2)}, u32[]{:S(2)}) %collective-permute-start.5) | collective-permute-done | bytes 81952 | tf_op jit(solution)/shard_map/ppermute | solution.py:382
  9.8 2.9 %collective-permute-start.6 = (f32[40,256]{1,0:T(8,128)S(1)}, f32[40,256]{1,0:T(8,128)S(1)}, u32[]{:S(2)}, u32[]{:S(2)}) collective-permute-start(f32[40,256]{1,0:T(8,128)S(1)} %slice_select_fusion.1), channel_id=1, source_target_pairs={{0,2},{1,3},{2,0},{3,1},{4,6},{5,7},{6,4},{7,5},{8,10},{9,11},{10,... | collective-permute-start | bytes 122888 | tf_op jit(solution)/shard_map/ppermute | solution.py:382
  12.8 0.0 collective-permute-start
  12.8 2.0 %collective-permute-done.6 = f32[40,256]{1,0:T(8,128)S(1)} collective-permute-done((f32[40,256]{1,0:T(8,128)S(1)}, f32[40,256]{1,0:T(8,128)S(1)}, u32[]{:S(2)}, u32[]{:S(2)}) %collective-permute-start.6) | collective-permute-done | bytes 40992 | tf_op jit(solution)/shard_map/ppermute | solution.py:382
  14.7 2.1 %collective-permute-start.7 = (f32[40,256]{1,0:T(8,128)S(1)}, f32[40,256]{1,0:T(8,128)S(1)}, u32[]{:S(2)}, u32[]{:S(2)}) collective-permute-start(f32[40,256]{1,0:T(8,128)S(1)} %select_add_fusion.1), channel_id=1, source_target_pairs={{0,4},{1,5},{2,6},{3,7},{4,0},{5,1},{6,2},{7,3},{8,12},{9,13},{10,... | collective-permute-start | bytes 122888 | tf_op jit(solution)/shard_map/ppermute | solution.py:382
  16.9 0.0 collective-permute-done
  16.9 1.6 %collective-permute-start.1 = (f32[80,256]{1,0:T(8,128)S(1)}, f32[80,256]{1,0:T(8,128)S(1)}, u32[]{:S(2)}, u32[]{:S(2)}) collective-permute-start(f32[80,256]{1,0:T(8,128)S(1)} %slice_select_fusion), channel_id=1, source_target_pairs={{0,2},{1,3},{2,0},{3,1},{4,6},{5,7},{6,4},{7,5},{8,10},{9,11},{10,... | collective-permute-start | bytes 245768 | tf_op jit(solution)/shard_map/ppermute | solution.py:382
  18.5 0.3 collective-permute-done.7
  18.9 3.0 %collective-permute-start.8 = (f32[40,256]{1,0:T(8,128)S(1)}, f32[40,256]{1,0:T(8,128)S(1)}, u32[]{:S(2)}, u32[]{:S(2)}) collective-permute-start(f32[40,256]{1,0:T(8,128)S(1)} %add.30), channel_id=1, source_target_pairs={{0,8},{1,9},{2,10},{3,11},{4,12},{5,13},{6,14},{7,15},{8,0},{9,1},... | collective-permute-start | bytes 122888 | tf_op jit(solution)/shard_map/ppermute | solution.py:382
  21.9 2.0 %collective-permute-done.8 = f32[40,256]{1,0:T(8,128)S(1)} collective-permute-done((f32[40,256]{1,0:T(8,128)S(1)}, f32[40,256]{1,0:T(8,128)S(1)}, u32[]{:S(2)}, u32[]{:S(2)}) %collective-permute-start.8) | collective-permute-done | bytes 40992 | tf_op jit(solution)/shard_map/ppermute | solution.py:382
  23.9 1.9 %collective-permute-start.9 = (f32[40,256]{1,0:T(8,128)S(1)}, f32[40,256]{1,0:T(8,128)S(1)}, u32[]{:S(2)}, u32[]{:S(2)}) collective-permute-start(f32[40,256]{1,0:T(8,128)S(1)} %add.31), channel_id=1, source_target_pairs={{0,2},{1,3},{2,0},{3,1},{4,6},{5,7},{6,4},{7,5},{8,10},{9,11},{10,... | collective-permute-start | bytes 122888 | tf_op jit(solution)/shard_map/ppermute | solution.py:382
  25.8 0.0 collective-permute-done.1
  25.8 1.6 %collective-permute-start.2 = (f32[80,256]{1,0:T(8,128)S(1)}, f32[80,256]{1,0:T(8,128)S(1)}, u32[]{:S(2)}, u32[]{:S(2)}) collective-permute-start(f32[80,256]{1,0:T(8,128)S(1)} %select_add_fusion), channel_id=1, source_target_pairs={{0,4},{1,5},{2,6},{3,7},{4,0},{5,1},{6,2},{7,3},{8,12},{9,13},{10,... | collective-permute-start | bytes 245768 | tf_op jit(solution)/shard_map/ppermute | solution.py:382
  27.4 0.5 collective-permute-done.9
  27.9 3.1 %collective-permute-done.2 = f32[80,256]{1,0:T(8,128)S(1)} collective-permute-done((f32[80,256]{1,0:T(8,128)S(1)}, f32[80,256]{1,0:T(8,128)S(1)}, u32[]{:S(2)}, u32[]{:S(2)}) %collective-permute-start.2) | collective-permute-done | bytes 81952 | tf_op jit(solution)/shard_map/ppermute | solution.py:382
  31.0 2.4 %collective-permute-start.3 = (f32[80,256]{1,0:T(8,128)S(1)}, f32[80,256]{1,0:T(8,128)S(1)}, u32[]{:S(2)}, u32[]{:S(2)}) collective-permute-start(f32[80,256]{1,0:T(8,128)S(1)} %add.26), channel_id=1, source_target_pairs={{0,8},{1,9},{2,10},{3,11},{4,12},{5,13},{6,14},{7,15},{8,0},{9,1},... | collective-permute-start | bytes 245768 | tf_op jit(solution)/shard_map/ppermute | solution.py:382
  33.4 0.0 collective-permute-start.10
  33.4 3.0 %collective-permute-done.3 = f32[80,256]{1,0:T(8,128)S(1)} collective-permute-done((f32[80,256]{1,0:T(8,128)S(1)}, f32[80,256]{1,0:T(8,128)S(1)}, u32[]{:S(2)}, u32[]{:S(2)}) %collective-permute-start.3) | collective-permute-done | bytes 81952 | tf_op jit(solution)/shard_map/ppermute | solution.py:382
  36.4 0.4 collective-permute-start.4
  36.8 0.0 collective-permute-done.10.other
  36.8 4.1 %shard_map.79 = (f32[128,256]{1,0:T(8,128)S(1)}, f32[256,256]{1,0:T(8,128)S(1)}, f32[8,256]{1,0:T(8,128)S(1)}) custom-call(f32[80,256]{1,0:T(8,128)S(1)} %pad_maximum_fusion.1.mine, f32[80,256]{1,0:T(8,128)S(1)} %collective-permute-done.10.other), custom_call_target="tpu_custom_call" | custom-call | flops 5000000000 | bytes 262144 | tf_op jit(solution)/shard_map/pallas_call | solution.py:345
  40.9 0.0 collective-permute-done.4
  41.0 0.1 collective-permute-start.11
  41.1 1.4 %collective-permute-done.11.other = f32[160,256]{1,0:T(8,128)S(1)} collective-permute-done((f32[160,256]{1,0:T(8,128)S(1)}, f32[160,256]{1,0:T(8,128)S(1)}, u32[]{:S(2)}, u32[]{:S(2)}) %collective-permute-start.11) | collective-permute-done | bytes 163872 | tf_op jit(solution)/shard_map/ppermute | solution.py:382
  42.4 14.9 %shard_map.80 = (f32[4096,256]{1,0:T(8,128)}, f32[1,4096]{1,0:T(1,128)}) custom-call(f32[160,256]{1,0:T(8,128)S(1)} %pad_maximum_fusion.mine, f32[160,256]{1,0:T(8,128)S(1)} %collective-permute-done.11.other, f32[128,256]{1,0:T(8,128)S(1)} %get-tuple-element.27.v_in, f32[256,256]{1,0:T(8,128)S(1)} %get-tuple-element.28.system, ...), custom_call_target="tpu_custom_call" | custom-call | tf_op jit(solution)/shard_map/pallas_call | solution.py:363
  (14 shorter events, 0.2 us)
Async XLA Ops:
  0.6 3.5 %copy-start = (f32[4096]{0:T(1024)S(1)}, f32[4096]{0:T(1024)}, u32[]{:S(2)}) copy-start(f32[4096]{0:T(1024)} %param.7) | copy-start | bytes 49156
  0.6 3.5 %copy-start.1 = (s32[2,128]{1,0:T(2,128)S(1)}, s32[2,128]{1,0:T(2,128)}, u32[]{:S(2)}) copy-start(s32[2,128]{1,0:T(2,128)} %rows_v.1) | copy-start | bytes 3076
  0.7 3.5 %copy-start.4 = (s32[2]{0:T(128)S(1)}, s32[2]{0:T(128)}, u32[]{:S(2)}) copy-start(s32[2]{0:T(128)} %owner_s.1) | copy-start | bytes 28
  0.7 3.5 %copy-start.3 = (f32[2,128]{1,0:T(2,128)S(1)}, f32[2,128]{1,0:T(2,128)}, u32[]{:S(2)}) copy-start(f32[2,128]{1,0:T(2,128)} %error_var.1) | copy-start | bytes 3076
  0.7 3.5 %copy-start.2 = (f32[2,128]{1,0:T(2,128)S(1)}, f32[2,128]{1,0:T(2,128)}, u32[]{:S(2)}) copy-start(f32[2,128]{1,0:T(2,128)} %observed.1) | copy-start | bytes 3076
  8.3 1.4 %collective-permute-start.5 = (f32[80,256]{1,0:T(8,128)S(1)}, f32[80,256]{1,0:T(8,128)S(1)}, u32[]{:S(2)}, u32[]{:S(2)}) collective-permute-start(f32[80,256]{1,0:T(8,128)S(1)} %get-tuple-element.22), channel_id=1, source_target_pairs={{0,1},{1,0},{2,3},{3,2},{4,5},{5,4},{6,7},{7,6},{8,9},{9,8},{10,11... | collective-permute-start | bytes 245768 | tf_op jit(solution)/shard_map/ppermute | solution.py:382
  9.8 4.9 %collective-permute-start.6 = (f32[40,256]{1,0:T(8,128)S(1)}, f32[40,256]{1,0:T(8,128)S(1)}, u32[]{:S(2)}, u32[]{:S(2)}) collective-permute-start(f32[40,256]{1,0:T(8,128)S(1)} %slice_select_fusion.1), channel_id=1, source_target_pairs={{0,2},{1,3},{2,0},{3,1},{4,6},{5,7},{6,4},{7,5},{8,10},{9,11},{10,... | collective-permute-start | bytes 122888 | tf_op jit(solution)/shard_map/ppermute | solution.py:382
  12.8 4.1 %collective-permute-start = (f32[160,256]{1,0:T(8,128)S(1)}, f32[160,256]{1,0:T(8,128)S(1)}, u32[]{:S(2)}, u32[]{:S(2)}) collective-permute-start(f32[160,256]{1,0:T(8,128)S(1)} %get-tuple-element.20), channel_id=1, source_target_pairs={{0,1},{1,0},{2,3},{3,2},{4,5},{5,4},{6,7},{7,6},{8,9},{9,8},{10,11... | collective-permute-start | bytes 491528 | tf_op jit(solution)/shard_map/ppermute | solution.py:382
  14.7 4.1 %collective-permute-start.7 = (f32[40,256]{1,0:T(8,128)S(1)}, f32[40,256]{1,0:T(8,128)S(1)}, u32[]{:S(2)}, u32[]{:S(2)}) collective-permute-start(f32[40,256]{1,0:T(8,128)S(1)} %select_add_fusion.1), channel_id=1, source_target_pairs={{0,4},{1,5},{2,6},{3,7},{4,0},{5,1},{6,2},{7,3},{8,12},{9,13},{10,... | collective-permute-start | bytes 122888 | tf_op jit(solution)/shard_map/ppermute | solution.py:382
  16.9 8.9 %collective-permute-start.1 = (f32[80,256]{1,0:T(8,128)S(1)}, f32[80,256]{1,0:T(8,128)S(1)}, u32[]{:S(2)}, u32[]{:S(2)}) collective-permute-start(f32[80,256]{1,0:T(8,128)S(1)} %slice_select_fusion), channel_id=1, source_target_pairs={{0,2},{1,3},{2,0},{3,1},{4,6},{5,7},{6,4},{7,5},{8,10},{9,11},{10,... | collective-permute-start | bytes 245768 | tf_op jit(solution)/shard_map/ppermute | solution.py:382
  18.9 5.0 %collective-permute-start.8 = (f32[40,256]{1,0:T(8,128)S(1)}, f32[40,256]{1,0:T(8,128)S(1)}, u32[]{:S(2)}, u32[]{:S(2)}) collective-permute-start(f32[40,256]{1,0:T(8,128)S(1)} %add.30), channel_id=1, source_target_pairs={{0,8},{1,9},{2,10},{3,11},{4,12},{5,13},{6,14},{7,15},{8,0},{9,1},... | collective-permute-start | bytes 122888 | tf_op jit(solution)/shard_map/ppermute | solution.py:382
  23.9 4.0 %collective-permute-start.9 = (f32[40,256]{1,0:T(8,128)S(1)}, f32[40,256]{1,0:T(8,128)S(1)}, u32[]{:S(2)}, u32[]{:S(2)}) collective-permute-start(f32[40,256]{1,0:T(8,128)S(1)} %add.31), channel_id=1, source_target_pairs={{0,2},{1,3},{2,0},{3,1},{4,6},{5,7},{6,4},{7,5},{8,10},{9,11},{10,... | collective-permute-start | bytes 122888 | tf_op jit(solution)/shard_map/ppermute | solution.py:382
  25.8 5.2 %collective-permute-start.2 = (f32[80,256]{1,0:T(8,128)S(1)}, f32[80,256]{1,0:T(8,128)S(1)}, u32[]{:S(2)}, u32[]{:S(2)}) collective-permute-start(f32[80,256]{1,0:T(8,128)S(1)} %select_add_fusion), channel_id=1, source_target_pairs={{0,4},{1,5},{2,6},{3,7},{4,0},{5,1},{6,2},{7,3},{8,12},{9,13},{10,... | collective-permute-start | bytes 245768 | tf_op jit(solution)/shard_map/ppermute | solution.py:382
  31.0 5.4 %collective-permute-start.3 = (f32[80,256]{1,0:T(8,128)S(1)}, f32[80,256]{1,0:T(8,128)S(1)}, u32[]{:S(2)}, u32[]{:S(2)}) collective-permute-start(f32[80,256]{1,0:T(8,128)S(1)} %add.26), channel_id=1, source_target_pairs={{0,8},{1,9},{2,10},{3,11},{4,12},{5,13},{6,14},{7,15},{8,0},{9,1},... | collective-permute-start | bytes 245768 | tf_op jit(solution)/shard_map/ppermute | solution.py:382
  33.4 3.4 %collective-permute-start.10 = (f32[80,256]{1,0:T(8,128)S(1)}, f32[80,256]{1,0:T(8,128)S(1)}, u32[]{:S(2)}, u32[]{:S(2)}) collective-permute-start(f32[80,256]{1,0:T(8,128)S(1)} %pad_maximum_fusion.1.mine), channel_id=1, source_target_pairs={{0,1},{1,0},{2,3},{3,2},{4,5},{5,4},{6,7},{7,6},{8,9},{9,8},{10,11... | collective-permute-start | bytes 245768 | tf_op jit(solution)/shard_map/ppermute | solution.py:382
  36.4 4.5 %collective-permute-start.4 = (f32[80,256]{1,0:T(8,128)S(1)}, f32[80,256]{1,0:T(8,128)S(1)}, u32[]{:S(2)}, u32[]{:S(2)}) collective-permute-start(f32[80,256]{1,0:T(8,128)S(1)} %add.27), channel_id=1, source_target_pairs={{0,2},{1,3},{2,0},{3,1},{4,6},{5,7},{6,4},{7,5},{8,10},{9,11},{10,... | collective-permute-start | bytes 245768 | tf_op jit(solution)/shard_map/ppermute | solution.py:382
  41.0 1.5 %collective-permute-start.11 = (f32[160,256]{1,0:T(8,128)S(1)}, f32[160,256]{1,0:T(8,128)S(1)}, u32[]{:S(2)}, u32[]{:S(2)}) collective-permute-start(f32[160,256]{1,0:T(8,128)S(1)} %pad_maximum_fusion.mine), channel_id=1, source_target_pairs={{0,1},{1,0},{2,3},{3,2},{4,5},{5,4},{6,7},{7,6},{8,9},{9,8},{10,11... | collective-permute-start | bytes 491528 | tf_op jit(solution)/shard_map/ppermute | solution.py:382

commit v4 on v2

v4 whole, which is shorter than its diff:
```python
import functools

import jax
import jax.numpy as jnp
from jax import lax
from jax.experimental import pallas as pl
from jax.experimental.pallas import tpu as pltpu
from jax.sharding import PartitionSpec as P

RELAX = 0.6
HI = lax.Precision.HIGHEST
AXIS = "rows"
F32 = jnp.float32
BF16 = jnp.bfloat16
LANES = 128
SUB = 8
OBS = 128
VMEM_LIMIT = 51 * 1024 * 1024
STEP = 16

A0, A1, B0, B1, G00, G01, G11 = range(0, 7 * 128, 128)
PACKED = 7 * 128
INNOV = G00 + 64


def dot(a, b, dims=((1,), (0,)), precision=HI):
    return lax.dot_general(a, b, (dims, ((), ())), precision=precision, preferred_element_type=F32)


def column(row):
    return jnp.broadcast_to(row, (LANES, LANES)).T


def split(x):
    high = x.astype(BF16)
    return high, (x - high.astype(F32)).astype(BF16)


def chunk_copy(source, target, sem, chunks):
    size = source.shape[0] // chunks

    def copy(i):
        part = pl.ds(i * size, size)
        return pltpu.make_async_copy(source.at[part], target.at[part], sem.at[i])

    return copy


def gram_kernel(chunks, x_hbm, out, x_buf, sem):
    members = x_buf.shape[1]
    size = x_buf.shape[0] // chunks
    half = members // 2
    copy = chunk_copy(x_hbm, x_buf, sem, chunks)
    for i in range(chunks):
        copy(i).start()
    total = None
    for i in range(chunks):
        copy(i).wait()
        high, low = split(x_buf[i * size : (i + 1) * size, :])
        part = dot(high, jnp.concatenate([high, low], axis=1), ((0,), (0,)), None)
        total = part if total is None else total + part
    cross = total[:, members:]
    total = total[:, :members] + cross + cross.T
    out[:half, :] = total[:half, :half]
    out[half : 2 * half, :] = total[:half, half:]
    out[2 * half :, :] = total[half:, half:]


def gather_kernel(
    owner_s, rows_s, rows_v, observed, error_var, mean_v, gram, x_hbm, keep, send, full, picked, sem
):
    me = lax.axis_index(AXIS)
    members = picked.shape[2]
    half = members // 2

    for k in range(2):

        @pl.when(owner_s[k] == me)
        def _(k=k):
            def fetch(o, _):
                pltpu.make_async_copy(
                    x_hbm.at[pl.ds(rows_s[k, o], 1)], picked.at[k, pl.ds(o, 1)], sem.at[k]
                ).start()
                return 0

            lax.fori_loop(0, OBS, fetch, 0, unroll=8)

    innovations = []
    scales = []
    lane = lax.broadcasted_iota(jnp.int32, (OBS, LANES), 1)
    for k in range(2):
        index = column(rows_v[k : k + 1, :].astype(F32)).astype(jnp.int32)
        prior = jnp.zeros((OBS, LANES), F32)
        for r in range(mean_v.shape[0]):
            prior = prior + jnp.where(index == lane + r * LANES, mean_v[r : r + 1, :], 0.0)
        prior = jnp.sum(prior.T, axis=0, keepdims=True)
        scale = lax.rsqrt(error_var[k : k + 1, :] * (members - 1.0))
        scales.append(column(scale))
        innov = jnp.where(owner_s[k] == me, scale * (observed[k : k + 1, :] - prior), 0.0)
        innovations += [innov[:, : half // 2], innov[:, half // 2 :]]

    full[G00:, :] = gram[...]
    for i, innov in enumerate(innovations):
        full[INNOV + i : INNOV + i + 1, : half // 2] = innov
    full[:G00, :] = jnp.zeros((G00, LANES), F32)
    for k, left, right in ((0, A0, A1), (1, B0, B1)):

        @pl.when(owner_s[k] == me)
        def _(k=k, left=left, right=right):
            pltpu.make_async_copy(x_hbm.at[pl.ds(0, OBS)], picked.at[k], sem.at[k]).wait()
            full[left : left + OBS, :] = picked[k, :, :half] * scales[k]
            full[right : right + OBS, :] = picked[k, :, half:] * scales[k]

    mine = me & 1
    span = PACKED // 2
    keep[...] = full[pl.ds(pl.multiple_of(mine * span, SUB), span), :]
    send[...] = full[pl.ds(pl.multiple_of((1 - mine) * span, SUB), span), :]


def tree(terms):
    while len(terms) > 1:
        terms = [terms[i] + terms[i + 1] if i + 1 < len(terms) else terms[i] for i in range(0, len(terms), 2)]
    return terms[0]


def factor(a):
    count = LANES // SUB
    lane = lax.broadcasted_iota(jnp.int32, (SUB, LANES), 1)
    sub = lax.broadcasted_iota(jnp.int32, (SUB, LANES), 0)
    rows = [a[SUB * i : SUB * (i + 1), :] for i in range(count)]
    out = []

    def spread(x, c):
        return jnp.broadcast_to(x[:, c : c + 1], (SUB, LANES))

    def row(x, j):
        return jnp.broadcast_to(x[j : j + 1, :], (SUB, LANES))

    groups = STEP // SUB
    for s in range(0, count, groups):
        base = SUB * s
        here = (lane >= base) & (lane < base + STEP)
        cols = [[spread(rows[s + g], base + q) for g in range(groups)] for q in range(STEP)]
        work = [
            jnp.where(here, (lane - base == sub + SUB * g).astype(F32), rows[s + g]) for g in range(groups)
        ]
        done = [jnp.zeros((SUB, LANES), F32) for _ in range(groups)]
        for p in range(0, STEP, 2):
            at, j = divmod(p, SUB)
            first, second = sub == j, sub == j + 1
            pair = first | second
            pa, pb, pc = row(cols[p][at], j), row(cols[p][at], j + 1), row(cols[p + 1][at], j + 1)
            det = pa * pc - pb * pb
            inv = pl.reciprocal(det, approx=True)
            top, low = row(work[at], j), row(work[at], j + 1)
            done[at] = jnp.where(first, top * lax.rsqrt(pa), done[at])
            done[at] = jnp.where(second, (pa * low - pb * top) * lax.rsqrt(pa * det), done[at])
            raw, scaled = [], []
            for g in range(groups):
                m0, m1 = cols[p][g], cols[p + 1][g]
                if g == at:
                    m0 = jnp.where(first, -1.0, jnp.where(second, 0.0, m0))
                    m1 = jnp.where(second, -1.0, jnp.where(first, 0.0, m1))
                u0, u1 = m0 * pc - m1 * pb, m1 * pa - m0 * pb
                raw.append((u0, u1))
                scaled.append((u0 * inv, u1 * inv))
            for q in range(p + 2, STEP + 1):
                kept = cols[q] if q < STEP else work
                t, l = row(kept[at], j), row(kept[at], j + 1)
                moved = []
                for g in range(groups):
                    old = jnp.where(pair, 0.0, kept[g]) if g == at else kept[g]
                    if q < p + 4:
                        moved.append(old - (raw[g][0] * t + raw[g][1] * l) * inv)
                    else:
                        moved.append(old - (scaled[g][0] * t + scaled[g][1] * l))
                if q < STEP:
                    cols[q] = moved
                else:
                    work = moved
        for g in range(groups):
            out.append(jnp.where(lane <= base + SUB * g + sub, done[g], 0.0))
        lines = [row(work[p // SUB], p % SUB) for p in range(STEP)]
        for i in range(s + groups, count):
            change = tree([spread(rows[i], base + p) * lines[p] for p in range(STEP)])
            rows[i] = jnp.where(here, 0.0, rows[i]) - change
    return jnp.concatenate(out, axis=0)


def blend(before, after):
    return 1.0 + RELAX * (jnp.sqrt(before / after) - 1.0)


def add_up(x):
    return jnp.sum(jnp.sum(x, axis=0, keepdims=True), axis=1, keepdims=True)


def dot3(a, b):
    a_high, a_low = split(a)
    b_high, b_low = split(b)
    return dot(
        jnp.concatenate([a_high, a_low, a_high], axis=1), jnp.concatenate([b_high, b_high, b_low], axis=0), precision=None
    )


def identity(size):
    return (
        lax.broadcasted_iota(jnp.int32, (size, size), 0) == lax.broadcasted_iota(jnp.int32, (size, size), 1)
    ).astype(F32)


def update_kernel(
    chunks, mine_v, other_v, mean_v, x_hbm, out_hbm, mean_out, full, x_buf, o_buf, in_sem, out_sem
):
    members = x_buf.shape[1]
    size = x_buf.shape[0] // chunks
    load = chunk_copy(x_hbm, x_buf, in_sem, chunks)
    store = chunk_copy(o_buf, out_hbm, out_sem, chunks)
    for i in range(chunks):
        load(i).start()

    mine = lax.axis_index(AXIS) & 1
    span = PACKED // 2
    full[pl.ds(pl.multiple_of(mine * span, SUB), span), :] = mine_v[...]
    full[pl.ds(pl.multiple_of((1 - mine) * span, SUB), span), :] = other_v[...]

    half = members // 2
    quarter = half // 2

    def block(at):
        return full[at : at + half, :]

    def innovation(k):
        at = INNOV + 2 * k
        return column(jnp.concatenate([full[at : at + 1, :quarter], full[at + 1 : at + 2, :quarter]], axis=1))

    first = jnp.concatenate([block(A0), block(A1)], axis=1)
    second = jnp.concatenate([block(B0), block(B1)], axis=1)
    g00, g01, g11 = block(G00), block(G01), block(G11)
    line = lax.broadcasted_iota(jnp.int32, (half, half), 0)
    lane = lax.broadcasted_iota(jnp.int32, (half, half), 1)
    g00 = jnp.where((line >= quarter) & (lane < quarter), g00.T, g00)
    gram = jnp.concatenate(
        [jnp.concatenate([g00, g01], axis=1), jnp.concatenate([g01.T, g11], axis=1)], axis=0
    )
    eye = identity(half)

    inv_m = factor(eye + dot(first, first, ((1,), (1,))))
    v_and_f = dot(inv_m, jnp.concatenate([first, innovation(0)], axis=1))
    v, f = v_and_f[:, :members], v_and_f[:, members:]
    before = add_up(eye * (g00 + g11))
    after1 = before - add_up(dot3(v, gram) * v)
    factor1 = blend(before, after1)
    increment = jnp.sum(v * jnp.concatenate([f, f], axis=1), axis=0, keepdims=True)
    innov2 = innovation(1) - jnp.sum(second * increment, axis=1, keepdims=True)

    a1 = dot(first, first, ((0,), (0,)))
    a2 = dot(second, jnp.concatenate([second, innov2], axis=1), ((0,), (0,)))
    square = factor1 * factor1
    k00 = eye + a1[:half, :half] + a2[:half, :half] * square
    k01 = a1[:half, half:] + a2[:half, half:members] * square
    k11 = eye + a1[half:, half:] + a2[half:, half:members] * square
    inv00 = factor(k00)
    u = dot(inv00, k01)
    inv11 = factor(k11 - dot(u, u, ((0,), (0,))))
    inv10 = -dot(inv11, dot(u, inv00, ((0,), (0,))))
    y0 = dot(inv00, a2[:half, members:] * square)
    y1 = dot(inv11, a2[half:, members:] * square - dot(u, y0, ((0,), (0,))))
    bottom = jnp.concatenate([inv10, inv11], axis=1)
    top_trace = add_up(dot3(inv00, g00) * inv00)
    after2 = top_trace + add_up(dot3(bottom, gram) * bottom)
    factor2 = factor1 * blend(after1, after2)
    increment0 = jnp.sum(y0 * inv00 + y1 * inv10, axis=0, keepdims=True)
    increment1 = jnp.sum(y1 * inv11, axis=0, keepdims=True)
    increment = increment + jnp.concatenate([increment0, increment1], axis=1)

    inverse = jnp.concatenate([jnp.concatenate([inv00, jnp.zeros_like(inv00)], axis=1), bottom], axis=0)
    high, low = split(inverse)
    transform = jnp.concatenate([high, high, low], axis=1)
    step_line = lax.broadcasted_iota(jnp.int32, (LANES, LANES), 0)
    diagonal = step_line == lax.broadcasted_iota(jnp.int32, (LANES, LANES), 1)

    def apply(i, at):
        load(i).wait()
        x = x_buf[pl.ds(at, size), :]
        high, low = split(x)
        moved = dot(jnp.concatenate([high, low, high], axis=1), transform, ((1,), (1,)), None)
        o_buf[pl.ds(at, size), :] = moved * factor2
        store(i).start()
        steps = jnp.sum(x * increment, axis=1, keepdims=True)
        for j in range(0, size, LANES):
            step = jnp.sum(jnp.where(diagonal, steps[j : j + LANES, :], 0.0), axis=0, keepdims=True)
            part = pl.ds(at + j, LANES)
            mean_out[:, part] = mean_v[:, part] + step

    apply(0, 0)

    def body(i, _):
        apply(i, pl.multiple_of(i * size, size))
        return 0

    lax.fori_loop(1, chunks, body, 0)
    for i in range(chunks):
        store(i).wait()


def spec(space):
    return pl.BlockSpec(memory_space=space)


def params():
    return pltpu.CompilerParams(vmem_limit_bytes=VMEM_LIMIT)


def cost(flops, bytes_accessed):
    return pl.CostEstimate(flops=flops, bytes_accessed=bytes_accessed, transcendentals=0)


def cost(flops, bytes_accessed):
    return pl.CostEstimate(flops=flops, bytes_accessed=bytes_accessed, transcendentals=0)


def gram_of(ensemble):
    rows, members = ensemble.shape
    chunks = 4
    return pl.pallas_call(
        functools.partial(gram_kernel, chunks),
        out_shape=jax.ShapeDtypeStruct((PACKED - G00, LANES), F32),
        in_specs=[spec(pltpu.HBM)],
        out_specs=spec(pltpu.VMEM),
        scratch_shapes=[pltpu.VMEM((rows, members), F32), pltpu.SemaphoreType.DMA((chunks,))],
        cost_estimate=cost(4 * rows * members * members, 4 * rows * members),
        compiler_params=params(),
    )(ensemble)


def gather(ensemble, mean_state, observed, error_var, owner, obs_rows, gram):
    members = ensemble.shape[1]
    half = jax.ShapeDtypeStruct((PACKED // 2, LANES), F32)
    return pl.pallas_call(
        gather_kernel,
        out_shape=(half, half),
        in_specs=[spec(pltpu.SMEM), spec(pltpu.SMEM)] + [spec(pltpu.VMEM)] * 5 + [spec(pltpu.HBM)],
        out_specs=[spec(pltpu.VMEM)] * 2,
        scratch_shapes=[
            pltpu.VMEM((PACKED, LANES), F32),
            pltpu.VMEM((2, OBS, members), F32),
            pltpu.SemaphoreType.DMA((2,)),
        ],
        compiler_params=params(),
    )(owner, obs_rows, obs_rows, observed, error_var, mean_state.reshape(-1, LANES), gram, ensemble)


def update(packed, ensemble, mean_state):
    rows, members = ensemble.shape
    chunks = 8
    out, mean = pl.pallas_call(
        functools.partial(update_kernel, chunks),
        out_shape=(jax.ShapeDtypeStruct((rows, members), F32), jax.ShapeDtypeStruct((1, rows), F32)),
        in_specs=[spec(pltpu.VMEM)] * 3 + [spec(pltpu.HBM)],
        out_specs=(spec(pltpu.HBM), spec(pltpu.VMEM)),
        scratch_shapes=[
            pltpu.VMEM((PACKED, LANES), F32),
            pltpu.VMEM((rows, members), F32),
            pltpu.VMEM((rows, members), F32),
            pltpu.SemaphoreType.DMA((chunks,)),
            pltpu.SemaphoreType.DMA((chunks,)),
        ],
        compiler_params=params(),
    )(*packed, mean_state.reshape(1, rows), ensemble)
    return out, mean.reshape(rows)


def swap(value, count, mask):
    return lax.ppermute(value, AXIS, [(i, i ^ mask) for i in range(count)])


def total(keep, send, count):
    odd = ((lax.axis_index(AXIS) >> 1) & 1) == 1
    value = keep + swap(send, count, 1)
    low, high = jnp.split(value, 2, axis=0)
    value = jnp.where(odd, high, low) + swap(jnp.where(odd, low, high), count, 2)
    mask = 4
    while mask < count:
        value = value + swap(value, count, mask)
        mask *= 2
    got = swap(value, count, 2)
    value = jnp.concatenate([jnp.where(odd, got, value), jnp.where(odd, value, got)], axis=0)
    return value, swap(value, count, 1)


def on_device(count, ensemble, mean_state, observed, error_var, owner, obs_rows):
    gram = gram_of(ensemble)
    keep, send = gather(ensemble, mean_state, observed, error_var, owner, obs_rows, gram)
    return update(total(keep, send, count), ensemble, mean_state)


def solution(mesh):
    count = mesh.shape[AXIS]
    in_specs = (
        P(("groups", "rows"), None),
        P(("groups", "rows")),
        P("groups", None),
        P("groups", None),
        P("groups"),
        P("groups", None),
    )
    out_specs = (P(("groups", "rows"), None), P(("groups", "rows")))

    def body(*args):
        return on_device(count, *args)

    return jax.shard_map(body, mesh=mesh, in_specs=in_specs, out_specs=out_specs, check_vma=False)
```

time: 57.1 us -> 50.6 us (0.89)
  Pallas kernels: 27.1 us -> 22.1 us
  starting transfers between devices: 13.6 us -> 8.92 us
  waiting for transfers between devices: 15.2 us -> 18.2 us
    ppermute x12 -> x6, starting transfers between devices: 13.6 us -> 8.92 us  [swap(): return lax.ppermute(value, AXIS, [(i, i ^ mask) for i in range(count)])]
    ppermute x12 -> x6, waiting for transfers between devices: 15.2 us -> 18.2 us  [swap(): return lax.ppermute(value, AXIS, [(i, i ^ mask) for i in range(count)])]
    pallas_call x2, Pallas kernels: 7.54 us -> 4.97 us  [the longest x1 3.38 us: gram_of(): pl.pallas_call(functools.partial(gram_kernel, chunks), out_shape=jax.Shap...]
    pallas_call x1, Pallas kernels: 19.5 us -> 17.2 us  [update(): pl.pallas_call(functools.partial(update_kernel, chunks), out_shape=(jax.S...]
  transfers between devices with their start and end apart: 12 -> 6, of which waited for: 8 -> 6; matrix products, arithmetic and copies ran while one was open for 0% -> 0% of each run, Pallas kernels for 7% -> 0%
where the time goes in v4:
time: 50.6 us; the launch traced here: 50.4 us
  Pallas kernels  22.1 us (44%)
  waiting for transfers between devices  18.2 us (36%)
  starting transfers between devices  8.92 us (18%)
  between operations  0.93 us (2%)
    ppermute x6, waiting for transfers between devices, swap(): return lax.ppermute(value, AXIS, [(i, i ^ mask) for i in range(count)])  18.2 us
    pallas_call x1, Pallas kernels, update(): pl.pallas_call(functools.partial(update_kernel, chunks), out_shape=(jax.S...  17.2 us
    ppermute x6, starting transfers between devices, swap(): return lax.ppermute(value, AXIS, [(i, i ^ mask) for i in range(count)])  8.92 us
    pallas_call x1, Pallas kernels, gram_of(): pl.pallas_call(functools.partial(gram_kernel, chunks), out_shape=jax.Shap...  3.38 us
    pallas_call x1, Pallas kernels, gather(): pl.pallas_call(gather_kernel, out_shape=(half, half), in_specs=[spec(pltp...  1.59 us
  transfers between devices with their start and end apart: 6, of which 6 were waited for; matrix products, arithmetic and copies ran while one was open for 0% of the time, Pallas kernels for 0%

profile of v4, /device:TPU:0, one launch (start us, length us, event | category | flops | bytes accessed | tf_op | source)
XLA Modules:
  0.0 50.4 jit_solution(5537727406447845797)
XLA Ops:
  0.6 0.0 copy-start
  0.6 0.0 copy-start.1
  0.7 0.0 copy-start.4
  0.7 0.0 copy-start.3
  0.7 0.0 copy-start.2
  0.7 3.4 %shard_map.77.gram = f32[384,128]{1,0:T(8,128)S(1)} custom-call(f32[4096,256]{1,0:T(8,128)} %x_hbm.5), custom_call_target="tpu_custom_call" | custom-call | flops 1073741824 | bytes 4194304 | tf_op jit(solution)/shard_map/pallas_call | solution.py:326
  4.1 0.0 copy-done
  4.1 0.0 copy-done.1
  4.1 0.0 copy-done.4
  4.1 0.0 copy-done.3
  4.1 0.0 copy-done.2
  4.1 1.6 %shard_map.78 = (f32[448,128]{1,0:T(8,128)S(1)}, f32[448,128]{1,0:T(8,128)S(1)}) custom-call(s32[2]{0:T(128)S(1)} %copy-done.4, s32[2,128]{1,0:T(2,128)S(1)} %copy-done.1, s32[2,128]{1,0:T(2,128)S(1)} %copy-done.1, f32[2,128]{1,0:T(2,128)S(1)} %copy-done.2, f32[2,128]{1,0:T(2,128)S(1)} %copy-done.3, f32[32,128]{1,0:T(8,128)S(1)} %bitcast.3, ...), custom_call_target="tpu_custom_call" | custom-call | tf_op jit(solution)/shard_map/pallas_call | solution.py:340
  5.7 1.5 %collective-permute-start = (f32[448,128]{1,0:T(8,128)S(1)}, f32[448,128]{1,0:T(8,128)S(1)}, u32[]{:S(2)}, u32[]{:S(2)}) collective-permute-start(f32[448,128]{1,0:T(8,128)S(1)} %get-tuple-element.7), channel_id=1, source_target_pairs={{0,1},{1,0},{2,3},{3,2},{4,5},{5,4},{6,7},{7,6},{8,9},{9,8},{10,11... | collective-permute-start | bytes 688136 | tf_op jit(solution)/shard_map/ppermute | solution.py:375
  7.2 1.1 %collective-permute-done = f32[448,128]{1,0:T(8,128)S(1)} collective-permute-done((f32[448,128]{1,0:T(8,128)S(1)}, f32[448,128]{1,0:T(8,128)S(1)}, u32[]{:S(2)}, u32[]{:S(2)}) %collective-permute-start) | collective-permute-done | bytes 229408 | tf_op jit(solution)/shard_map/ppermute | solution.py:375
  8.3 2.3 %collective-permute-start.1 = (f32[224,128]{1,0:T(8,128)S(1)}, f32[224,128]{1,0:T(8,128)S(1)}, u32[]{:S(2)}, u32[]{:S(2)}) collective-permute-start(f32[224,128]{1,0:T(8,128)S(1)} %slice_select_fusion), channel_id=1, source_target_pairs={{0,2},{1,3},{2,0},{3,1},{4,6},{5,7},{6,4},{7,5},{8,10},{9,11},{10,... | collective-permute-start | bytes 344072 | tf_op jit(solution)/shard_map/ppermute | solution.py:375
  10.6 3.7 %collective-permute-done.1 = f32[224,128]{1,0:T(8,128)S(1)} collective-permute-done((f32[224,128]{1,0:T(8,128)S(1)}, f32[224,128]{1,0:T(8,128)S(1)}, u32[]{:S(2)}, u32[]{:S(2)}) %collective-permute-start.1) | collective-permute-done | bytes 114720 | tf_op jit(solution)/shard_map/ppermute | solution.py:375
  14.3 1.4 %collective-permute-start.2 = (f32[224,128]{1,0:T(8,128)S(1)}, f32[224,128]{1,0:T(8,128)S(1)}, u32[]{:S(2)}, u32[]{:S(2)}) collective-permute-start(f32[224,128]{1,0:T(8,128)S(1)} %select_add_fusion), channel_id=1, source_target_pairs={{0,4},{1,5},{2,6},{3,7},{4,0},{5,1},{6,2},{7,3},{8,12},{9,13},{10,... | collective-permute-start | bytes 344072 | tf_op jit(solution)/shard_map/ppermute | solution.py:375
  15.7 3.5 %collective-permute-done.2 = f32[224,128]{1,0:T(8,128)S(1)} collective-permute-done((f32[224,128]{1,0:T(8,128)S(1)}, f32[224,128]{1,0:T(8,128)S(1)}, u32[]{:S(2)}, u32[]{:S(2)}) %collective-permute-start.2) | collective-permute-done | bytes 114720 | tf_op jit(solution)/shard_map/ppermute | solution.py:375
  19.2 2.4 %collective-permute-start.3 = (f32[224,128]{1,0:T(8,128)S(1)}, f32[224,128]{1,0:T(8,128)S(1)}, u32[]{:S(2)}, u32[]{:S(2)}) collective-permute-start(f32[224,128]{1,0:T(8,128)S(1)} %add.14), channel_id=1, source_target_pairs={{0,8},{1,9},{2,10},{3,11},{4,12},{5,13},{6,14},{7,15},{8,0},{9,1},... | collective-permute-start | bytes 344072 | tf_op jit(solution)/shard_map/ppermute | solution.py:375
  21.6 5.0 %collective-permute-done.3 = f32[224,128]{1,0:T(8,128)S(1)} collective-permute-done((f32[224,128]{1,0:T(8,128)S(1)}, f32[224,128]{1,0:T(8,128)S(1)}, u32[]{:S(2)}, u32[]{:S(2)}) %collective-permute-start.3) | collective-permute-done | bytes 114720 | tf_op jit(solution)/shard_map/ppermute | solution.py:375
  26.6 1.4 %collective-permute-start.4 = (f32[224,128]{1,0:T(8,128)S(1)}, f32[224,128]{1,0:T(8,128)S(1)}, u32[]{:S(2)}, u32[]{:S(2)}) collective-permute-start(f32[224,128]{1,0:T(8,128)S(1)} %add.15), channel_id=1, source_target_pairs={{0,2},{1,3},{2,0},{3,1},{4,6},{5,7},{6,4},{7,5},{8,10},{9,11},{10,... | collective-permute-start | bytes 344072 | tf_op jit(solution)/shard_map/ppermute | solution.py:375
  28.0 3.5 %collective-permute-done.4 = f32[224,128]{1,0:T(8,128)S(1)} collective-permute-done((f32[224,128]{1,0:T(8,128)S(1)}, f32[224,128]{1,0:T(8,128)S(1)}, u32[]{:S(2)}, u32[]{:S(2)}) %collective-permute-start.4) | collective-permute-done | bytes 114720 | tf_op jit(solution)/shard_map/ppermute | solution.py:375
  31.5 0.1 collective-permute-start.5
  31.6 1.5 %collective-permute-done.5.other_v = f32[448,128]{1,0:T(8,128)S(1)} collective-permute-done((f32[448,128]{1,0:T(8,128)S(1)}, f32[448,128]{1,0:T(8,128)S(1)}, u32[]{:S(2)}, u32[]{:S(2)}) %collective-permute-start.5) | collective-permute-done | bytes 229408 | tf_op jit(solution)/shard_map/ppermute | solution.py:375
  33.0 17.2 %shard_map.79 = (f32[4096,256]{1,0:T(8,128)}, f32[1,4096]{1,0:T(1,128)}) custom-call(f32[448,128]{1,0:T(8,128)S(1)} %pad_maximum_fusion.mine_v, f32[448,128]{1,0:T(8,128)S(1)} %collective-permute-done.5.other_v, f32[1,4096]{1,0:T(1,128)S(1)} %bitcast.4, f32[4096,256]{1,0:T(8,128)} %x_hbm.5), custom_call_target="tpu_custom_call" | custom-call | tf_op jit(solution)/shard_map/pallas_call | solution.py:357
  (7 shorter events, 0.1 us)
Async XLA Ops:
  0.6 3.4 %copy-start = (f32[4096]{0:T(1024)S(1)}, f32[4096]{0:T(1024)}, u32[]{:S(2)}) copy-start(f32[4096]{0:T(1024)} %param.7) | copy-start | bytes 49156
  0.6 3.4 %copy-start.1 = (s32[2,128]{1,0:T(2,128)S(1)}, s32[2,128]{1,0:T(2,128)}, u32[]{:S(2)}) copy-start(s32[2,128]{1,0:T(2,128)} %rows_v.1) | copy-start | bytes 3076
  0.7 3.4 %copy-start.4 = (s32[2]{0:T(128)S(1)}, s32[2]{0:T(128)}, u32[]{:S(2)}) copy-start(s32[2]{0:T(128)} %owner_s.1) | copy-start | bytes 28
  0.7 3.4 %copy-start.3 = (f32[2,128]{1,0:T(2,128)S(1)}, f32[2,128]{1,0:T(2,128)}, u32[]{:S(2)}) copy-start(f32[2,128]{1,0:T(2,128)} %error_var.1) | copy-start | bytes 3076
  0.7 3.4 %copy-start.2 = (f32[2,128]{1,0:T(2,128)S(1)}, f32[2,128]{1,0:T(2,128)}, u32[]{:S(2)}) copy-start(f32[2,128]{1,0:T(2,128)} %observed.1) | copy-start | bytes 3076
  5.7 2.6 %collective-permute-start = (f32[448,128]{1,0:T(8,128)S(1)}, f32[448,128]{1,0:T(8,128)S(1)}, u32[]{:S(2)}, u32[]{:S(2)}) collective-permute-start(f32[448,128]{1,0:T(8,128)S(1)} %get-tuple-element.7), channel_id=1, source_target_pairs={{0,1},{1,0},{2,3},{3,2},{4,5},{5,4},{6,7},{7,6},{8,9},{9,8},{10,11... | collective-permute-start | bytes 688136 | tf_op jit(solution)/shard_map/ppermute | solution.py:375
  8.3 5.9 %collective-permute-start.1 = (f32[224,128]{1,0:T(8,128)S(1)}, f32[224,128]{1,0:T(8,128)S(1)}, u32[]{:S(2)}, u32[]{:S(2)}) collective-permute-start(f32[224,128]{1,0:T(8,128)S(1)} %slice_select_fusion), channel_id=1, source_target_pairs={{0,2},{1,3},{2,0},{3,1},{4,6},{5,7},{6,4},{7,5},{8,10},{9,11},{10,... | collective-permute-start | bytes 344072 | tf_op jit(solution)/shard_map/ppermute | solution.py:375
  14.3 4.9 %collective-permute-start.2 = (f32[224,128]{1,0:T(8,128)S(1)}, f32[224,128]{1,0:T(8,128)S(1)}, u32[]{:S(2)}, u32[]{:S(2)}) collective-permute-start(f32[224,128]{1,0:T(8,128)S(1)} %select_add_fusion), channel_id=1, source_target_pairs={{0,4},{1,5},{2,6},{3,7},{4,0},{5,1},{6,2},{7,3},{8,12},{9,13},{10,... | collective-permute-start | bytes 344072 | tf_op jit(solution)/shard_map/ppermute | solution.py:375
  19.2 7.3 %collective-permute-start.3 = (f32[224,128]{1,0:T(8,128)S(1)}, f32[224,128]{1,0:T(8,128)S(1)}, u32[]{:S(2)}, u32[]{:S(2)}) collective-permute-start(f32[224,128]{1,0:T(8,128)S(1)} %add.14), channel_id=1, source_target_pairs={{0,8},{1,9},{2,10},{3,11},{4,12},{5,13},{6,14},{7,15},{8,0},{9,1},... | collective-permute-start | bytes 344072 | tf_op jit(solution)/shard_map/ppermute | solution.py:375
  26.6 4.9 %collective-permute-start.4 = (f32[224,128]{1,0:T(8,128)S(1)}, f32[224,128]{1,0:T(8,128)S(1)}, u32[]{:S(2)}, u32[]{:S(2)}) collective-permute-start(f32[224,128]{1,0:T(8,128)S(1)} %add.15), channel_id=1, source_target_pairs={{0,2},{1,3},{2,0},{3,1},{4,6},{5,7},{6,4},{7,5},{8,10},{9,11},{10,... | collective-permute-start | bytes 344072 | tf_op jit(solution)/shard_map/ppermute | solution.py:375
  31.5 1.6 %collective-permute-start.5 = (f32[448,128]{1,0:T(8,128)S(1)}, f32[448,128]{1,0:T(8,128)S(1)}, u32[]{:S(2)}, u32[]{:S(2)}) collective-permute-start(f32[448,128]{1,0:T(8,128)S(1)} %pad_maximum_fusion.mine_v), channel_id=1, source_target_pairs={{0,1},{1,0},{2,3},{3,2},{4,5},{5,4},{6,7},{7,6},{8,9},{9,8},{10,11... | collective-permute-start | bytes 688136 | tf_op jit(solution)/shard_map/ppermute | solution.py:375

commit v5 on v4

--- a/solution.py
+++ b/solution.py
@@ -181,9 +181,18 @@
         for g in range(groups):
             out.append(jnp.where(lane <= base + SUB * g + sub, done[g], 0.0))
         lines = [row(work[p // SUB], p % SUB) for p in range(STEP)]
-        for i in range(s + groups, count):
+        later = s + 2 * groups
+        for i in range(s + groups, min(later, count)):
             change = tree([spread(rows[i], base + p) * lines[p] for p in range(STEP)])
             rows[i] = jnp.where(here, 0.0, rows[i]) - change
+        if later < count:
+            rest = jnp.concatenate(rows[later:], axis=0)
+            inside = jnp.concatenate([here] * (count - later), axis=0)
+            pieces = [jnp.zeros((base, LANES), F32)] if base else []
+            pieces += work + [jnp.zeros((LANES - base - STEP, LANES), F32)]
+            change = dot(jnp.where(inside, rest, 0.0), jnp.concatenate(pieces, axis=0))
+            rest = jnp.where(inside, 0.0, rest) - change
+            rows[later:] = [rest[SUB * i : SUB * (i + 1), :] for i in range(count - later)]
     return jnp.concatenate(out, axis=0)
 
 
@@ -376,16 +385,16 @@
 
 
 def total(keep, send, count):
-    odd = ((lax.axis_index(AXIS) >> 1) & 1) == 1
     value = keep + swap(send, count, 1)
-    low, high = jnp.split(value, 2, axis=0)
-    value = jnp.where(odd, high, low) + swap(jnp.where(odd, low, high), count, 2)
-    mask = 4
-    while mask < count:
-        value = value + swap(value, count, mask)
-        mask *= 2
-    got = swap(value, count, 2)
-    value = jnp.concatenate([jnp.where(odd, got, value), jnp.where(odd, value, got)], axis=0)
+    parts = count // 2
+    groups = [list(range(start, count, 2)) for start in (0, 1)]
+
+    def trade(x):
+        return lax.all_to_all(x, AXIS, split_axis=0, concat_axis=0, axis_index_groups=groups)
+
+    shares = value.reshape(parts, value.shape[0] // parts, LANES)
+    share = jnp.sum(trade(shares), axis=0)
+    value = trade(jnp.broadcast_to(share, (parts,) + share.shape)).reshape(value.shape)
     return value, swap(value, count, 1)
 
 

time: 50.6 us -> 51.2 us (1.012)
  blocking collectives: 0 us -> 27 us
  waiting for transfers between devices: 18.2 us -> 2.6 us
  starting transfers between devices: 8.92 us -> 0.51 us
  Pallas kernels: 22.1 us -> 19.8 us
    all_to_all x0 -> x2, blocking collectives: none -> 27 us  [trade(): lax.all_to_all(x, AXIS, split_axis=0, concat_axis=0, axis_index_groups=gr...]
    ppermute x6 -> x2, waiting for transfers between devices: 18.2 us -> 2.6 us  [swap(): return lax.ppermute(value, AXIS, [(i, i ^ mask) for i in range(count)])]
    ppermute x6 -> x2, starting transfers between devices: 8.92 us -> 0.51 us  [swap(): return lax.ppermute(value, AXIS, [(i, i ^ mask) for i in range(count)])]
    pallas_call x1, Pallas kernels: 17.2 us -> 15 us  [update(): pl.pallas_call(functools.partial(update_kernel, chunks), out_shape=(jax.S...]
  transfers between devices with their start and end apart: 6 -> 2, of which waited for: 6 -> 2; matrix products, arithmetic and copies ran while one was open for 0% -> 0% of each run, Pallas kernels for 0% -> 0%
where the time goes in v5:
time: 51.2 us; the launch traced here: 51 us
  blocking collectives  27 us (53%)
  Pallas kernels  19.8 us (39%)
  waiting for transfers between devices  2.6 us (5%)
  between operations  0.9 us (2%)
    all_to_all x2, blocking collectives, trade(): lax.all_to_all(x, AXIS, split_axis=0, concat_axis=0, axis_index_groups=gr...  27 us
    pallas_call x1, Pallas kernels, update(): pl.pallas_call(functools.partial(update_kernel, chunks), out_shape=(jax.S...  15 us
    pallas_call x1, Pallas kernels, gram_of(): pl.pallas_call(functools.partial(gram_kernel, chunks), out_shape=jax.Shap...  3.38 us
    ppermute x2, waiting for transfers between devices, swap(): return lax.ppermute(value, AXIS, [(i, i ^ mask) for i in range(count)])  2.6 us
    pallas_call x1, Pallas kernels, gather(): pl.pallas_call(gather_kernel, out_shape=(half, half), in_specs=[spec(pltp...  1.44 us
  transfers between devices with their start and end apart: 2, of which 2 were waited for; matrix products, arithmetic and copies ran while one was open for 0% of the time, Pallas kernels for 0%

profile of v5, /device:TPU:0, one launch (start us, length us, event | category | flops | bytes accessed | tf_op | source)
XLA Modules:
  0.0 51.0 jit_solution(9541655510333648318)
XLA Ops:
  0.6 0.0 copy-start
  0.6 0.0 copy-start.1
  0.7 0.0 copy-start.4
  0.7 0.0 copy-start.3
  0.7 0.0 copy-start.2
  0.7 3.4 %shard_map.77.gram = f32[384,128]{1,0:T(8,128)S(1)} custom-call(f32[4096,256]{1,0:T(8,128)} %x_hbm.5), custom_call_target="tpu_custom_call" | custom-call | flops 1073741824 | bytes 4194304 | tf_op jit(solution)/shard_map/pallas_call | solution.py:335
  4.1 0.0 copy-done
  4.1 0.0 copy-done.1
  4.1 0.0 copy-done.4
  4.1 0.0 copy-done.3
  4.1 0.0 copy-done.2
  4.1 1.4 %shard_map.78 = (f32[448,128]{1,0:T(8,128)S(1)}, f32[448,128]{1,0:T(8,128)S(1)}) custom-call(s32[2]{0:T(128)S(1)} %copy-done.4, s32[2,128]{1,0:T(2,128)S(1)} %copy-done.1, s32[2,128]{1,0:T(2,128)S(1)} %copy-done.1, f32[2,128]{1,0:T(2,128)S(1)} %copy-done.2, f32[2,128]{1,0:T(2,128)S(1)} %copy-done.3, f32[32,128]{1,0:T(8,128)S(1)} %bitcast.7, ...), custom_call_target="tpu_custom_call" | custom-call | tf_op jit(solution)/shard_map/pallas_call | solution.py:349
  5.6 0.5 collective-permute-start
  6.1 1.1 %collective-permute-done = f32[448,128]{1,0:T(8,128)S(1)} collective-permute-done((f32[448,128]{1,0:T(8,128)S(1)}, f32[448,128]{1,0:T(8,128)S(1)}, u32[]{:S(2)}, u32[]{:S(2)}) %collective-permute-start) | collective-permute-done | bytes 229408 | tf_op jit(solution)/shard_map/ppermute | solution.py:384
  7.2 15.7 %all_to_all.10 = f32[8,56,128]{2,1,0:T(8,128)S(1)} all-to-all(f32[8,56,128]{2,1,0:T(8,128)S(1)} %bitcast.9), channel_id=1, replica_groups={{0,2,4,6,8,10,12,14},{1,3,5,7,9,11,13,15},{16,18,20,22,24,26,28,30},{17..., dimensions={0} | all-to-all | bytes 458752 | tf_op jit(solution)/shard_map/all_to_all | solution.py:393
  23.0 11.3 %all_to_all.11 = f32[8,56,128]{2,1,0:T(8,128)S(1)} all-to-all(f32[8,56,128]{2,1,0:T(8,128)S(1)} %broadcast_in_dim.3), channel_id=1, replica_groups={{0,2,4,6,8,10,12,14},{1,3,5,7,9,11,13,15},{16,18,20,22,24,26,28,30},{17..., dimensions={0} | all-to-all | bytes 458752 | tf_op jit(solution)/shard_map/all_to_all | solution.py:393
  34.3 0.0 collective-permute-start.1
  34.3 1.5 %collective-permute-done.1.other_v = f32[448,128]{1,0:T(8,128)S(1)} collective-permute-done((f32[448,128]{1,0:T(8,128)S(1)}, f32[448,128]{1,0:T(8,128)S(1)}, u32[]{:S(2)}, u32[]{:S(2)}) %collective-permute-start.1) | collective-permute-done | bytes 229408 | tf_op jit(solution)/shard_map/ppermute | solution.py:384
  35.8 15.0 %shard_map.79 = (f32[4096,256]{1,0:T(8,128)}, f32[1,4096]{1,0:T(1,128)}) custom-call(f32[448,128]{1,0:T(8,128)S(1)} %bitcast.6, f32[448,128]{1,0:T(8,128)S(1)} %collective-permute-done.1.other_v, f32[1,4096]{1,0:T(1,128)S(1)} %bitcast.8, f32[4096,256]{1,0:T(8,128)} %x_hbm.5), custom_call_target="tpu_custom_call" | custom-call | tf_op jit(solution)/shard_map/pallas_call | solution.py:366
  (3 shorter events, 0.1 us)
Async XLA Ops:
  0.6 3.4 %copy-start = (f32[4096]{0:T(1024)S(1)}, f32[4096]{0:T(1024)}, u32[]{:S(2)}) copy-start(f32[4096]{0:T(1024)} %param.7) | copy-start | bytes 49156
  0.6 3.4 %copy-start.1 = (s32[2,128]{1,0:T(2,128)S(1)}, s32[2,128]{1,0:T(2,128)}, u32[]{:S(2)}) copy-start(s32[2,128]{1,0:T(2,128)} %rows_v.1) | copy-start | bytes 3076
  0.7 3.4 %copy-start.4 = (s32[2]{0:T(128)S(1)}, s32[2]{0:T(128)}, u32[]{:S(2)}) copy-start(s32[2]{0:T(128)} %owner_s.1) | copy-start | bytes 28
  0.7 3.4 %copy-start.3 = (f32[2,128]{1,0:T(2,128)S(1)}, f32[2,128]{1,0:T(2,128)}, u32[]{:S(2)}) copy-start(f32[2,128]{1,0:T(2,128)} %error_var.1) | copy-start | bytes 3076
  0.7 3.4 %copy-start.2 = (f32[2,128]{1,0:T(2,128)S(1)}, f32[2,128]{1,0:T(2,128)}, u32[]{:S(2)}) copy-start(f32[2,128]{1,0:T(2,128)} %observed.1) | copy-start | bytes 3076
  5.6 1.6 %collective-permute-start = (f32[448,128]{1,0:T(8,128)S(1)}, f32[448,128]{1,0:T(8,128)S(1)}, u32[]{:S(2)}, u32[]{:S(2)}) collective-permute-start(f32[448,128]{1,0:T(8,128)S(1)} %get-tuple-element.7), channel_id=1, source_target_pairs={{0,1},{1,0},{2,3},{3,2},{4,5},{5,4},{6,7},{7,6},{8,9},{9,8},{10,11... | collective-permute-start | bytes 688136 | tf_op jit(solution)/shard_map/ppermute | solution.py:384
  34.3 1.5 %collective-permute-start.1 = (f32[448,128]{1,0:T(8,128)S(1)}, f32[448,128]{1,0:T(8,128)S(1)}, u32[]{:S(2)}, u32[]{:S(2)}) collective-permute-start(f32[448,128]{1,0:T(8,128)S(1)} %bitcast.5), channel_id=1, source_target_pairs={{0,1},{1,0},{2,3},{3,2},{4,5},{5,4},{6,7},{7,6},{8,9},{9,8},{10,11... | collective-permute-start | bytes 688136 | tf_op jit(solution)/shard_map/ppermute | solution.py:384

commit v6 on v4

--- a/solution.py
+++ b/solution.py
@@ -181,9 +181,18 @@
         for g in range(groups):
             out.append(jnp.where(lane <= base + SUB * g + sub, done[g], 0.0))
         lines = [row(work[p // SUB], p % SUB) for p in range(STEP)]
-        for i in range(s + groups, count):
+        later = s + 2 * groups
+        for i in range(s + groups, min(later, count)):
             change = tree([spread(rows[i], base + p) * lines[p] for p in range(STEP)])
             rows[i] = jnp.where(here, 0.0, rows[i]) - change
+        if later < count:
+            rest = jnp.concatenate(rows[later:], axis=0)
+            inside = jnp.concatenate([here] * (count - later), axis=0)
+            pieces = [jnp.zeros((base, LANES), F32)] if base else []
+            pieces += work + [jnp.zeros((LANES - base - STEP, LANES), F32)]
+            change = dot(jnp.where(inside, rest, 0.0), jnp.concatenate(pieces, axis=0))
+            rest = jnp.where(inside, 0.0, rest) - change
+            rows[later:] = [rest[SUB * i : SUB * (i + 1), :] for i in range(count - later)]
     return jnp.concatenate(out, axis=0)
 
 
@@ -193,14 +202,6 @@
 
 def add_up(x):
     return jnp.sum(jnp.sum(x, axis=0, keepdims=True), axis=1, keepdims=True)
-
-
-def dot3(a, b):
-    a_high, a_low = split(a)
-    b_high, b_low = split(b)
-    return dot(
-        jnp.concatenate([a_high, a_low, a_high], axis=1), jnp.concatenate([b_high, b_high, b_low], axis=0), precision=None
-    )
 
 
 def identity(size):
@@ -246,33 +247,40 @@
     eye = identity(half)
 
     inv_m = factor(eye + dot(first, first, ((1,), (1,))))
-    v_and_f = dot(inv_m, jnp.concatenate([first, innovation(0)], axis=1))
-    v, f = v_and_f[:, :members], v_and_f[:, members:]
+    seen = dot(dot(first, gram), first, ((1,), (1,)))
     before = add_up(eye * (g00 + g11))
-    after1 = before - add_up(dot3(v, gram) * v)
+    after1 = before - add_up(dot(inv_m, seen) * inv_m)
     factor1 = blend(before, after1)
-    increment = jnp.sum(v * jnp.concatenate([f, f], axis=1), axis=0, keepdims=True)
-    innov2 = innovation(1) - jnp.sum(second * increment, axis=1, keepdims=True)
 
     a1 = dot(first, first, ((0,), (0,)))
-    a2 = dot(second, jnp.concatenate([second, innov2], axis=1), ((0,), (0,)))
+    a2 = dot(second, second, ((0,), (0,)))
     square = factor1 * factor1
     k00 = eye + a1[:half, :half] + a2[:half, :half] * square
-    k01 = a1[:half, half:] + a2[:half, half:members] * square
-    k11 = eye + a1[half:, half:] + a2[half:, half:members] * square
+    k01 = a1[:half, half:] + a2[:half, half:] * square
+    k11 = eye + a1[half:, half:] + a2[half:, half:] * square
     inv00 = factor(k00)
     u = dot(inv00, k01)
     inv11 = factor(k11 - dot(u, u, ((0,), (0,))))
-    inv10 = -dot(inv11, dot(u, inv00, ((0,), (0,))))
-    y0 = dot(inv00, a2[:half, members:] * square)
-    y1 = dot(inv11, a2[half:, members:] * square - dot(u, y0, ((0,), (0,))))
-    bottom = jnp.concatenate([inv10, inv11], axis=1)
-    top_trace = add_up(dot3(inv00, g00) * inv00)
-    after2 = top_trace + add_up(dot3(bottom, gram) * bottom)
+
+    v_and_f = dot(inv_m, jnp.concatenate([first, innovation(0)], axis=1))
+    v, f = v_and_f[:, :members], v_and_f[:, members:]
+    increment = jnp.sum(v * jnp.concatenate([f, f], axis=1), axis=0, keepdims=True)
+    innov2 = innovation(1) - jnp.sum(second * increment, axis=1, keepdims=True)
+    target = dot(second, innov2, ((0,), (0,))) * square
+    y0 = dot(inv00, target[:half, :])
+    below = target[half:, :] - dot(u, y0, ((0,), (0,)))
+
+    q = dot(u, inv00, ((0,), (0,)))
+    inv10 = -dot(inv11, q)
+    y1 = dot(inv11, below)
+    left = g01.T - dot(q, g00)
+    rest = g11 - dot(q, g01) - dot(left, q, ((1,), (1,)))
+    after2 = add_up(dot(inv00, g00) * inv00) + add_up(dot(inv11, rest) * inv11)
     factor2 = factor1 * blend(after1, after2)
     increment0 = jnp.sum(y0 * inv00 + y1 * inv10, axis=0, keepdims=True)
     increment1 = jnp.sum(y1 * inv11, axis=0, keepdims=True)
     increment = increment + jnp.concatenate([increment0, increment1], axis=1)
+    bottom = jnp.concatenate([inv10, inv11], axis=1)
 
     inverse = jnp.concatenate([jnp.concatenate([inv00, jnp.zeros_like(inv00)], axis=1), bottom], axis=0)
     high, low = split(inverse)

time: 50.6 us -> 49 us (0.968)
  Pallas kernels: 22.1 us -> 20.3 us
  waiting for transfers between devices: 18.2 us -> 18.9 us
    pallas_call x1, Pallas kernels: 17.2 us -> 15.4 us  [update(): pl.pallas_call(functools.partial(update_kernel, chunks), out_shape=(jax.S...]
    ppermute x6, waiting for transfers between devices: 18.2 us -> 18.9 us  [swap(): return lax.ppermute(value, AXIS, [(i, i ^ mask) for i in range(count)])]
where the time goes in v6:
time: 49 us; the launch traced here: 48.9 us
  Pallas kernels  20.3 us (41%)
  waiting for transfers between devices  18.9 us (39%)
  starting transfers between devices  8.53 us (17%)
  between operations  0.94 us (2%)
    ppermute x6, waiting for transfers between devices, swap(): return lax.ppermute(value, AXIS, [(i, i ^ mask) for i in range(count)])  18.9 us
    pallas_call x1, Pallas kernels, update(): pl.pallas_call(functools.partial(update_kernel, chunks), out_shape=(jax.S...  15.4 us
    ppermute x6, starting transfers between devices, swap(): return lax.ppermute(value, AXIS, [(i, i ^ mask) for i in range(count)])  8.53 us
    pallas_call x1, Pallas kernels, gram_of(): pl.pallas_call(functools.partial(gram_kernel, chunks), out_shape=jax.Shap...  3.38 us
    pallas_call x1, Pallas kernels, gather(): pl.pallas_call(gather_kernel, out_shape=(half, half), in_specs=[spec(pltp...  1.59 us
  transfers between devices with their start and end apart: 6, of which 6 were waited for; matrix products, arithmetic and copies ran while one was open for 0% of the time, Pallas kernels for 0%

profile of v6, /device:TPU:0, one launch (start us, length us, event | category | flops | bytes accessed | tf_op | source)
XLA Modules:
  0.0 48.9 jit_solution(2816045009591824934)
XLA Ops:
  0.6 0.0 copy-start
  0.6 0.0 copy-start.1
  0.7 0.0 copy-start.4
  0.7 0.0 copy-start.3
  0.7 0.0 copy-start.2
  0.7 3.4 %shard_map.77.gram = f32[384,128]{1,0:T(8,128)S(1)} custom-call(f32[4096,256]{1,0:T(8,128)} %x_hbm.5), custom_call_target="tpu_custom_call" | custom-call | flops 1073741824 | bytes 4194304 | tf_op jit(solution)/shard_map/pallas_call | solution.py:334
  4.1 0.0 copy-done
  4.1 0.0 copy-done.1
  4.1 0.0 copy-done.4
  4.1 0.0 copy-done.3
  4.1 0.0 copy-done.2
  4.1 1.6 %shard_map.78 = (f32[448,128]{1,0:T(8,128)S(1)}, f32[448,128]{1,0:T(8,128)S(1)}) custom-call(s32[2]{0:T(128)S(1)} %copy-done.4, s32[2,128]{1,0:T(2,128)S(1)} %copy-done.1, s32[2,128]{1,0:T(2,128)S(1)} %copy-done.1, f32[2,128]{1,0:T(2,128)S(1)} %copy-done.2, f32[2,128]{1,0:T(2,128)S(1)} %copy-done.3, f32[32,128]{1,0:T(8,128)S(1)} %bitcast.3, ...), custom_call_target="tpu_custom_call" | custom-call | tf_op jit(solution)/shard_map/pallas_call | solution.py:348
  5.7 0.5 %collective-permute-start = (f32[448,128]{1,0:T(8,128)S(1)}, f32[448,128]{1,0:T(8,128)S(1)}, u32[]{:S(2)}, u32[]{:S(2)}) collective-permute-start(f32[448,128]{1,0:T(8,128)S(1)} %get-tuple-element.7), channel_id=1, source_target_pairs={{0,1},{1,0},{2,3},{3,2},{4,5},{5,4},{6,7},{7,6},{8,9},{9,8},{10,11... | collective-permute-start | bytes 688136 | tf_op jit(solution)/shard_map/ppermute | solution.py:383
  6.2 1.1 %collective-permute-done = f32[448,128]{1,0:T(8,128)S(1)} collective-permute-done((f32[448,128]{1,0:T(8,128)S(1)}, f32[448,128]{1,0:T(8,128)S(1)}, u32[]{:S(2)}, u32[]{:S(2)}) %collective-permute-start) | collective-permute-done | bytes 229408 | tf_op jit(solution)/shard_map/ppermute | solution.py:383
  7.4 3.0 %collective-permute-start.1 = (f32[224,128]{1,0:T(8,128)S(1)}, f32[224,128]{1,0:T(8,128)S(1)}, u32[]{:S(2)}, u32[]{:S(2)}) collective-permute-start(f32[224,128]{1,0:T(8,128)S(1)} %slice_select_fusion), channel_id=1, source_target_pairs={{0,2},{1,3},{2,0},{3,1},{4,6},{5,7},{6,4},{7,5},{8,10},{9,11},{10,... | collective-permute-start | bytes 344072 | tf_op jit(solution)/shard_map/ppermute | solution.py:383
  10.4 3.4 %collective-permute-done.1 = f32[224,128]{1,0:T(8,128)S(1)} collective-permute-done((f32[224,128]{1,0:T(8,128)S(1)}, f32[224,128]{1,0:T(8,128)S(1)}, u32[]{:S(2)}, u32[]{:S(2)}) %collective-permute-start.1) | collective-permute-done | bytes 114720 | tf_op jit(solution)/shard_map/ppermute | solution.py:383
  13.8 2.6 %collective-permute-start.2 = (f32[224,128]{1,0:T(8,128)S(1)}, f32[224,128]{1,0:T(8,128)S(1)}, u32[]{:S(2)}, u32[]{:S(2)}) collective-permute-start(f32[224,128]{1,0:T(8,128)S(1)} %select_add_fusion), channel_id=1, source_target_pairs={{0,4},{1,5},{2,6},{3,7},{4,0},{5,1},{6,2},{7,3},{8,12},{9,13},{10,... | collective-permute-start | bytes 344072 | tf_op jit(solution)/shard_map/ppermute | solution.py:383
  16.4 2.9 %collective-permute-done.2 = f32[224,128]{1,0:T(8,128)S(1)} collective-permute-done((f32[224,128]{1,0:T(8,128)S(1)}, f32[224,128]{1,0:T(8,128)S(1)}, u32[]{:S(2)}, u32[]{:S(2)}) %collective-permute-start.2) | collective-permute-done | bytes 114720 | tf_op jit(solution)/shard_map/ppermute | solution.py:383
  19.4 2.3 %collective-permute-start.3 = (f32[224,128]{1,0:T(8,128)S(1)}, f32[224,128]{1,0:T(8,128)S(1)}, u32[]{:S(2)}, u32[]{:S(2)}) collective-permute-start(f32[224,128]{1,0:T(8,128)S(1)} %add.14), channel_id=1, source_target_pairs={{0,8},{1,9},{2,10},{3,11},{4,12},{5,13},{6,14},{7,15},{8,0},{9,1},... | collective-permute-start | bytes 344072 | tf_op jit(solution)/shard_map/ppermute | solution.py:383
  21.7 5.2 %collective-permute-done.3 = f32[224,128]{1,0:T(8,128)S(1)} collective-permute-done((f32[224,128]{1,0:T(8,128)S(1)}, f32[224,128]{1,0:T(8,128)S(1)}, u32[]{:S(2)}, u32[]{:S(2)}) %collective-permute-start.3) | collective-permute-done | bytes 114720 | tf_op jit(solution)/shard_map/ppermute | solution.py:383
  26.9 0.1 collective-permute-start.4
  27.0 4.8 %collective-permute-done.4 = f32[224,128]{1,0:T(8,128)S(1)} collective-permute-done((f32[224,128]{1,0:T(8,128)S(1)}, f32[224,128]{1,0:T(8,128)S(1)}, u32[]{:S(2)}, u32[]{:S(2)}) %collective-permute-start.4) | collective-permute-done | bytes 114720 | tf_op jit(solution)/shard_map/ppermute | solution.py:383
  31.8 0.1 collective-permute-start.5
  31.9 1.5 %collective-permute-done.5.other_v = f32[448,128]{1,0:T(8,128)S(1)} collective-permute-done((f32[448,128]{1,0:T(8,128)S(1)}, f32[448,128]{1,0:T(8,128)S(1)}, u32[]{:S(2)}, u32[]{:S(2)}) %collective-permute-start.5) | collective-permute-done | bytes 229408 | tf_op jit(solution)/shard_map/ppermute | solution.py:383
  33.4 15.4 %shard_map.79 = (f32[4096,256]{1,0:T(8,128)}, f32[1,4096]{1,0:T(1,128)}) custom-call(f32[448,128]{1,0:T(8,128)S(1)} %pad_maximum_fusion.mine_v, f32[448,128]{1,0:T(8,128)S(1)} %collective-permute-done.5.other_v, f32[1,4096]{1,0:T(1,128)S(1)} %bitcast.4, f32[4096,256]{1,0:T(8,128)} %x_hbm.5), custom_call_target="tpu_custom_call" | custom-call | tf_op jit(solution)/shard_map/pallas_call | solution.py:365
  (7 shorter events, 0.1 us)
Async XLA Ops:
  0.6 3.4 %copy-start = (f32[4096]{0:T(1024)S(1)}, f32[4096]{0:T(1024)}, u32[]{:S(2)}) copy-start(f32[4096]{0:T(1024)} %param.7) | copy-start | bytes 49156
  0.6 3.4 %copy-start.1 = (s32[2,128]{1,0:T(2,128)S(1)}, s32[2,128]{1,0:T(2,128)}, u32[]{:S(2)}) copy-start(s32[2,128]{1,0:T(2,128)} %rows_v.1) | copy-start | bytes 3076
  0.7 3.4 %copy-start.4 = (s32[2]{0:T(128)S(1)}, s32[2]{0:T(128)}, u32[]{:S(2)}) copy-start(s32[2]{0:T(128)} %owner_s.1) | copy-start | bytes 28
  0.7 3.4 %copy-start.3 = (f32[2,128]{1,0:T(2,128)S(1)}, f32[2,128]{1,0:T(2,128)}, u32[]{:S(2)}) copy-start(f32[2,128]{1,0:T(2,128)} %error_var.1) | copy-start | bytes 3076
  0.7 3.4 %copy-start.2 = (f32[2,128]{1,0:T(2,128)S(1)}, f32[2,128]{1,0:T(2,128)}, u32[]{:S(2)}) copy-start(f32[2,128]{1,0:T(2,128)} %observed.1) | copy-start | bytes 3076
  5.7 1.6 %collective-permute-start = (f32[448,128]{1,0:T(8,128)S(1)}, f32[448,128]{1,0:T(8,128)S(1)}, u32[]{:S(2)}, u32[]{:S(2)}) collective-permute-start(f32[448,128]{1,0:T(8,128)S(1)} %get-tuple-element.7), channel_id=1, source_target_pairs={{0,1},{1,0},{2,3},{3,2},{4,5},{5,4},{6,7},{7,6},{8,9},{9,8},{10,11... | collective-permute-start | bytes 688136 | tf_op jit(solution)/shard_map/ppermute | solution.py:383
  7.4 6.4 %collective-permute-start.1 = (f32[224,128]{1,0:T(8,128)S(1)}, f32[224,128]{1,0:T(8,128)S(1)}, u32[]{:S(2)}, u32[]{:S(2)}) collective-permute-start(f32[224,128]{1,0:T(8,128)S(1)} %slice_select_fusion), channel_id=1, source_target_pairs={{0,2},{1,3},{2,0},{3,1},{4,6},{5,7},{6,4},{7,5},{8,10},{9,11},{10,... | collective-permute-start | bytes 344072 | tf_op jit(solution)/shard_map/ppermute | solution.py:383
  13.8 5.5 %collective-permute-start.2 = (f32[224,128]{1,0:T(8,128)S(1)}, f32[224,128]{1,0:T(8,128)S(1)}, u32[]{:S(2)}, u32[]{:S(2)}) collective-permute-start(f32[224,128]{1,0:T(8,128)S(1)} %select_add_fusion), channel_id=1, source_target_pairs={{0,4},{1,5},{2,6},{3,7},{4,0},{5,1},{6,2},{7,3},{8,12},{9,13},{10,... | collective-permute-start | bytes 344072 | tf_op jit(solution)/shard_map/ppermute | solution.py:383
  19.4 7.5 %collective-permute-start.3 = (f32[224,128]{1,0:T(8,128)S(1)}, f32[224,128]{1,0:T(8,128)S(1)}, u32[]{:S(2)}, u32[]{:S(2)}) collective-permute-start(f32[224,128]{1,0:T(8,128)S(1)} %add.14), channel_id=1, source_target_pairs={{0,8},{1,9},{2,10},{3,11},{4,12},{5,13},{6,14},{7,15},{8,0},{9,1},... | collective-permute-start | bytes 344072 | tf_op jit(solution)/shard_map/ppermute | solution.py:383
  26.9 4.9 %collective-permute-start.4 = (f32[224,128]{1,0:T(8,128)S(1)}, f32[224,128]{1,0:T(8,128)S(1)}, u32[]{:S(2)}, u32[]{:S(2)}) collective-permute-start(f32[224,128]{1,0:T(8,128)S(1)} %add.15), channel_id=1, source_target_pairs={{0,2},{1,3},{2,0},{3,1},{4,6},{5,7},{6,4},{7,5},{8,10},{9,11},{10,... | collective-permute-start | bytes 344072 | tf_op jit(solution)/shard_map/ppermute | solution.py:383
  31.8 1.6 %collective-permute-start.5 = (f32[448,128]{1,0:T(8,128)S(1)}, f32[448,128]{1,0:T(8,128)S(1)}, u32[]{:S(2)}, u32[]{:S(2)}) collective-permute-start(f32[448,128]{1,0:T(8,128)S(1)} %pad_maximum_fusion.mine_v), channel_id=1, source_target_pairs={{0,1},{1,0},{2,3},{3,2},{4,5},{5,4},{6,7},{7,6},{8,9},{9,8},{10,11... | collective-permute-start | bytes 688136 | tf_op jit(solution)/shard_map/ppermute | solution.py:383

commit v7 on v6

--- a/solution.py
+++ b/solution.py
@@ -16,7 +16,7 @@
 SUB = 8
 OBS = 128
 VMEM_LIMIT = 51 * 1024 * 1024
-STEP = 16
+STEP = 8
 
 A0, A1, B0, B1, G00, G01, G11 = range(0, 7 * 128, 128)
 PACKED = 7 * 128
@@ -204,6 +204,13 @@
     return jnp.sum(jnp.sum(x, axis=0, keepdims=True), axis=1, keepdims=True)
 
 
+def dot3(a, b):
+    a_high, a_low = split(a)
+    b_high, b_low = split(b)
+    left = jnp.concatenate([a_high, a_low, a_high], axis=1)
+    return dot(left, jnp.concatenate([b_high, b_high, b_low], axis=0), precision=None)
+
+
 def identity(size):
     return (
         lax.broadcasted_iota(jnp.int32, (size, size), 0) == lax.broadcasted_iota(jnp.int32, (size, size), 1)
@@ -233,7 +240,7 @@
 
     def innovation(k):
         at = INNOV + 2 * k
-        return column(jnp.concatenate([full[at : at + 1, :quarter], full[at + 1 : at + 2, :quarter]], axis=1))
+        return jnp.concatenate([full[at : at + 1, :quarter], full[at + 1 : at + 2, :quarter]], axis=1)
 
     first = jnp.concatenate([block(A0), block(A1)], axis=1)
     second = jnp.concatenate([block(B0), block(B1)], axis=1)
@@ -247,44 +254,35 @@
     eye = identity(half)
 
     inv_m = factor(eye + dot(first, first, ((1,), (1,))))
-    seen = dot(dot(first, gram), first, ((1,), (1,)))
+    v = dot(inv_m, first)
     before = add_up(eye * (g00 + g11))
-    after1 = before - add_up(dot(inv_m, seen) * inv_m)
+    after1 = before - add_up(dot3(v, gram) * v)
     factor1 = blend(before, after1)
-
-    a1 = dot(first, first, ((0,), (0,)))
-    a2 = dot(second, second, ((0,), (0,)))
-    square = factor1 * factor1
-    k00 = eye + a1[:half, :half] + a2[:half, :half] * square
-    k01 = a1[:half, half:] + a2[:half, half:] * square
-    k11 = eye + a1[half:, half:] + a2[half:, half:] * square
-    inv00 = factor(k00)
-    u = dot(inv00, k01)
-    inv11 = factor(k11 - dot(u, u, ((0,), (0,))))
-
-    v_and_f = dot(inv_m, jnp.concatenate([first, innovation(0)], axis=1))
-    v, f = v_and_f[:, :members], v_and_f[:, members:]
-    increment = jnp.sum(v * jnp.concatenate([f, f], axis=1), axis=0, keepdims=True)
-    innov2 = innovation(1) - jnp.sum(second * increment, axis=1, keepdims=True)
-    target = dot(second, innov2, ((0,), (0,))) * square
-    y0 = dot(inv00, target[:half, :])
-    below = target[half:, :] - dot(u, y0, ((0,), (0,)))
-
-    q = dot(u, inv00, ((0,), (0,)))
-    inv10 = -dot(inv11, q)
-    y1 = dot(inv11, below)
-    left = g01.T - dot(q, g00)
-    rest = g11 - dot(q, g01) - dot(left, q, ((1,), (1,)))
-    after2 = add_up(dot(inv00, g00) * inv00) + add_up(dot(inv11, rest) * inv11)
-    factor2 = factor1 * blend(after1, after2)
+    f = jnp.sum(inv_m * innovation(0), axis=1, keepdims=True)
+    increment = jnp.sum(v * f, axis=0, keepdims=True)
+    innov2 = column(innovation(1))[:, :1] - jnp.sum(second * increment, axis=1, keepdims=True)
+    target = jnp.sum(second * innov2, axis=0, keepdims=True) * (factor1 * factor1)
+
+    z = jnp.concatenate([first.T, second.T * factor1], axis=1)
+    system = dot(z, z, ((1,), (1,)))
+    inv00 = factor(eye + system[:half, :half])
+    l10 = dot(system[half:, :half], inv00, ((1,), (1,)))
+    inv11 = factor(eye + system[half:, half:] - dot(l10, l10, ((1,), (1,))))
+    inv10 = -dot(inv11, dot(l10, inv00))
+    y0 = jnp.sum(inv00 * target[:, :half], axis=1, keepdims=True)
+    y1 = jnp.sum(inv10 * target[:, :half] + inv11 * target[:, half:], axis=1, keepdims=True)
     increment0 = jnp.sum(y0 * inv00 + y1 * inv10, axis=0, keepdims=True)
     increment1 = jnp.sum(y1 * inv11, axis=0, keepdims=True)
     increment = increment + jnp.concatenate([increment0, increment1], axis=1)
     bottom = jnp.concatenate([inv10, inv11], axis=1)
-
-    inverse = jnp.concatenate([jnp.concatenate([inv00, jnp.zeros_like(inv00)], axis=1), bottom], axis=0)
-    high, low = split(inverse)
-    transform = jnp.concatenate([high, high, low], axis=1)
+    after2 = add_up(dot3(inv00, g00) * inv00) + add_up(dot3(bottom, gram) * bottom)
+    factor2 = factor1 * blend(after1, after2)
+
+    turned = jnp.concatenate(
+        [jnp.concatenate([inv00.T, inv10.T], axis=1), jnp.concatenate([jnp.zeros_like(inv00), inv11.T], axis=1)], axis=0
+    )
+    high, low = split(turned)
+    transform = jnp.concatenate([high, high, low], axis=0)
     step_line = lax.broadcasted_iota(jnp.int32, (LANES, LANES), 0)
     diagonal = step_line == lax.broadcasted_iota(jnp.int32, (LANES, LANES), 1)
 
@@ -292,7 +290,7 @@
         load(i).wait()
         x = x_buf[pl.ds(at, size), :]
         high, low = split(x)
-        moved = dot(jnp.concatenate([high, low, high], axis=1), transform, ((1,), (1,)), None)
+        moved = dot(jnp.concatenate([high, low, high], axis=1), transform, precision=None)
         o_buf[pl.ds(at, size), :] = moved * factor2
         store(i).start()
         steps = jnp.sum(x * increment, axis=1, keepdims=True)

time: 49 us -> 50.8 us (1.037); the launches traced: 48.9 us -> 49.8 us
  waiting for transfers between devices: 18.9 us -> 14.8 us
  starting transfers between devices: 8.53 us -> 11.2 us
  Pallas kernels: 20.3 us -> 22.8 us
    ppermute x6, waiting for transfers between devices: 18.9 us -> 14.8 us  [swap(): return lax.ppermute(value, AXIS, [(i, i ^ mask) for i in range(count)])]
    ppermute x6, starting transfers between devices: 8.53 us -> 11.2 us  [swap(): return lax.ppermute(value, AXIS, [(i, i ^ mask) for i in range(count)])]
    pallas_call x1, Pallas kernels: 15.4 us -> 17.8 us  [update(): pl.pallas_call(functools.partial(update_kernel, chunks), out_shape=(jax.S...]
where the time goes in v7:
time: 50.8 us; the launch traced here: 49.8 us
  Pallas kernels  22.8 us (45%)
  waiting for transfers between devices  14.8 us (29%)
  starting transfers between devices  11.2 us (22%)
  between operations  0.93 us (2%)
    pallas_call x1, Pallas kernels, update(): pl.pallas_call(functools.partial(update_kernel, chunks), out_shape=(jax.S...  17.8 us
    ppermute x6, waiting for transfers between devices, swap(): return lax.ppermute(value, AXIS, [(i, i ^ mask) for i in range(count)])  14.8 us
    ppermute x6, starting transfers between devices, swap(): return lax.ppermute(value, AXIS, [(i, i ^ mask) for i in range(count)])  11.2 us
    pallas_call x1, Pallas kernels, gram_of(): pl.pallas_call(functools.partial(gram_kernel, chunks), out_shape=jax.Shap...  3.38 us
    pallas_call x1, Pallas kernels, gather(): pl.pallas_call(gather_kernel, out_shape=(half, half), in_specs=[spec(pltp...  1.59 us
  transfers between devices with their start and end apart: 6, of which 6 were waited for; matrix products, arithmetic and copies ran while one was open for 0% of the time, Pallas kernels for 0%

profile of v7, /device:TPU:0, one launch (start us, length us, event | category | flops | bytes accessed | tf_op | source)
XLA Modules:
  0.0 49.8 jit_solution(2545297815476046830)
XLA Ops:
  0.6 0.0 copy-start
  0.6 0.0 copy-start.1
  0.7 0.0 copy-start.4
  0.7 0.0 copy-start.3
  0.7 0.0 copy-start.2
  0.7 3.4 %shard_map.77.gram = f32[384,128]{1,0:T(8,128)S(1)} custom-call(f32[4096,256]{1,0:T(8,128)} %x_hbm.5), custom_call_target="tpu_custom_call" | custom-call | flops 1073741824 | bytes 4194304 | tf_op jit(solution)/shard_map/pallas_call | solution.py:332
  4.1 0.0 copy-done
  4.1 0.0 copy-done.1
  4.1 0.0 copy-done.4
  4.1 0.0 copy-done.3
  4.1 0.0 copy-done.2
  4.1 1.6 %shard_map.78 = (f32[448,128]{1,0:T(8,128)S(1)}, f32[448,128]{1,0:T(8,128)S(1)}) custom-call(s32[2]{0:T(128)S(1)} %copy-done.4, s32[2,128]{1,0:T(2,128)S(1)} %copy-done.1, s32[2,128]{1,0:T(2,128)S(1)} %copy-done.1, f32[2,128]{1,0:T(2,128)S(1)} %copy-done.2, f32[2,128]{1,0:T(2,128)S(1)} %copy-done.3, f32[32,128]{1,0:T(8,128)S(1)} %bitcast.3, ...), custom_call_target="tpu_custom_call" | custom-call | tf_op jit(solution)/shard_map/pallas_call | solution.py:346
  5.7 0.5 %collective-permute-start = (f32[448,128]{1,0:T(8,128)S(1)}, f32[448,128]{1,0:T(8,128)S(1)}, u32[]{:S(2)}, u32[]{:S(2)}) collective-permute-start(f32[448,128]{1,0:T(8,128)S(1)} %get-tuple-element.7), channel_id=1, source_target_pairs={{0,1},{1,0},{2,3},{3,2},{4,5},{5,4},{6,7},{7,6},{8,9},{9,8},{10,11... | collective-permute-start | bytes 688136 | tf_op jit(solution)/shard_map/ppermute | solution.py:381
  6.2 1.1 %collective-permute-done = f32[448,128]{1,0:T(8,128)S(1)} collective-permute-done((f32[448,128]{1,0:T(8,128)S(1)}, f32[448,128]{1,0:T(8,128)S(1)}, u32[]{:S(2)}, u32[]{:S(2)}) %collective-permute-start) | collective-permute-done | bytes 229408 | tf_op jit(solution)/shard_map/ppermute | solution.py:381
  7.4 3.0 %collective-permute-start.1 = (f32[224,128]{1,0:T(8,128)S(1)}, f32[224,128]{1,0:T(8,128)S(1)}, u32[]{:S(2)}, u32[]{:S(2)}) collective-permute-start(f32[224,128]{1,0:T(8,128)S(1)} %slice_select_fusion), channel_id=1, source_target_pairs={{0,2},{1,3},{2,0},{3,1},{4,6},{5,7},{6,4},{7,5},{8,10},{9,11},{10,... | collective-permute-start | bytes 344072 | tf_op jit(solution)/shard_map/ppermute | solution.py:381
  10.4 3.4 %collective-permute-done.1 = f32[224,128]{1,0:T(8,128)S(1)} collective-permute-done((f32[224,128]{1,0:T(8,128)S(1)}, f32[224,128]{1,0:T(8,128)S(1)}, u32[]{:S(2)}, u32[]{:S(2)}) %collective-permute-start.1) | collective-permute-done | bytes 114720 | tf_op jit(solution)/shard_map/ppermute | solution.py:381
  13.8 1.9 %collective-permute-start.2 = (f32[224,128]{1,0:T(8,128)S(1)}, f32[224,128]{1,0:T(8,128)S(1)}, u32[]{:S(2)}, u32[]{:S(2)}) collective-permute-start(f32[224,128]{1,0:T(8,128)S(1)} %select_add_fusion), channel_id=1, source_target_pairs={{0,4},{1,5},{2,6},{3,7},{4,0},{5,1},{6,2},{7,3},{8,12},{9,13},{10,... | collective-permute-start | bytes 344072 | tf_op jit(solution)/shard_map/ppermute | solution.py:381
  15.7 3.0 %collective-permute-done.2 = f32[224,128]{1,0:T(8,128)S(1)} collective-permute-done((f32[224,128]{1,0:T(8,128)S(1)}, f32[224,128]{1,0:T(8,128)S(1)}, u32[]{:S(2)}, u32[]{:S(2)}) %collective-permute-start.2) | collective-permute-done | bytes 114720 | tf_op jit(solution)/shard_map/ppermute | solution.py:381
  18.7 3.4 %collective-permute-start.3 = (f32[224,128]{1,0:T(8,128)S(1)}, f32[224,128]{1,0:T(8,128)S(1)}, u32[]{:S(2)}, u32[]{:S(2)}) collective-permute-start(f32[224,128]{1,0:T(8,128)S(1)} %add.14), channel_id=1, source_target_pairs={{0,8},{1,9},{2,10},{3,11},{4,12},{5,13},{6,14},{7,15},{8,0},{9,1},... | collective-permute-start | bytes 344072 | tf_op jit(solution)/shard_map/ppermute | solution.py:381
  22.1 3.0 %collective-permute-done.3 = f32[224,128]{1,0:T(8,128)S(1)} collective-permute-done((f32[224,128]{1,0:T(8,128)S(1)}, f32[224,128]{1,0:T(8,128)S(1)}, u32[]{:S(2)}, u32[]{:S(2)}) %collective-permute-start.3) | collective-permute-done | bytes 114720 | tf_op jit(solution)/shard_map/ppermute | solution.py:381
  25.1 2.4 %collective-permute-start.4 = (f32[224,128]{1,0:T(8,128)S(1)}, f32[224,128]{1,0:T(8,128)S(1)}, u32[]{:S(2)}, u32[]{:S(2)}) collective-permute-start(f32[224,128]{1,0:T(8,128)S(1)} %add.15), channel_id=1, source_target_pairs={{0,2},{1,3},{2,0},{3,1},{4,6},{5,7},{6,4},{7,5},{8,10},{9,11},{10,... | collective-permute-start | bytes 344072 | tf_op jit(solution)/shard_map/ppermute | solution.py:381
  27.5 2.8 %collective-permute-done.4 = f32[224,128]{1,0:T(8,128)S(1)} collective-permute-done((f32[224,128]{1,0:T(8,128)S(1)}, f32[224,128]{1,0:T(8,128)S(1)}, u32[]{:S(2)}, u32[]{:S(2)}) %collective-permute-start.4) | collective-permute-done | bytes 114720 | tf_op jit(solution)/shard_map/ppermute | solution.py:381
  30.3 0.1 collective-permute-start.5
  30.4 1.5 %collective-permute-done.5.other_v = f32[448,128]{1,0:T(8,128)S(1)} collective-permute-done((f32[448,128]{1,0:T(8,128)S(1)}, f32[448,128]{1,0:T(8,128)S(1)}, u32[]{:S(2)}, u32[]{:S(2)}) %collective-permute-start.5) | collective-permute-done | bytes 229408 | tf_op jit(solution)/shard_map/ppermute | solution.py:381
  31.9 17.8 %shard_map.79 = (f32[4096,256]{1,0:T(8,128)}, f32[1,4096]{1,0:T(1,128)}) custom-call(f32[448,128]{1,0:T(8,128)S(1)} %pad_maximum_fusion.mine_v, f32[448,128]{1,0:T(8,128)S(1)} %collective-permute-done.5.other_v, f32[1,4096]{1,0:T(1,128)S(1)} %bitcast.4, f32[4096,256]{1,0:T(8,128)} %x_hbm.5), custom_call_target="tpu_custom_call" | custom-call | tf_op jit(solution)/shard_map/pallas_call | solution.py:363
  (7 shorter events, 0.1 us)
Async XLA Ops:
  0.6 3.4 %copy-start = (f32[4096]{0:T(1024)S(1)}, f32[4096]{0:T(1024)}, u32[]{:S(2)}) copy-start(f32[4096]{0:T(1024)} %param.7) | copy-start | bytes 49156
  0.6 3.4 %copy-start.1 = (s32[2,128]{1,0:T(2,128)S(1)}, s32[2,128]{1,0:T(2,128)}, u32[]{:S(2)}) copy-start(s32[2,128]{1,0:T(2,128)} %rows_v.1) | copy-start | bytes 3076
  0.7 3.4 %copy-start.4 = (s32[2]{0:T(128)S(1)}, s32[2]{0:T(128)}, u32[]{:S(2)}) copy-start(s32[2]{0:T(128)} %owner_s.1) | copy-start | bytes 28
  0.7 3.4 %copy-start.3 = (f32[2,128]{1,0:T(2,128)S(1)}, f32[2,128]{1,0:T(2,128)}, u32[]{:S(2)}) copy-start(f32[2,128]{1,0:T(2,128)} %error_var.1) | copy-start | bytes 3076
  0.7 3.4 %copy-start.2 = (f32[2,128]{1,0:T(2,128)S(1)}, f32[2,128]{1,0:T(2,128)}, u32[]{:S(2)}) copy-start(f32[2,128]{1,0:T(2,128)} %observed.1) | copy-start | bytes 3076
  5.7 1.6 %collective-permute-start = (f32[448,128]{1,0:T(8,128)S(1)}, f32[448,128]{1,0:T(8,128)S(1)}, u32[]{:S(2)}, u32[]{:S(2)}) collective-permute-start(f32[448,128]{1,0:T(8,128)S(1)} %get-tuple-element.7), channel_id=1, source_target_pairs={{0,1},{1,0},{2,3},{3,2},{4,5},{5,4},{6,7},{7,6},{8,9},{9,8},{10,11... | collective-permute-start | bytes 688136 | tf_op jit(solution)/shard_map/ppermute | solution.py:381
  7.4 6.4 %collective-permute-start.1 = (f32[224,128]{1,0:T(8,128)S(1)}, f32[224,128]{1,0:T(8,128)S(1)}, u32[]{:S(2)}, u32[]{:S(2)}) collective-permute-start(f32[224,128]{1,0:T(8,128)S(1)} %slice_select_fusion), channel_id=1, source_target_pairs={{0,2},{1,3},{2,0},{3,1},{4,6},{5,7},{6,4},{7,5},{8,10},{9,11},{10,... | collective-permute-start | bytes 344072 | tf_op jit(solution)/shard_map/ppermute | solution.py:381
  13.8 4.9 %collective-permute-start.2 = (f32[224,128]{1,0:T(8,128)S(1)}, f32[224,128]{1,0:T(8,128)S(1)}, u32[]{:S(2)}, u32[]{:S(2)}) collective-permute-start(f32[224,128]{1,0:T(8,128)S(1)} %select_add_fusion), channel_id=1, source_target_pairs={{0,4},{1,5},{2,6},{3,7},{4,0},{5,1},{6,2},{7,3},{8,12},{9,13},{10,... | collective-permute-start | bytes 344072 | tf_op jit(solution)/shard_map/ppermute | solution.py:381
  18.7 6.4 %collective-permute-start.3 = (f32[224,128]{1,0:T(8,128)S(1)}, f32[224,128]{1,0:T(8,128)S(1)}, u32[]{:S(2)}, u32[]{:S(2)}) collective-permute-start(f32[224,128]{1,0:T(8,128)S(1)} %add.14), channel_id=1, source_target_pairs={{0,8},{1,9},{2,10},{3,11},{4,12},{5,13},{6,14},{7,15},{8,0},{9,1},... | collective-permute-start | bytes 344072 | tf_op jit(solution)/shard_map/ppermute | solution.py:381
  25.1 5.2 %collective-permute-start.4 = (f32[224,128]{1,0:T(8,128)S(1)}, f32[224,128]{1,0:T(8,128)S(1)}, u32[]{:S(2)}, u32[]{:S(2)}) collective-permute-start(f32[224,128]{1,0:T(8,128)S(1)} %add.15), channel_id=1, source_target_pairs={{0,2},{1,3},{2,0},{3,1},{4,6},{5,7},{6,4},{7,5},{8,10},{9,11},{10,... | collective-permute-start | bytes 344072 | tf_op jit(solution)/shard_map/ppermute | solution.py:381
  30.3 1.6 %collective-permute-start.5 = (f32[448,128]{1,0:T(8,128)S(1)}, f32[448,128]{1,0:T(8,128)S(1)}, u32[]{:S(2)}, u32[]{:S(2)}) collective-permute-start(f32[448,128]{1,0:T(8,128)S(1)} %pad_maximum_fusion.mine_v), channel_id=1, source_target_pairs={{0,1},{1,0},{2,3},{3,2},{4,5},{5,4},{6,7},{7,6},{8,9},{9,8},{10,11... | collective-permute-start | bytes 688136 | tf_op jit(solution)/shard_map/ppermute | solution.py:381

commit v8 on v7

--- a/solution.py
+++ b/solution.py
@@ -16,11 +16,12 @@
 SUB = 8
 OBS = 128
 VMEM_LIMIT = 51 * 1024 * 1024
-STEP = 8
+STEP = 16
 
 A0, A1, B0, B1, G00, G01, G11 = range(0, 7 * 128, 128)
-PACKED = 7 * 128
-INNOV = G00 + 64
+PACKED = G11 + 64
+INNOV = G00 + 96
+INNOV_LANES = 32
 
 
 def dot(a, b, dims=((1,), (0,)), precision=HI):
@@ -61,9 +62,13 @@
         total = part if total is None else total + part
     cross = total[:, members:]
     total = total[:, :members] + cross + cross.T
-    out[:half, :] = total[:half, :half]
+    quarter = half // 2
+    out[:quarter, :] = total[:quarter, :half]
+    out[quarter:half, :] = jnp.concatenate(
+        [total[half + quarter :, half + quarter :], total[quarter:half, quarter:half]], axis=1
+    )
     out[half : 2 * half, :] = total[:half, half:]
-    out[2 * half :, :] = total[half:, half:]
+    out[2 * half :, :] = total[half : half + quarter, half:]
 
 
 def gather_kernel(
@@ -97,11 +102,11 @@
         scale = lax.rsqrt(error_var[k : k + 1, :] * (members - 1.0))
         scales.append(column(scale))
         innov = jnp.where(owner_s[k] == me, scale * (observed[k : k + 1, :] - prior), 0.0)
-        innovations += [innov[:, : half // 2], innov[:, half // 2 :]]
+        innovations += [innov[:, j : j + INNOV_LANES] for j in range(0, OBS, INNOV_LANES)]
 
     full[G00:, :] = gram[...]
     for i, innov in enumerate(innovations):
-        full[INNOV + i : INNOV + i + 1, : half // 2] = innov
+        full[INNOV + i : INNOV + i + 1, :INNOV_LANES] = innov
     full[:G00, :] = jnp.zeros((G00, LANES), F32)
     for k, left, right in ((0, A0, A1), (1, B0, B1)):
 
@@ -239,15 +244,21 @@
         return full[at : at + half, :]
 
     def innovation(k):
-        at = INNOV + 2 * k
-        return jnp.concatenate([full[at : at + 1, :quarter], full[at + 1 : at + 2, :quarter]], axis=1)
+        count = OBS // INNOV_LANES
+        at = INNOV + count * k
+        return jnp.concatenate([full[at + j : at + j + 1, :INNOV_LANES] for j in range(count)], axis=1)
 
     first = jnp.concatenate([block(A0), block(A1)], axis=1)
     second = jnp.concatenate([block(B0), block(B1)], axis=1)
-    g00, g01, g11 = block(G00), block(G01), block(G11)
+    g00, g01, top = block(G00), block(G01), full[G11:, :]
     line = lax.broadcasted_iota(jnp.int32, (half, half), 0)
     lane = lax.broadcasted_iota(jnp.int32, (half, half), 1)
-    g00 = jnp.where((line >= quarter) & (lane < quarter), g00.T, g00)
+    last = jnp.concatenate([jnp.zeros((quarter, quarter), F32), g00[quarter:, :quarter]], axis=1)
+    corner = (line >= quarter) & (lane < quarter)
+    g00 = jnp.where(corner, g00.T, g00)
+    g11 = jnp.concatenate([top, last], axis=0)
+    inner = (line >= INNOV - G00) & (lane >= quarter) & (lane < quarter + INNOV_LANES)
+    g11 = jnp.where(corner | inner, g11.T, g11)
     gram = jnp.concatenate(
         [jnp.concatenate([g00, g01], axis=1), jnp.concatenate([g01.T, g11], axis=1)], axis=0
     )
@@ -299,13 +310,8 @@
             part = pl.ds(at + j, LANES)
             mean_out[:, part] = mean_v[:, part] + step
 
-    apply(0, 0)
-
-    def body(i, _):
-        apply(i, pl.multiple_of(i * size, size))
-        return 0
-
-    lax.fori_loop(1, chunks, body, 0)
+    for i in range(chunks):
+        apply(i, i * size)
     for i in range(chunks):
         store(i).wait()
 
@@ -328,7 +334,7 @@
 
 def gram_of(ensemble):
     rows, members = ensemble.shape
-    chunks = 4
+    chunks = 8
     return pl.pallas_call(
         functools.partial(gram_kernel, chunks),
         out_shape=jax.ShapeDtypeStruct((PACKED - G00, LANES), F32),

time: 50.8 us -> 49.4 us (0.972)
  Pallas kernels: 22.8 us -> 22 us
  waiting for transfers between devices: 14.8 us -> 14.2 us
    pallas_call x1, Pallas kernels: 17.8 us -> 16.5 us  [update(): pl.pallas_call(functools.partial(update_kernel, chunks), out_shape=(jax.S...]
    ppermute x6, waiting for transfers between devices: 14.8 us -> 14.2 us  [swap(): return lax.ppermute(value, AXIS, [(i, i ^ mask) for i in range(count)])]
where the time goes in v8:
time: 49.4 us; the launch traced here: 48.5 us
  Pallas kernels  22 us (45%)
  waiting for transfers between devices  14.2 us (29%)
  starting transfers between devices  11.2 us (23%)
  between operations  0.93 us (2%)
    pallas_call x1, Pallas kernels, update(): pl.pallas_call(functools.partial(update_kernel, chunks), out_shape=(jax.S...  16.5 us
    ppermute x6, waiting for transfers between devices, swap(): return lax.ppermute(value, AXIS, [(i, i ^ mask) for i in range(count)])  14.2 us
    ppermute x6, starting transfers between devices, swap(): return lax.ppermute(value, AXIS, [(i, i ^ mask) for i in range(count)])  11.2 us
    pallas_call x1, Pallas kernels, gram_of(): pl.pallas_call(functools.partial(gram_kernel, chunks), out_shape=jax.Shap...  3.87 us
    pallas_call x1, Pallas kernels, gather(): pl.pallas_call(gather_kernel, out_shape=(half, half), in_specs=[spec(pltp...  1.59 us
  transfers between devices with their start and end apart: 6, of which 6 were waited for; matrix products, arithmetic and copies ran while one was open for 0% of the time, Pallas kernels for 0%

profile of v8, /device:TPU:0, one launch (start us, length us, event | category | flops | bytes accessed | tf_op | source)
XLA Modules:
  0.0 48.5 jit_solution(1301786607446040340)
XLA Ops:
  0.6 0.0 copy-start
  0.6 0.0 copy-start.1
  0.7 0.0 copy-start.4
  0.7 0.0 copy-start.3
  0.7 0.0 copy-start.2
  0.7 3.9 %shard_map.77.gram = f32[320,128]{1,0:T(8,128)S(1)} custom-call(f32[4096,256]{1,0:T(8,128)} %x_hbm.5), custom_call_target="tpu_custom_call" | custom-call | flops 1073741824 | bytes 4194304 | tf_op jit(solution)/shard_map/pallas_call | solution.py:338
  4.6 0.0 copy-done
  4.6 0.0 copy-done.1
  4.6 0.0 copy-done.4
  4.6 0.0 copy-done.3
  4.6 0.0 copy-done.2
  4.6 1.6 %shard_map.78 = (f32[416,128]{1,0:T(8,128)S(1)}, f32[416,128]{1,0:T(8,128)S(1)}) custom-call(s32[2]{0:T(128)S(1)} %copy-done.4, s32[2,128]{1,0:T(2,128)S(1)} %copy-done.1, s32[2,128]{1,0:T(2,128)S(1)} %copy-done.1, f32[2,128]{1,0:T(2,128)S(1)} %copy-done.2, f32[2,128]{1,0:T(2,128)S(1)} %copy-done.3, f32[32,128]{1,0:T(8,128)S(1)} %bitcast.3, ...), custom_call_target="tpu_custom_call" | custom-call | tf_op jit(solution)/shard_map/pallas_call | solution.py:352
  6.2 0.5 %collective-permute-start = (f32[416,128]{1,0:T(8,128)S(1)}, f32[416,128]{1,0:T(8,128)S(1)}, u32[]{:S(2)}, u32[]{:S(2)}) collective-permute-start(f32[416,128]{1,0:T(8,128)S(1)} %get-tuple-element.7), channel_id=1, source_target_pairs={{0,1},{1,0},{2,3},{3,2},{4,5},{5,4},{6,7},{7,6},{8,9},{9,8},{10,11... | collective-permute-start | bytes 638984 | tf_op jit(solution)/shard_map/ppermute | solution.py:387
  6.7 1.1 %collective-permute-done = f32[416,128]{1,0:T(8,128)S(1)} collective-permute-done((f32[416,128]{1,0:T(8,128)S(1)}, f32[416,128]{1,0:T(8,128)S(1)}, u32[]{:S(2)}, u32[]{:S(2)}) %collective-permute-start) | collective-permute-done | bytes 213024 | tf_op jit(solution)/shard_map/ppermute | solution.py:387
  7.9 3.0 %collective-permute-start.1 = (f32[208,128]{1,0:T(8,128)S(1)}, f32[208,128]{1,0:T(8,128)S(1)}, u32[]{:S(2)}, u32[]{:S(2)}) collective-permute-start(f32[208,128]{1,0:T(8,128)S(1)} %slice_select_fusion), channel_id=1, source_target_pairs={{0,2},{1,3},{2,0},{3,1},{4,6},{5,7},{6,4},{7,5},{8,10},{9,11},{10,... | collective-permute-start | bytes 319496 | tf_op jit(solution)/shard_map/ppermute | solution.py:387
  10.8 3.3 %collective-permute-done.1 = f32[208,128]{1,0:T(8,128)S(1)} collective-permute-done((f32[208,128]{1,0:T(8,128)S(1)}, f32[208,128]{1,0:T(8,128)S(1)}, u32[]{:S(2)}, u32[]{:S(2)}) %collective-permute-start.1) | collective-permute-done | bytes 106528 | tf_op jit(solution)/shard_map/ppermute | solution.py:387
  14.1 2.3 %collective-permute-start.2 = (f32[208,128]{1,0:T(8,128)S(1)}, f32[208,128]{1,0:T(8,128)S(1)}, u32[]{:S(2)}, u32[]{:S(2)}) collective-permute-start(f32[208,128]{1,0:T(8,128)S(1)} %select_add_fusion), channel_id=1, source_target_pairs={{0,4},{1,5},{2,6},{3,7},{4,0},{5,1},{6,2},{7,3},{8,12},{9,13},{10,... | collective-permute-start | bytes 319496 | tf_op jit(solution)/shard_map/ppermute | solution.py:387
  16.5 2.7 %collective-permute-done.2 = f32[208,128]{1,0:T(8,128)S(1)} collective-permute-done((f32[208,128]{1,0:T(8,128)S(1)}, f32[208,128]{1,0:T(8,128)S(1)}, u32[]{:S(2)}, u32[]{:S(2)}) %collective-permute-start.2) | collective-permute-done | bytes 106528 | tf_op jit(solution)/shard_map/ppermute | solution.py:387
  19.2 2.8 %collective-permute-start.3 = (f32[208,128]{1,0:T(8,128)S(1)}, f32[208,128]{1,0:T(8,128)S(1)}, u32[]{:S(2)}, u32[]{:S(2)}) collective-permute-start(f32[208,128]{1,0:T(8,128)S(1)} %add.14), channel_id=1, source_target_pairs={{0,8},{1,9},{2,10},{3,11},{4,12},{5,13},{6,14},{7,15},{8,0},{9,1},... | collective-permute-start | bytes 319496 | tf_op jit(solution)/shard_map/ppermute | solution.py:387
  22.0 3.0 %collective-permute-done.3 = f32[208,128]{1,0:T(8,128)S(1)} collective-permute-done((f32[208,128]{1,0:T(8,128)S(1)}, f32[208,128]{1,0:T(8,128)S(1)}, u32[]{:S(2)}, u32[]{:S(2)}) %collective-permute-start.3) | collective-permute-done | bytes 106528 | tf_op jit(solution)/shard_map/ppermute | solution.py:387
  25.0 2.6 %collective-permute-start.4 = (f32[208,128]{1,0:T(8,128)S(1)}, f32[208,128]{1,0:T(8,128)S(1)}, u32[]{:S(2)}, u32[]{:S(2)}) collective-permute-start(f32[208,128]{1,0:T(8,128)S(1)} %add.15), channel_id=1, source_target_pairs={{0,2},{1,3},{2,0},{3,1},{4,6},{5,7},{6,4},{7,5},{8,10},{9,11},{10,... | collective-permute-start | bytes 319496 | tf_op jit(solution)/shard_map/ppermute | solution.py:387
  27.5 2.7 %collective-permute-done.4 = f32[208,128]{1,0:T(8,128)S(1)} collective-permute-done((f32[208,128]{1,0:T(8,128)S(1)}, f32[208,128]{1,0:T(8,128)S(1)}, u32[]{:S(2)}, u32[]{:S(2)}) %collective-permute-start.4) | collective-permute-done | bytes 106528 | tf_op jit(solution)/shard_map/ppermute | solution.py:387
  30.3 0.1 collective-permute-start.5
  30.4 1.5 %collective-permute-done.5.other_v = f32[416,128]{1,0:T(8,128)S(1)} collective-permute-done((f32[416,128]{1,0:T(8,128)S(1)}, f32[416,128]{1,0:T(8,128)S(1)}, u32[]{:S(2)}, u32[]{:S(2)}) %collective-permute-start.5) | collective-permute-done | bytes 213024 | tf_op jit(solution)/shard_map/ppermute | solution.py:387
  31.8 16.5 %shard_map.79 = (f32[4096,256]{1,0:T(8,128)}, f32[1,4096]{1,0:T(1,128)}) custom-call(f32[416,128]{1,0:T(8,128)S(1)} %pad_maximum_fusion.mine_v, f32[416,128]{1,0:T(8,128)S(1)} %collective-permute-done.5.other_v, f32[1,4096]{1,0:T(1,128)S(1)} %bitcast.4, f32[4096,256]{1,0:T(8,128)} %x_hbm.5), custom_call_target="tpu_custom_call" | custom-call | tf_op jit(solution)/shard_map/pallas_call | solution.py:369
  (7 shorter events, 0.1 us)
Async XLA Ops:
  0.6 3.9 %copy-start = (f32[4096]{0:T(1024)S(1)}, f32[4096]{0:T(1024)}, u32[]{:S(2)}) copy-start(f32[4096]{0:T(1024)} %param.7) | copy-start | bytes 49156
  0.6 3.9 %copy-start.1 = (s32[2,128]{1,0:T(2,128)S(1)}, s32[2,128]{1,0:T(2,128)}, u32[]{:S(2)}) copy-start(s32[2,128]{1,0:T(2,128)} %rows_v.1) | copy-start | bytes 3076
  0.7 3.9 %copy-start.4 = (s32[2]{0:T(128)S(1)}, s32[2]{0:T(128)}, u32[]{:S(2)}) copy-start(s32[2]{0:T(128)} %owner_s.1) | copy-start | bytes 28
  0.7 3.9 %copy-start.3 = (f32[2,128]{1,0:T(2,128)S(1)}, f32[2,128]{1,0:T(2,128)}, u32[]{:S(2)}) copy-start(f32[2,128]{1,0:T(2,128)} %error_var.1) | copy-start | bytes 3076
  0.7 3.9 %copy-start.2 = (f32[2,128]{1,0:T(2,128)S(1)}, f32[2,128]{1,0:T(2,128)}, u32[]{:S(2)}) copy-start(f32[2,128]{1,0:T(2,128)} %observed.1) | copy-start | bytes 3076
  6.2 1.6 %collective-permute-start = (f32[416,128]{1,0:T(8,128)S(1)}, f32[416,128]{1,0:T(8,128)S(1)}, u32[]{:S(2)}, u32[]{:S(2)}) collective-permute-start(f32[416,128]{1,0:T(8,128)S(1)} %get-tuple-element.7), channel_id=1, source_target_pairs={{0,1},{1,0},{2,3},{3,2},{4,5},{5,4},{6,7},{7,6},{8,9},{9,8},{10,11... | collective-permute-start | bytes 638984 | tf_op jit(solution)/shard_map/ppermute | solution.py:387
  7.9 6.2 %collective-permute-start.1 = (f32[208,128]{1,0:T(8,128)S(1)}, f32[208,128]{1,0:T(8,128)S(1)}, u32[]{:S(2)}, u32[]{:S(2)}) collective-permute-start(f32[208,128]{1,0:T(8,128)S(1)} %slice_select_fusion), channel_id=1, source_target_pairs={{0,2},{1,3},{2,0},{3,1},{4,6},{5,7},{6,4},{7,5},{8,10},{9,11},{10,... | collective-permute-start | bytes 319496 | tf_op jit(solution)/shard_map/ppermute | solution.py:387
  14.1 5.0 %collective-permute-start.2 = (f32[208,128]{1,0:T(8,128)S(1)}, f32[208,128]{1,0:T(8,128)S(1)}, u32[]{:S(2)}, u32[]{:S(2)}) collective-permute-start(f32[208,128]{1,0:T(8,128)S(1)} %select_add_fusion), channel_id=1, source_target_pairs={{0,4},{1,5},{2,6},{3,7},{4,0},{5,1},{6,2},{7,3},{8,12},{9,13},{10,... | collective-permute-start | bytes 319496 | tf_op jit(solution)/shard_map/ppermute | solution.py:387
  19.2 5.8 %collective-permute-start.3 = (f32[208,128]{1,0:T(8,128)S(1)}, f32[208,128]{1,0:T(8,128)S(1)}, u32[]{:S(2)}, u32[]{:S(2)}) collective-permute-start(f32[208,128]{1,0:T(8,128)S(1)} %add.14), channel_id=1, source_target_pairs={{0,8},{1,9},{2,10},{3,11},{4,12},{5,13},{6,14},{7,15},{8,0},{9,1},... | collective-permute-start | bytes 319496 | tf_op jit(solution)/shard_map/ppermute | solution.py:387
  25.0 5.2 %collective-permute-start.4 = (f32[208,128]{1,0:T(8,128)S(1)}, f32[208,128]{1,0:T(8,128)S(1)}, u32[]{:S(2)}, u32[]{:S(2)}) collective-permute-start(f32[208,128]{1,0:T(8,128)S(1)} %add.15), channel_id=1, source_target_pairs={{0,2},{1,3},{2,0},{3,1},{4,6},{5,7},{6,4},{7,5},{8,10},{9,11},{10,... | collective-permute-start | bytes 319496 | tf_op jit(solution)/shard_map/ppermute | solution.py:387
  30.3 1.5 %collective-permute-start.5 = (f32[416,128]{1,0:T(8,128)S(1)}, f32[416,128]{1,0:T(8,128)S(1)}, u32[]{:S(2)}, u32[]{:S(2)}) collective-permute-start(f32[416,128]{1,0:T(8,128)S(1)} %pad_maximum_fusion.mine_v), channel_id=1, source_target_pairs={{0,1},{1,0},{2,3},{3,2},{4,5},{5,4},{6,7},{7,6},{8,9},{9,8},{10,11... | collective-permute-start | bytes 638984 | tf_op jit(solution)/shard_map/ppermute | solution.py:387

commit v9 on v8

--- a/solution.py
+++ b/solution.py
@@ -246,7 +246,7 @@
     def innovation(k):
         count = OBS // INNOV_LANES
         at = INNOV + count * k
-        return jnp.concatenate([full[at + j : at + j + 1, :INNOV_LANES] for j in range(count)], axis=1)
+        return column(jnp.concatenate([full[at + j : at + j + 1, :INNOV_LANES] for j in range(count)], axis=1))
 
     first = jnp.concatenate([block(A0), block(A1)], axis=1)
     second = jnp.concatenate([block(B0), block(B1)], axis=1)
@@ -265,29 +265,33 @@
     eye = identity(half)
 
     inv_m = factor(eye + dot(first, first, ((1,), (1,))))
-    v = dot(inv_m, first)
+    v_and_f = dot(inv_m, jnp.concatenate([first, innovation(0)], axis=1))
+    v, f = v_and_f[:, :members], v_and_f[:, members:]
     before = add_up(eye * (g00 + g11))
     after1 = before - add_up(dot3(v, gram) * v)
     factor1 = blend(before, after1)
-    f = jnp.sum(inv_m * innovation(0), axis=1, keepdims=True)
-    increment = jnp.sum(v * f, axis=0, keepdims=True)
-    innov2 = column(innovation(1))[:, :1] - jnp.sum(second * increment, axis=1, keepdims=True)
-    target = jnp.sum(second * innov2, axis=0, keepdims=True) * (factor1 * factor1)
-
-    z = jnp.concatenate([first.T, second.T * factor1], axis=1)
-    system = dot(z, z, ((1,), (1,)))
-    inv00 = factor(eye + system[:half, :half])
-    l10 = dot(system[half:, :half], inv00, ((1,), (1,)))
-    inv11 = factor(eye + system[half:, half:] - dot(l10, l10, ((1,), (1,))))
-    inv10 = -dot(inv11, dot(l10, inv00))
-    y0 = jnp.sum(inv00 * target[:, :half], axis=1, keepdims=True)
-    y1 = jnp.sum(inv10 * target[:, :half] + inv11 * target[:, half:], axis=1, keepdims=True)
+    increment = jnp.sum(v * jnp.concatenate([f, f], axis=1), axis=0, keepdims=True)
+    innov2 = innovation(1) - jnp.sum(second * increment, axis=1, keepdims=True)
+
+    a1 = dot(first, first, ((0,), (0,)))
+    a2 = dot(second, jnp.concatenate([second, innov2], axis=1), ((0,), (0,)))
+    square = factor1 * factor1
+    k00 = eye + a1[:half, :half] + a2[:half, :half] * square
+    k01 = a1[:half, half:] + a2[:half, half:members] * square
+    k11 = eye + a1[half:, half:] + a2[half:, half:members] * square
+    inv00 = factor(k00)
+    u = dot(inv00, k01)
+    inv11 = factor(k11 - dot(u, u, ((0,), (0,))))
+    inv10 = -dot(inv11, dot(u, inv00, ((0,), (0,))))
+    y0 = dot(inv00, a2[:half, members:] * square)
+    y1 = dot(inv11, a2[half:, members:] * square - dot(u, y0, ((0,), (0,))))
+    bottom = jnp.concatenate([inv10, inv11], axis=1)
+    top_trace = add_up(dot3(inv00, g00) * inv00)
+    after2 = top_trace + add_up(dot3(bottom, gram) * bottom)
+    factor2 = factor1 * blend(after1, after2)
     increment0 = jnp.sum(y0 * inv00 + y1 * inv10, axis=0, keepdims=True)
     increment1 = jnp.sum(y1 * inv11, axis=0, keepdims=True)
     increment = increment + jnp.concatenate([increment0, increment1], axis=1)
-    bottom = jnp.concatenate([inv10, inv11], axis=1)
-    after2 = add_up(dot3(inv00, g00) * inv00) + add_up(dot3(bottom, gram) * bottom)
-    factor2 = factor1 * blend(after1, after2)
 
     turned = jnp.concatenate(
         [jnp.concatenate([inv00.T, inv10.T], axis=1), jnp.concatenate([jnp.zeros_like(inv00), inv11.T], axis=1)], axis=0
@@ -310,8 +314,13 @@
             part = pl.ds(at + j, LANES)
             mean_out[:, part] = mean_v[:, part] + step
 
-    for i in range(chunks):
-        apply(i, i * size)
+    apply(0, 0)
+
+    def body(i, _):
+        apply(i, pl.multiple_of(i * size, size))
+        return 0
+
+    lax.fori_loop(1, chunks, body, 0)
     for i in range(chunks):
         store(i).wait()
 
@@ -334,7 +343,7 @@
 
 def gram_of(ensemble):
     rows, members = ensemble.shape
-    chunks = 8
+    chunks = 4
     return pl.pallas_call(
         functools.partial(gram_kernel, chunks),
         out_shape=jax.ShapeDtypeStruct((PACKED - G00, LANES), F32),

time: 49.4 us -> 47.4 us (0.960); the launches traced: 48.5 us -> 47.1 us
  waiting for transfers between devices: 14.2 us -> 17.1 us
  starting transfers between devices: 11.2 us -> 8.96 us
  Pallas kernels: 22 us -> 19.9 us
    ppermute x6, waiting for transfers between devices: 14.2 us -> 17.1 us  [swap(): return lax.ppermute(value, AXIS, [(i, i ^ mask) for i in range(count)])]
    ppermute x6, starting transfers between devices: 11.2 us -> 8.96 us  [swap(): return lax.ppermute(value, AXIS, [(i, i ^ mask) for i in range(count)])]
    pallas_call x1, Pallas kernels: 16.5 us -> 14.9 us  [update(): pl.pallas_call(functools.partial(update_kernel, chunks), out_shape=(jax.S...]
where the time goes in v9:
time: 47.4 us; the launch traced here: 47.1 us
  Pallas kernels  19.9 us (42%)
  waiting for transfers between devices  17.1 us (36%)
  starting transfers between devices  8.96 us (19%)
  between operations  0.93 us (2%)
    ppermute x6, waiting for transfers between devices, swap(): return lax.ppermute(value, AXIS, [(i, i ^ mask) for i in range(count)])  17.1 us
    pallas_call x1, Pallas kernels, update(): pl.pallas_call(functools.partial(update_kernel, chunks), out_shape=(jax.S...  14.9 us
    ppermute x6, starting transfers between devices, swap(): return lax.ppermute(value, AXIS, [(i, i ^ mask) for i in range(count)])  8.96 us
    pallas_call x1, Pallas kernels, gram_of(): pl.pallas_call(functools.partial(gram_kernel, chunks), out_shape=jax.Shap...  3.45 us
    pallas_call x1, Pallas kernels, gather(): pl.pallas_call(gather_kernel, out_shape=(half, half), in_specs=[spec(pltp...  1.59 us
  transfers between devices with their start and end apart: 6, of which 6 were waited for; matrix products, arithmetic and copies ran while one was open for 0% of the time, Pallas kernels for 0%

profile of v9, /device:TPU:0, one launch (start us, length us, event | category | flops | bytes accessed | tf_op | source)
XLA Modules:
  0.0 47.1 jit_solution(14363077546566263762)
XLA Ops:
  0.6 0.0 copy-start
  0.6 0.0 copy-start.1
  0.7 0.0 copy-start.4
  0.7 0.0 copy-start.3
  0.7 0.0 copy-start.2
  0.7 3.4 %shard_map.77.gram = f32[320,128]{1,0:T(8,128)S(1)} custom-call(f32[4096,256]{1,0:T(8,128)} %x_hbm.5), custom_call_target="tpu_custom_call" | custom-call | flops 1073741824 | bytes 4194304 | tf_op jit(solution)/shard_map/pallas_call | solution.py:347
  4.1 0.0 copy-done
  4.1 0.0 copy-done.1
  4.2 0.0 copy-done.4
  4.2 0.0 copy-done.3
  4.2 0.0 copy-done.2
  4.2 1.6 %shard_map.78 = (f32[416,128]{1,0:T(8,128)S(1)}, f32[416,128]{1,0:T(8,128)S(1)}) custom-call(s32[2]{0:T(128)S(1)} %copy-done.4, s32[2,128]{1,0:T(2,128)S(1)} %copy-done.1, s32[2,128]{1,0:T(2,128)S(1)} %copy-done.1, f32[2,128]{1,0:T(2,128)S(1)} %copy-done.2, f32[2,128]{1,0:T(2,128)S(1)} %copy-done.3, f32[32,128]{1,0:T(8,128)S(1)} %bitcast.3, ...), custom_call_target="tpu_custom_call" | custom-call | tf_op jit(solution)/shard_map/pallas_call | solution.py:361
  5.8 0.5 %collective-permute-start = (f32[416,128]{1,0:T(8,128)S(1)}, f32[416,128]{1,0:T(8,128)S(1)}, u32[]{:S(2)}, u32[]{:S(2)}) collective-permute-start(f32[416,128]{1,0:T(8,128)S(1)} %get-tuple-element.7), channel_id=1, source_target_pairs={{0,1},{1,0},{2,3},{3,2},{4,5},{5,4},{6,7},{7,6},{8,9},{9,8},{10,11... | collective-permute-start | bytes 638984 | tf_op jit(solution)/shard_map/ppermute | solution.py:396
  6.3 1.1 %collective-permute-done = f32[416,128]{1,0:T(8,128)S(1)} collective-permute-done((f32[416,128]{1,0:T(8,128)S(1)}, f32[416,128]{1,0:T(8,128)S(1)}, u32[]{:S(2)}, u32[]{:S(2)}) %collective-permute-start) | collective-permute-done | bytes 213024 | tf_op jit(solution)/shard_map/ppermute | solution.py:396
  7.4 3.0 %collective-permute-start.1 = (f32[208,128]{1,0:T(8,128)S(1)}, f32[208,128]{1,0:T(8,128)S(1)}, u32[]{:S(2)}, u32[]{:S(2)}) collective-permute-start(f32[208,128]{1,0:T(8,128)S(1)} %slice_select_fusion), channel_id=1, source_target_pairs={{0,2},{1,3},{2,0},{3,1},{4,6},{5,7},{6,4},{7,5},{8,10},{9,11},{10,... | collective-permute-start | bytes 319496 | tf_op jit(solution)/shard_map/ppermute | solution.py:396
  10.4 3.3 %collective-permute-done.1 = f32[208,128]{1,0:T(8,128)S(1)} collective-permute-done((f32[208,128]{1,0:T(8,128)S(1)}, f32[208,128]{1,0:T(8,128)S(1)}, u32[]{:S(2)}, u32[]{:S(2)}) %collective-permute-start.1) | collective-permute-done | bytes 106528 | tf_op jit(solution)/shard_map/ppermute | solution.py:396
  13.7 1.9 %collective-permute-start.2 = (f32[208,128]{1,0:T(8,128)S(1)}, f32[208,128]{1,0:T(8,128)S(1)}, u32[]{:S(2)}, u32[]{:S(2)}) collective-permute-start(f32[208,128]{1,0:T(8,128)S(1)} %select_add_fusion), channel_id=1, source_target_pairs={{0,4},{1,5},{2,6},{3,7},{4,0},{5,1},{6,2},{7,3},{8,12},{9,13},{10,... | collective-permute-start | bytes 319496 | tf_op jit(solution)/shard_map/ppermute | solution.py:396
  15.6 2.9 %collective-permute-done.2 = f32[208,128]{1,0:T(8,128)S(1)} collective-permute-done((f32[208,128]{1,0:T(8,128)S(1)}, f32[208,128]{1,0:T(8,128)S(1)}, u32[]{:S(2)}, u32[]{:S(2)}) %collective-permute-start.2) | collective-permute-done | bytes 106528 | tf_op jit(solution)/shard_map/ppermute | solution.py:396
  18.5 3.1 %collective-permute-start.3 = (f32[208,128]{1,0:T(8,128)S(1)}, f32[208,128]{1,0:T(8,128)S(1)}, u32[]{:S(2)}, u32[]{:S(2)}) collective-permute-start(f32[208,128]{1,0:T(8,128)S(1)} %add.14), channel_id=1, source_target_pairs={{0,8},{1,9},{2,10},{3,11},{4,12},{5,13},{6,14},{7,15},{8,0},{9,1},... | collective-permute-start | bytes 319496 | tf_op jit(solution)/shard_map/ppermute | solution.py:396
  21.6 4.1 %collective-permute-done.3 = f32[208,128]{1,0:T(8,128)S(1)} collective-permute-done((f32[208,128]{1,0:T(8,128)S(1)}, f32[208,128]{1,0:T(8,128)S(1)}, u32[]{:S(2)}, u32[]{:S(2)}) %collective-permute-start.3) | collective-permute-done | bytes 106528 | tf_op jit(solution)/shard_map/ppermute | solution.py:396
  25.7 0.4 collective-permute-start.4
  26.2 4.3 %collective-permute-done.4 = f32[208,128]{1,0:T(8,128)S(1)} collective-permute-done((f32[208,128]{1,0:T(8,128)S(1)}, f32[208,128]{1,0:T(8,128)S(1)}, u32[]{:S(2)}, u32[]{:S(2)}) %collective-permute-start.4) | collective-permute-done | bytes 106528 | tf_op jit(solution)/shard_map/ppermute | solution.py:396
  30.5 0.1 collective-permute-start.5
  30.6 1.5 %collective-permute-done.5.other_v = f32[416,128]{1,0:T(8,128)S(1)} collective-permute-done((f32[416,128]{1,0:T(8,128)S(1)}, f32[416,128]{1,0:T(8,128)S(1)}, u32[]{:S(2)}, u32[]{:S(2)}) %collective-permute-start.5) | collective-permute-done | bytes 213024 | tf_op jit(solution)/shard_map/ppermute | solution.py:396
  32.1 14.9 %shard_map.79 = (f32[4096,256]{1,0:T(8,128)}, f32[1,4096]{1,0:T(1,128)}) custom-call(f32[416,128]{1,0:T(8,128)S(1)} %pad_maximum_fusion.mine_v, f32[416,128]{1,0:T(8,128)S(1)} %collective-permute-done.5.other_v, f32[1,4096]{1,0:T(1,128)S(1)} %bitcast.4, f32[4096,256]{1,0:T(8,128)} %x_hbm.5), custom_call_target="tpu_custom_call" | custom-call | tf_op jit(solution)/shard_map/pallas_call | solution.py:378
  (7 shorter events, 0.1 us)
Async XLA Ops:
  0.6 3.5 %copy-start = (f32[4096]{0:T(1024)S(1)}, f32[4096]{0:T(1024)}, u32[]{:S(2)}) copy-start(f32[4096]{0:T(1024)} %param.7) | copy-start | bytes 49156
  0.6 3.5 %copy-start.1 = (s32[2,128]{1,0:T(2,128)S(1)}, s32[2,128]{1,0:T(2,128)}, u32[]{:S(2)}) copy-start(s32[2,128]{1,0:T(2,128)} %rows_v.1) | copy-start | bytes 3076
  0.7 3.5 %copy-start.4 = (s32[2]{0:T(128)S(1)}, s32[2]{0:T(128)}, u32[]{:S(2)}) copy-start(s32[2]{0:T(128)} %owner_s.1) | copy-start | bytes 28
  0.7 3.5 %copy-start.3 = (f32[2,128]{1,0:T(2,128)S(1)}, f32[2,128]{1,0:T(2,128)}, u32[]{:S(2)}) copy-start(f32[2,128]{1,0:T(2,128)} %error_var.1) | copy-start | bytes 3076
  0.7 3.5 %copy-start.2 = (f32[2,128]{1,0:T(2,128)S(1)}, f32[2,128]{1,0:T(2,128)}, u32[]{:S(2)}) copy-start(f32[2,128]{1,0:T(2,128)} %observed.1) | copy-start | bytes 3076
  5.8 1.6 %collective-permute-start = (f32[416,128]{1,0:T(8,128)S(1)}, f32[416,128]{1,0:T(8,128)S(1)}, u32[]{:S(2)}, u32[]{:S(2)}) collective-permute-start(f32[416,128]{1,0:T(8,128)S(1)} %get-tuple-element.7), channel_id=1, source_target_pairs={{0,1},{1,0},{2,3},{3,2},{4,5},{5,4},{6,7},{7,6},{8,9},{9,8},{10,11... | collective-permute-start | bytes 638984 | tf_op jit(solution)/shard_map/ppermute | solution.py:396
  7.4 6.2 %collective-permute-start.1 = (f32[208,128]{1,0:T(8,128)S(1)}, f32[208,128]{1,0:T(8,128)S(1)}, u32[]{:S(2)}, u32[]{:S(2)}) collective-permute-start(f32[208,128]{1,0:T(8,128)S(1)} %slice_select_fusion), channel_id=1, source_target_pairs={{0,2},{1,3},{2,0},{3,1},{4,6},{5,7},{6,4},{7,5},{8,10},{9,11},{10,... | collective-permute-start | bytes 319496 | tf_op jit(solution)/shard_map/ppermute | solution.py:396
  13.7 4.8 %collective-permute-start.2 = (f32[208,128]{1,0:T(8,128)S(1)}, f32[208,128]{1,0:T(8,128)S(1)}, u32[]{:S(2)}, u32[]{:S(2)}) collective-permute-start(f32[208,128]{1,0:T(8,128)S(1)} %select_add_fusion), channel_id=1, source_target_pairs={{0,4},{1,5},{2,6},{3,7},{4,0},{5,1},{6,2},{7,3},{8,12},{9,13},{10,... | collective-permute-start | bytes 319496 | tf_op jit(solution)/shard_map/ppermute | solution.py:396
  18.5 7.2 %collective-permute-start.3 = (f32[208,128]{1,0:T(8,128)S(1)}, f32[208,128]{1,0:T(8,128)S(1)}, u32[]{:S(2)}, u32[]{:S(2)}) collective-permute-start(f32[208,128]{1,0:T(8,128)S(1)} %add.14), channel_id=1, source_target_pairs={{0,8},{1,9},{2,10},{3,11},{4,12},{5,13},{6,14},{7,15},{8,0},{9,1},... | collective-permute-start | bytes 319496 | tf_op jit(solution)/shard_map/ppermute | solution.py:396
  25.7 4.8 %collective-permute-start.4 = (f32[208,128]{1,0:T(8,128)S(1)}, f32[208,128]{1,0:T(8,128)S(1)}, u32[]{:S(2)}, u32[]{:S(2)}) collective-permute-start(f32[208,128]{1,0:T(8,128)S(1)} %add.15), channel_id=1, source_target_pairs={{0,2},{1,3},{2,0},{3,1},{4,6},{5,7},{6,4},{7,5},{8,10},{9,11},{10,... | collective-permute-start | bytes 319496 | tf_op jit(solution)/shard_map/ppermute | solution.py:396
  30.5 1.5 %collective-permute-start.5 = (f32[416,128]{1,0:T(8,128)S(1)}, f32[416,128]{1,0:T(8,128)S(1)}, u32[]{:S(2)}, u32[]{:S(2)}) collective-permute-start(f32[416,128]{1,0:T(8,128)S(1)} %pad_maximum_fusion.mine_v), channel_id=1, source_target_pairs={{0,1},{1,0},{2,3},{3,2},{4,5},{5,4},{6,7},{7,6},{8,9},{9,8},{10,11... | collective-permute-start | bytes 638984 | tf_op jit(solution)/shard_map/ppermute | solution.py:396

commit v10 on v9

--- a/solution.py
+++ b/solution.py
@@ -22,6 +22,7 @@
 PACKED = G11 + 64
 INNOV = G00 + 96
 INNOV_LANES = 32
+EVEN_ROWS = 256
 
 
 def dot(a, b, dims=((1,), (0,)), precision=HI):
@@ -72,7 +73,7 @@
 
 
 def gather_kernel(
-    owner_s, rows_s, rows_v, observed, error_var, mean_v, gram, x_hbm, keep, send, full, picked, sem
+    owner_s, rows_s, rows_v, observed, error_var, mean_v, gram, x_hbm, even, odd, full, picked, sem
 ):
     me = lax.axis_index(AXIS)
     members = picked.shape[2]
@@ -116,10 +117,8 @@
             full[left : left + OBS, :] = picked[k, :, :half] * scales[k]
             full[right : right + OBS, :] = picked[k, :, half:] * scales[k]
 
-    mine = me & 1
-    span = PACKED // 2
-    keep[...] = full[pl.ds(pl.multiple_of(mine * span, SUB), span), :]
-    send[...] = full[pl.ds(pl.multiple_of((1 - mine) * span, SUB), span), :]
+    even[...] = full[:EVEN_ROWS, :]
+    odd[...] = full[EVEN_ROWS:, :]
 
 
 def tree(terms):
@@ -223,7 +222,7 @@
 
 
 def update_kernel(
-    chunks, mine_v, other_v, mean_v, x_hbm, out_hbm, mean_out, full, x_buf, o_buf, in_sem, out_sem
+    chunks, even_mine, even_got, odd_mine, odd_got, mean_v, x_hbm, out_hbm, mean_out, full, x_buf, o_buf, in_sem, out_sem
 ):
     members = x_buf.shape[1]
     size = x_buf.shape[0] // chunks
@@ -232,10 +231,9 @@
     for i in range(chunks):
         load(i).start()
 
-    mine = lax.axis_index(AXIS) & 1
-    span = PACKED // 2
-    full[pl.ds(pl.multiple_of(mine * span, SUB), span), :] = mine_v[...]
-    full[pl.ds(pl.multiple_of((1 - mine) * span, SUB), span), :] = other_v[...]
+    is_odd = (lax.axis_index(AXIS) & 1) == 1
+    full[:EVEN_ROWS, :] = jnp.where(is_odd, even_got[...], even_mine[...])
+    full[EVEN_ROWS:, :] = jnp.where(is_odd, odd_mine[...], odd_got[...])
 
     half = members // 2
     quarter = half // 2
@@ -357,10 +355,12 @@
 
 def gather(ensemble, mean_state, observed, error_var, owner, obs_rows, gram):
     members = ensemble.shape[1]
-    half = jax.ShapeDtypeStruct((PACKED // 2, LANES), F32)
     return pl.pallas_call(
         gather_kernel,
-        out_shape=(half, half),
+        out_shape=(
+            jax.ShapeDtypeStruct((EVEN_ROWS, LANES), F32),
+            jax.ShapeDtypeStruct((PACKED - EVEN_ROWS, LANES), F32),
+        ),
         in_specs=[spec(pltpu.SMEM), spec(pltpu.SMEM)] + [spec(pltpu.VMEM)] * 5 + [spec(pltpu.HBM)],
         out_specs=[spec(pltpu.VMEM)] * 2,
         scratch_shapes=[
@@ -378,7 +378,7 @@
     out, mean = pl.pallas_call(
         functools.partial(update_kernel, chunks),
         out_shape=(jax.ShapeDtypeStruct((rows, members), F32), jax.ShapeDtypeStruct((1, rows), F32)),
-        in_specs=[spec(pltpu.VMEM)] * 3 + [spec(pltpu.HBM)],
+        in_specs=[spec(pltpu.VMEM)] * 5 + [spec(pltpu.HBM)],
         out_specs=(spec(pltpu.HBM), spec(pltpu.VMEM)),
         scratch_shapes=[
             pltpu.VMEM((PACKED, LANES), F32),
@@ -392,28 +392,30 @@
     return out, mean.reshape(rows)
 
 
-def swap(value, count, mask):
-    return lax.ppermute(value, AXIS, [(i, i ^ mask) for i in range(count)])
-
-
-def total(keep, send, count):
-    odd = ((lax.axis_index(AXIS) >> 1) & 1) == 1
-    value = keep + swap(send, count, 1)
+def swap(value, senders, mask):
+    return lax.ppermute(value, AXIS, [(i, i ^ mask) for i in senders])
+
+
+def total(value, count, core):
+    mine = range(core, count, 2)
+    upper = ((lax.axis_index(AXIS) >> 1) & 1) == 1
     low, high = jnp.split(value, 2, axis=0)
-    value = jnp.where(odd, high, low) + swap(jnp.where(odd, low, high), count, 2)
+    value = jnp.where(upper, high, low) + swap(jnp.where(upper, low, high), mine, 2)
     mask = 4
     while mask < count:
-        value = value + swap(value, count, mask)
+        value = value + swap(value, mine, mask)
         mask *= 2
-    got = swap(value, count, 2)
-    value = jnp.concatenate([jnp.where(odd, got, value), jnp.where(odd, value, got)], axis=0)
-    return value, swap(value, count, 1)
+    got = swap(value, mine, 2)
+    value = jnp.concatenate([jnp.where(upper, got, value), jnp.where(upper, value, got)], axis=0)
+    return value, swap(value, mine, 1)
 
 
 def on_device(count, ensemble, mean_state, observed, error_var, owner, obs_rows):
     gram = gram_of(ensemble)
-    keep, send = gather(ensemble, mean_state, observed, error_var, owner, obs_rows, gram)
-    return update(total(keep, send, count), ensemble, mean_state)
+    even, odd = gather(ensemble, mean_state, observed, error_var, owner, obs_rows, gram)
+    even_got, odd_got = swap(even, range(1, count, 2), 1), swap(odd, range(0, count, 2), 1)
+    even_got, odd_got = lax.optimization_barrier((even_got, odd_got))
+    return update(total(even + even_got, count, 0) + total(odd + odd_got, count, 1), ensemble, mean_state)
 
 
 def solution(mesh):

time: 47.4 us -> 59.4 us (1.25)
  starting transfers between devices: 8.96 us -> 27.3 us
  waiting for transfers between devices: 17.1 us -> 10.9 us
    ppermute x6 -> x12, starting transfers between devices: 8.96 us -> 27.3 us  [swap(): return lax.ppermute(value, AXIS, [(i, i ^ mask) for i in senders])]
    ppermute x6 -> x12, waiting for transfers between devices: 17.1 us -> 10.9 us  [swap(): return lax.ppermute(value, AXIS, [(i, i ^ mask) for i in senders])]
  transfers between devices with their start and end apart: 6 -> 12, of which waited for: 6 -> 6; matrix products, arithmetic and copies ran while one was open for 0% -> 0% of each run, Pallas kernels for 0% -> 0%
where the time goes in v10:
time: 59.4 us; the launch traced here: 59.2 us
  starting transfers between devices  27.3 us (46%)
  Pallas kernels  19.7 us (33%)
  waiting for transfers between devices  10.9 us (18%)
  between operations  1.1 us (2%)
    ppermute x12, starting transfers between devices, swap(): return lax.ppermute(value, AXIS, [(i, i ^ mask) for i in senders])  27.3 us
    pallas_call x1, Pallas kernels, update(): pl.pallas_call(functools.partial(update_kernel, chunks), out_shape=(jax.S...  14.8 us
    ppermute x12, waiting for transfers between devices, swap(): return lax.ppermute(value, AXIS, [(i, i ^ mask) for i in senders])  10.9 us
    pallas_call x1, Pallas kernels, gram_of(): pl.pallas_call(functools.partial(gram_kernel, chunks), out_shape=jax.Shap...  3.45 us
    pallas_call x1, Pallas kernels, gather(): pl.pallas_call(gather_kernel, out_shape=(jax.ShapeDtypeStruct((EVEN_ROWS,...  1.45 us
  transfers between devices with their start and end apart: 12, of which 6 were waited for; matrix products, arithmetic and copies ran while one was open for 0% of the time, Pallas kernels for 0%

profile of v10, /device:TPU:0, one launch (start us, length us, event | category | flops | bytes accessed | tf_op | source)
XLA Modules:
  0.0 59.2 jit_solution(6281250547544528182)
XLA Ops:
  0.6 0.0 copy-start
  0.6 0.0 copy-start.1
  0.7 0.0 copy-start.4
  0.7 0.0 copy-start.3
  0.7 0.0 copy-start.2
  0.7 3.4 %shard_map.77.gram = f32[320,128]{1,0:T(8,128)S(1)} custom-call(f32[4096,256]{1,0:T(8,128)} %x_hbm.5), custom_call_target="tpu_custom_call" | custom-call | flops 1073741824 | bytes 4194304 | tf_op jit(solution)/shard_map/pallas_call | solution.py:345
  4.1 0.0 copy-done
  4.1 0.0 copy-done.1
  4.2 0.0 copy-done.4
  4.2 0.0 copy-done.3
  4.2 0.0 copy-done.2
  4.2 1.4 %shard_map.78 = (f32[256,128]{1,0:T(8,128)S(1)}, f32[576,128]{1,0:T(8,128)S(1)}) custom-call(s32[2]{0:T(128)S(1)} %copy-done.4, s32[2,128]{1,0:T(2,128)S(1)} %copy-done.1, s32[2,128]{1,0:T(2,128)S(1)} %copy-done.1, f32[2,128]{1,0:T(2,128)S(1)} %copy-done.2, f32[2,128]{1,0:T(2,128)S(1)} %copy-done.3, f32[32,128]{1,0:T(8,128)S(1)} %bitcast.3, ...), custom_call_target="tpu_custom_call" | custom-call | tf_op jit(solution)/shard_map/pallas_call | solution.py:358
  5.6 2.4 %collective-permute-start.1 = (f32[576,128]{1,0:T(8,128)S(1)}, f32[576,128]{1,0:T(8,128)S(1)}, u32[]{:S(2)}, u32[]{:S(2)}) collective-permute-start(f32[576,128]{1,0:T(8,128)S(1)} %get-tuple-element.9), channel_id=1, source_target_pairs={{0,1},{2,3},{4,5},{6,7},{8,9},{10,11},{12,13},{14,15},{16,17},{18,... | collective-permute-start | bytes 884744 | tf_op jit(solution)/shard_map/ppermute | solution.py:396
  8.0 1.3 %collective-permute-start = (f32[256,128]{1,0:T(8,128)S(1)}, f32[256,128]{1,0:T(8,128)S(1)}, u32[]{:S(2)}, u32[]{:S(2)}) collective-permute-start(f32[256,128]{1,0:T(8,128)S(1)} %get-tuple-element.8), channel_id=1, source_target_pairs={{1,0},{3,2},{5,4},{7,6},{9,8},{11,10},{13,12},{15,14},{17,16},{19,... | collective-permute-start | bytes 393224 | tf_op jit(solution)/shard_map/ppermute | solution.py:396
  9.3 1.9 %collective-permute-done = f32[256,128]{1,0:T(8,128)S(1)} collective-permute-done((f32[256,128]{1,0:T(8,128)S(1)}, f32[256,128]{1,0:T(8,128)S(1)}, u32[]{:S(2)}, u32[]{:S(2)}) %collective-permute-start) | collective-permute-done | bytes 131104 | tf_op jit(solution)/shard_map/ppermute | solution.py:396
  11.3 0.0 collective-permute-done.1
  11.3 0.7 %collective-permute-start.7 = (f32[288,128]{1,0:T(8,128)S(1)}, f32[288,128]{1,0:T(8,128)S(1)}, u32[]{:S(2)}, u32[]{:S(2)}) collective-permute-start(f32[288,128]{1,0:T(8,128)S(1)} %slice_select_fusion), channel_id=1, source_target_pairs={{1,3},{3,1},{5,7},{7,5},{9,11},{11,9},{13,15},{15,13},{17,19},{19,... | collective-permute-start | bytes 442376 | tf_op jit(solution)/shard_map/ppermute | solution.py:396
  12.0 0.0 collective-permute-done.7
  12.0 0.7 %collective-permute-start.8 = (f32[288,128]{1,0:T(8,128)S(1)}, f32[288,128]{1,0:T(8,128)S(1)}, u32[]{:S(2)}, u32[]{:S(2)}) collective-permute-start(f32[288,128]{1,0:T(8,128)S(1)} %select_add_fusion), channel_id=1, source_target_pairs={{1,5},{3,7},{5,1},{7,3},{9,13},{11,15},{13,9},{15,11},{17,21},{19,... | collective-permute-start | bytes 442376 | tf_op jit(solution)/shard_map/ppermute | solution.py:396
  12.7 0.0 collective-permute-done.8
  12.8 0.7 %collective-permute-start.9 = (f32[288,128]{1,0:T(8,128)S(1)}, f32[288,128]{1,0:T(8,128)S(1)}, u32[]{:S(2)}, u32[]{:S(2)}) collective-permute-start(f32[288,128]{1,0:T(8,128)S(1)} %add.30), channel_id=1, source_target_pairs={{1,9},{3,11},{5,13},{7,15},{9,1},{11,3},{13,5},{15,7},{17,25},{19,... | collective-permute-start | bytes 442376 | tf_op jit(solution)/shard_map/ppermute | solution.py:396
  13.5 5.2 %collective-permute-start.2 = (f32[128,128]{1,0:T(8,128)S(1)}, f32[128,128]{1,0:T(8,128)S(1)}, u32[]{:S(2)}, u32[]{:S(2)}) collective-permute-start(f32[128,128]{1,0:T(8,128)S(1)} %slice_select_fusion.1), channel_id=1, source_target_pairs={{0,2},{2,0},{4,6},{6,4},{8,10},{10,8},{12,14},{14,12},{16,18},{18,... | collective-permute-start | bytes 196616 | tf_op jit(solution)/shard_map/ppermute | solution.py:396
  18.7 0.0 collective-permute-done.9
  18.7 0.7 %collective-permute-start.10 = (f32[288,128]{1,0:T(8,128)S(1)}, f32[288,128]{1,0:T(8,128)S(1)}, u32[]{:S(2)}, u32[]{:S(2)}) collective-permute-start(f32[288,128]{1,0:T(8,128)S(1)} %add.31), channel_id=1, source_target_pairs={{1,3},{3,1},{5,7},{7,5},{9,11},{11,9},{13,15},{15,13},{17,19},{19,... | collective-permute-start | bytes 442376 | tf_op jit(solution)/shard_map/ppermute | solution.py:396
  19.4 1.5 %collective-permute-done.2 = f32[128,128]{1,0:T(8,128)S(1)} collective-permute-done((f32[128,128]{1,0:T(8,128)S(1)}, f32[128,128]{1,0:T(8,128)S(1)}, u32[]{:S(2)}, u32[]{:S(2)}) %collective-permute-start.2) | collective-permute-done | bytes 65568 | tf_op jit(solution)/shard_map/ppermute | solution.py:396
  20.9 3.1 %collective-permute-start.3 = (f32[128,128]{1,0:T(8,128)S(1)}, f32[128,128]{1,0:T(8,128)S(1)}, u32[]{:S(2)}, u32[]{:S(2)}) collective-permute-start(f32[128,128]{1,0:T(8,128)S(1)} %select_add_fusion.1), channel_id=1, source_target_pairs={{0,4},{2,6},{4,0},{6,2},{8,12},{10,14},{12,8},{14,10},{16,20},{18,... | collective-permute-start | bytes 196616 | tf_op jit(solution)/shard_map/ppermute | solution.py:396
  24.0 3.1 %collective-permute-done.3 = f32[128,128]{1,0:T(8,128)S(1)} collective-permute-done((f32[128,128]{1,0:T(8,128)S(1)}, f32[128,128]{1,0:T(8,128)S(1)}, u32[]{:S(2)}, u32[]{:S(2)}) %collective-permute-start.3) | collective-permute-done | bytes 65568 | tf_op jit(solution)/shard_map/ppermute | solution.py:396
  27.1 4.4 %collective-permute-start.4 = (f32[128,128]{1,0:T(8,128)S(1)}, f32[128,128]{1,0:T(8,128)S(1)}, u32[]{:S(2)}, u32[]{:S(2)}) collective-permute-start(f32[128,128]{1,0:T(8,128)S(1)} %add.26), channel_id=1, source_target_pairs={{0,8},{2,10},{4,12},{6,14},{8,0},{10,2},{12,4},{14,6},{16,24},{18,... | collective-permute-start | bytes 196616 | tf_op jit(solution)/shard_map/ppermute | solution.py:396
  31.5 2.7 %collective-permute-done.4 = f32[128,128]{1,0:T(8,128)S(1)} collective-permute-done((f32[128,128]{1,0:T(8,128)S(1)}, f32[128,128]{1,0:T(8,128)S(1)}, u32[]{:S(2)}, u32[]{:S(2)}) %collective-permute-start.4) | collective-permute-done | bytes 65568 | tf_op jit(solution)/shard_map/ppermute | solution.py:396
  34.2 4.6 %collective-permute-start.5 = (f32[128,128]{1,0:T(8,128)S(1)}, f32[128,128]{1,0:T(8,128)S(1)}, u32[]{:S(2)}, u32[]{:S(2)}) collective-permute-start(f32[128,128]{1,0:T(8,128)S(1)} %add.27), channel_id=1, source_target_pairs={{0,2},{2,0},{4,6},{6,4},{8,10},{10,8},{12,14},{14,12},{16,18},{18,... | collective-permute-start | bytes 196616 | tf_op jit(solution)/shard_map/ppermute | solution.py:396
  38.8 0.0 collective-permute-done.10
  38.9 1.3 %collective-permute-start.11 = (f32[576,128]{1,0:T(8,128)S(1)}, f32[576,128]{1,0:T(8,128)S(1)}, u32[]{:S(2)}, u32[]{:S(2)}) collective-permute-start(f32[576,128]{1,0:T(8,128)S(1)} %pad_maximum_fusion.odd_mine), channel_id=1, source_target_pairs={{1,0},{3,2},{5,4},{7,6},{9,8},{11,10},{13,12},{15,14},{17,16},{19,... | collective-permute-start | bytes 884744 | tf_op jit(solution)/shard_map/ppermute | solution.py:396
  40.2 0.9 %collective-permute-done.5 = f32[128,128]{1,0:T(8,128)S(1)} collective-permute-done((f32[128,128]{1,0:T(8,128)S(1)}, f32[128,128]{1,0:T(8,128)S(1)}, u32[]{:S(2)}, u32[]{:S(2)}) %collective-permute-start.5) | collective-permute-done | bytes 65568 | tf_op jit(solution)/shard_map/ppermute | solution.py:396
  41.0 2.4 %collective-permute-start.6 = (f32[256,128]{1,0:T(8,128)S(1)}, f32[256,128]{1,0:T(8,128)S(1)}, u32[]{:S(2)}, u32[]{:S(2)}) collective-permute-start(f32[256,128]{1,0:T(8,128)S(1)} %pad_maximum_fusion.1.even_mine), channel_id=1, source_target_pairs={{0,1},{2,3},{4,5},{6,7},{8,9},{10,11},{12,13},{14,15},{16,17},{18,... | collective-permute-start | bytes 393224 | tf_op jit(solution)/shard_map/ppermute | solution.py:396
  43.4 0.8 %collective-permute-done.6.even_got = f32[256,128]{1,0:T(8,128)S(1)} collective-permute-done((f32[256,128]{1,0:T(8,128)S(1)}, f32[256,128]{1,0:T(8,128)S(1)}, u32[]{:S(2)}, u32[]{:S(2)}) %collective-permute-start.6) | collective-permute-done | bytes 131104 | tf_op jit(solution)/shard_map/ppermute | solution.py:396
  44.2 0.0 collective-permute-done.11.odd_got
  44.2 14.8 %shard_map.79 = (f32[4096,256]{1,0:T(8,128)}, f32[1,4096]{1,0:T(1,128)}) custom-call(f32[256,128]{1,0:T(8,128)S(1)} %pad_maximum_fusion.1.even_mine, f32[256,128]{1,0:T(8,128)S(1)} %collective-permute-done.6.even_got, f32[576,128]{1,0:T(8,128)S(1)} %pad_maximum_fusion.odd_mine, f32[576,128]{1,0:T(8,128)S(1)} %collective-permute-done.11.odd_got, ...), custom_call_target="tpu_custom_call" | custom-call | tf_op jit(solution)/shard_map/pallas_call | solution.py:378
  (14 shorter events, 0.2 us)
Async XLA Ops:
  0.6 3.5 %copy-start = (f32[4096]{0:T(1024)S(1)}, f32[4096]{0:T(1024)}, u32[]{:S(2)}) copy-start(f32[4096]{0:T(1024)} %param.7) | copy-start | bytes 49156
  0.6 3.5 %copy-start.1 = (s32[2,128]{1,0:T(2,128)S(1)}, s32[2,128]{1,0:T(2,128)}, u32[]{:S(2)}) copy-start(s32[2,128]{1,0:T(2,128)} %rows_v.1) | copy-start | bytes 3076
  0.7 3.5 %copy-start.4 = (s32[2]{0:T(128)S(1)}, s32[2]{0:T(128)}, u32[]{:S(2)}) copy-start(s32[2]{0:T(128)} %owner_s.1) | copy-start | bytes 28
  0.7 3.5 %copy-start.3 = (f32[2,128]{1,0:T(2,128)S(1)}, f32[2,128]{1,0:T(2,128)}, u32[]{:S(2)}) copy-start(f32[2,128]{1,0:T(2,128)} %error_var.1) | copy-start | bytes 3076
  0.7 3.5 %copy-start.2 = (f32[2,128]{1,0:T(2,128)S(1)}, f32[2,128]{1,0:T(2,128)}, u32[]{:S(2)}) copy-start(f32[2,128]{1,0:T(2,128)} %observed.1) | copy-start | bytes 3076
  5.6 5.6 %collective-permute-start.1 = (f32[576,128]{1,0:T(8,128)S(1)}, f32[576,128]{1,0:T(8,128)S(1)}, u32[]{:S(2)}, u32[]{:S(2)}) collective-permute-start(f32[576,128]{1,0:T(8,128)S(1)} %get-tuple-element.9), channel_id=1, source_target_pairs={{0,1},{2,3},{4,5},{6,7},{8,9},{10,11},{12,13},{14,15},{16,17},{18,... | collective-permute-start | bytes 884744 | tf_op jit(solution)/shard_map/ppermute | solution.py:396
  8.0 3.2 %collective-permute-start = (f32[256,128]{1,0:T(8,128)S(1)}, f32[256,128]{1,0:T(8,128)S(1)}, u32[]{:S(2)}, u32[]{:S(2)}) collective-permute-start(f32[256,128]{1,0:T(8,128)S(1)} %get-tuple-element.8), channel_id=1, source_target_pairs={{1,0},{3,2},{5,4},{7,6},{9,8},{11,10},{13,12},{15,14},{17,16},{19,... | collective-permute-start | bytes 393224 | tf_op jit(solution)/shard_map/ppermute | solution.py:396
  11.3 0.7 %collective-permute-start.7 = (f32[288,128]{1,0:T(8,128)S(1)}, f32[288,128]{1,0:T(8,128)S(1)}, u32[]{:S(2)}, u32[]{:S(2)}) collective-permute-start(f32[288,128]{1,0:T(8,128)S(1)} %slice_select_fusion), channel_id=1, source_target_pairs={{1,3},{3,1},{5,7},{7,5},{9,11},{11,9},{13,15},{15,13},{17,19},{19,... | collective-permute-start | bytes 442376 | tf_op jit(solution)/shard_map/ppermute | solution.py:396
  12.0 0.7 %collective-permute-start.8 = (f32[288,128]{1,0:T(8,128)S(1)}, f32[288,128]{1,0:T(8,128)S(1)}, u32[]{:S(2)}, u32[]{:S(2)}) collective-permute-start(f32[288,128]{1,0:T(8,128)S(1)} %select_add_fusion), channel_id=1, source_target_pairs={{1,5},{3,7},{5,1},{7,3},{9,13},{11,15},{13,9},{15,11},{17,21},{19,... | collective-permute-start | bytes 442376 | tf_op jit(solution)/shard_map/ppermute | solution.py:396
  12.8 5.9 %collective-permute-start.9 = (f32[288,128]{1,0:T(8,128)S(1)}, f32[288,128]{1,0:T(8,128)S(1)}, u32[]{:S(2)}, u32[]{:S(2)}) collective-permute-start(f32[288,128]{1,0:T(8,128)S(1)} %add.30), channel_id=1, source_target_pairs={{1,9},{3,11},{5,13},{7,15},{9,1},{11,3},{13,5},{15,7},{17,25},{19,... | collective-permute-start | bytes 442376 | tf_op jit(solution)/shard_map/ppermute | solution.py:396
  13.5 7.4 %collective-permute-start.2 = (f32[128,128]{1,0:T(8,128)S(1)}, f32[128,128]{1,0:T(8,128)S(1)}, u32[]{:S(2)}, u32[]{:S(2)}) collective-permute-start(f32[128,128]{1,0:T(8,128)S(1)} %slice_select_fusion.1), channel_id=1, source_target_pairs={{0,2},{2,0},{4,6},{6,4},{8,10},{10,8},{12,14},{14,12},{16,18},{18,... | collective-permute-start | bytes 196616 | tf_op jit(solution)/shard_map/ppermute | solution.py:396
  18.7 20.1 %collective-permute-start.10 = (f32[288,128]{1,0:T(8,128)S(1)}, f32[288,128]{1,0:T(8,128)S(1)}, u32[]{:S(2)}, u32[]{:S(2)}) collective-permute-start(f32[288,128]{1,0:T(8,128)S(1)} %add.31), channel_id=1, source_target_pairs={{1,3},{3,1},{5,7},{7,5},{9,11},{11,9},{13,15},{15,13},{17,19},{19,... | collective-permute-start | bytes 442376 | tf_op jit(solution)/shard_map/ppermute | solution.py:396
  20.9 6.2 %collective-permute-start.3 = (f32[128,128]{1,0:T(8,128)S(1)}, f32[128,128]{1,0:T(8,128)S(1)}, u32[]{:S(2)}, u32[]{:S(2)}) collective-permute-start(f32[128,128]{1,0:T(8,128)S(1)} %select_add_fusion.1), channel_id=1, source_target_pairs={{0,4},{2,6},{4,0},{6,2},{8,12},{10,14},{12,8},{14,10},{16,20},{18,... | collective-permute-start | bytes 196616 | tf_op jit(solution)/shard_map/ppermute | solution.py:396
  27.1 7.1 %collective-permute-start.4 = (f32[128,128]{1,0:T(8,128)S(1)}, f32[128,128]{1,0:T(8,128)S(1)}, u32[]{:S(2)}, u32[]{:S(2)}) collective-permute-start(f32[128,128]{1,0:T(8,128)S(1)} %add.26), channel_id=1, source_target_pairs={{0,8},{2,10},{4,12},{6,14},{8,0},{10,2},{12,4},{14,6},{16,24},{18,... | collective-permute-start | bytes 196616 | tf_op jit(solution)/shard_map/ppermute | solution.py:396
  34.2 6.9 %collective-permute-start.5 = (f32[128,128]{1,0:T(8,128)S(1)}, f32[128,128]{1,0:T(8,128)S(1)}, u32[]{:S(2)}, u32[]{:S(2)}) collective-permute-start(f32[128,128]{1,0:T(8,128)S(1)} %add.27), channel_id=1, source_target_pairs={{0,2},{2,0},{4,6},{6,4},{8,10},{10,8},{12,14},{14,12},{16,18},{18,... | collective-permute-start | bytes 196616 | tf_op jit(solution)/shard_map/ppermute | solution.py:396
  38.9 5.4 %collective-permute-start.11 = (f32[576,128]{1,0:T(8,128)S(1)}, f32[576,128]{1,0:T(8,128)S(1)}, u32[]{:S(2)}, u32[]{:S(2)}) collective-permute-start(f32[576,128]{1,0:T(8,128)S(1)} %pad_maximum_fusion.odd_mine), channel_id=1, source_target_pairs={{1,0},{3,2},{5,4},{7,6},{9,8},{11,10},{13,12},{15,14},{17,16},{19,... | collective-permute-start | bytes 884744 | tf_op jit(solution)/shard_map/ppermute | solution.py:396
  41.0 3.2 %collective-permute-start.6 = (f32[256,128]{1,0:T(8,128)S(1)}, f32[256,128]{1,0:T(8,128)S(1)}, u32[]{:S(2)}, u32[]{:S(2)}) collective-permute-start(f32[256,128]{1,0:T(8,128)S(1)} %pad_maximum_fusion.1.even_mine), channel_id=1, source_target_pairs={{0,1},{2,3},{4,5},{6,7},{8,9},{10,11},{12,13},{14,15},{16,17},{18,... | collective-permute-start | bytes 393224 | tf_op jit(solution)/shard_map/ppermute | solution.py:396
